TPU v7x, 512 devices: a whole 4x4x16 slice. The times are simulated.
512 devices in a mesh: kv: 8 (over y, core), req: 64 (over z, x).
Axes of the slice: x: 4, y: 4, z: 16, core: 2. Of those that a mesh axis runs over, the one named last changes fastest.
Arguments:
- queries: bfloat16 [2048, 4, 64, 128], P('req', None, 'kv'), may hold values from -4.8125 to 4.8125
- new_keys: bfloat16 [2048, 4, 8, 128], P('req', None, 'kv'), may hold values from -4.8125 to 4.8125
- new_values: bfloat16 [2048, 4, 8, 128], P('req', None, 'kv'), may hold values from -6 to 6
- suffix_keys: bfloat16 [2048, 128, 8, 128], P('req', None, 'kv'), may hold values from -4.8125 to 4.8125
- suffix_values: bfloat16 [2048, 128, 8, 128], P('req', None, 'kv'), may hold values from -6 to 6
- suffix_len: int32 [2048], P('req'), may hold values from 1 to 128, 229376 in all
- block_table: int32 [2048, 4], P('req'), may hold values from 0 to 127, all different within a row; in each aligned block of 32 rows (0 to 31, 32 to 63, ...) at most 2 rows name the same one
- prefix_keys: bfloat16 [128, 1024, 8, 128], P('req', None, 'kv'), may hold values from -4.8125 to 4.8125
- prefix_values: bfloat16 [128, 1024, 8, 128], P('req', None, 'kv'), may hold values from -6 to 6
Outputs:
- attended: bfloat16 [256, 8, 4, 8192], P('req', 'kv')
Inputs may be any that keep to these rules, and one draw needn't show every extreme that they name: `block_table`: among the 32 requests of one device (aligned blocks of rows) no span is named by more than 2 requests, a bound that some block reaches; a request names 4 different spans.
All inputs are finite; a program needn't handle non-finite values. No bound on the sum of `suffix_len` on one device may be relied on, other than what follows from the above.
Results may differ from a plain program's by a relative error of at most 0.0046.
Values may be sent and summed in bfloat16 or wider, within the bound.
No kernel may reach another device: no remote copies, remote signals or barrier semaphores. Data moves between devices by JAX's collectives and lax.ppermute only.
A program may use at most 64 MiB of HBM per device.

v0:
```python
import jax
import jax.numpy as jnp
from jax import lax
from jax.sharding import PartitionSpec as P


def span_states(queries_in, key_block, value_block):
    scaling = queries_in.shape[-1] ** (-0.5)
    scores = (
        jnp.einsum("bsngd,tnd->bsngt", queries_in, key_block, preferred_element_type=jnp.float32)
        * scaling
    )
    highest = jnp.max(scores, axis=-1)
    weights = jnp.exp(scores - highest[..., None])
    summed = jnp.sum(weights, axis=-1)
    product = jnp.einsum(
        "bsngt,tnd->bsngd",
        weights.astype(jnp.bfloat16),
        value_block,
        preferred_element_type=jnp.float32,
    )
    return (product / summed[..., None], highest + jnp.log(summed))


def own_states(grouped, cache_keys, cache_values, fresh_keys, fresh_values, live_len):
    scaling = grouped.shape[-1] ** (-0.5)
    step_count = grouped.shape[1]
    cache_slots = cache_keys.shape[1]
    cache_scores = (
        jnp.einsum("rsngd,rtnd->rsngt", grouped, cache_keys, preferred_element_type=jnp.float32)
        * scaling
    )
    fresh_scores = (
        jnp.einsum("rsngd,rtnd->rsngt", grouped, fresh_keys, preferred_element_type=jnp.float32)
        * scaling
    )
    cache_live = jnp.arange(cache_slots, dtype=jnp.int32)[None, :] < live_len[:, None]
    cache_scores = jnp.where(cache_live[:, None, None, None, :], cache_scores, -1e30)
    causal = (
        jnp.arange(step_count, dtype=jnp.int32)[None, :]
        <= jnp.arange(step_count, dtype=jnp.int32)[:, None]
    )
    fresh_scores = jnp.where(causal[None, :, None, None, :], fresh_scores, -1e30)
    highest = jnp.maximum(jnp.max(cache_scores, axis=-1), jnp.max(fresh_scores, axis=-1))
    cache_w = jnp.exp(cache_scores - highest[..., None])
    fresh_w = jnp.exp(fresh_scores - highest[..., None])
    summed = jnp.sum(cache_w, axis=-1) + jnp.sum(fresh_w, axis=-1)
    product = jnp.einsum(
        "rsngt,rtnd->rsngd",
        cache_w.astype(jnp.bfloat16),
        cache_values,
        preferred_element_type=jnp.float32,
    )
    product = product + jnp.einsum(
        "rsngt,rtnd->rsngd",
        fresh_w.astype(jnp.bfloat16),
        fresh_values,
        preferred_element_type=jnp.float32,
    )
    return (product / summed[..., None], highest + jnp.log(summed))


def merge_states(partials, log_sums, axis_pos):
    ceiling = jnp.max(log_sums, axis=axis_pos, keepdims=True)
    factors = jnp.exp(log_sums - ceiling)
    weighted = jnp.sum(factors[..., None] * partials, axis=axis_pos)
    return (weighted / jnp.sum(factors, axis=axis_pos)[..., None]).astype(jnp.bfloat16)


def local(
    queries,
    new_keys,
    new_values,
    suffix_keys,
    suffix_values,
    suffix_len,
    block_table,
    prefix_keys,
    prefix_values,
):
    requests, step_count, local_heads, head_width = queries.shape
    kv_local = new_keys.shape[2]
    group_size = local_heads // kv_local
    depth_count = block_table.shape[1]
    span_count = prefix_keys.shape[0]
    owners = lax.axis_size("req")
    capacity = max(2, 2 * requests * depth_count // (owners * span_count))
    grouped = queries.reshape(requests, step_count, kv_local, group_size, head_width)
    row_shape = grouped.shape[1:]
    named = block_table.reshape(-1)
    pair_count = named.shape[0]
    matching = named[:, None] == named[None, :]
    earlier = jnp.arange(pair_count)[None, :] < jnp.arange(pair_count)[:, None]
    ranking = jnp.sum(jnp.where(matching & earlier, 1, 0), axis=1).astype(jnp.int32)
    slot_ids = named * capacity + ranking
    slot_total = owners * span_count * capacity
    outgoing = jnp.zeros((slot_total,) + row_shape, jnp.bfloat16)
    outgoing = outgoing.at[slot_ids].set(jnp.repeat(grouped, depth_count, axis=0))
    outgoing = outgoing.reshape((owners, span_count, capacity) + row_shape)
    received = lax.all_to_all(outgoing, "req", split_axis=0, concat_axis=0, tiled=True)
    sources = received.shape[0]
    slots_here = received.shape[2]
    trailing = received.shape[3:]
    part_list = []
    log_list = []
    for span_pos in range(span_count):
        sliced = received[:, span_pos].reshape((sources // 8, 8 * slots_here) + trailing)

        def one_block(block_rows, span_pos=span_pos):
            return span_states(block_rows, prefix_keys[span_pos], prefix_values[span_pos])

        mixed, logs = lax.map(one_block, sliced)
        part_list.append(mixed.reshape((sources, slots_here) + trailing))
        log_list.append(logs.reshape((sources, slots_here) + trailing[:-1]))
    partial_out = jnp.stack(part_list, axis=1)
    log_out = jnp.stack(log_list, axis=1)
    remote_part = lax.all_to_all(partial_out, "req", split_axis=0, concat_axis=0, tiled=True)
    remote_log = lax.all_to_all(log_out, "req", split_axis=0, concat_axis=0, tiled=True)
    own_part, own_log = own_states(
        grouped, suffix_keys, suffix_values, new_keys, new_values, suffix_len
    )
    remote_part = remote_part.reshape((slot_total,) + row_shape)[slot_ids]
    remote_part = remote_part.reshape((requests, depth_count) + row_shape)
    remote_log = remote_log.reshape((slot_total,) + row_shape[:-1])[slot_ids]
    remote_log = remote_log.reshape((requests, depth_count) + row_shape[:-1])
    partials = jnp.concatenate([remote_part, own_part[:, None]], axis=1)
    partials = partials.reshape(requests, depth_count + 1, step_count, local_heads, head_width)
    log_sums = jnp.concatenate([remote_log, own_log[:, None]], axis=1)
    log_sums = log_sums.reshape(requests, depth_count + 1, step_count, local_heads)
    kv_count = lax.axis_size("kv")
    rows_out = requests // kv_count
    merged = merge_states(partials, log_sums, 1)
    merged = merged.reshape(rows_out, kv_count, step_count, local_heads * head_width)
    return lax.all_to_all(merged, "kv", split_axis=1, concat_axis=3, tiled=True)


def solution(mesh):
    placed = (
        P("req", None, "kv", None),
        P("req", None, "kv", None),
        P("req", None, "kv", None),
        P("req", None, "kv", None),
        P("req", None, "kv", None),
        P("req"),
        P("req", None),
        P("req", None, "kv", None),
        P("req", None, "kv", None),
    )
    return jax.shard_map(
        local, mesh=mesh, in_specs=placed, out_specs=P("req", "kv", None, None), check_vma=False
    )
```

profile of v0, /device:TPU:1, one launch (start us, length us, event | category | flops | bytes accessed | tf_op | source)
XLA Modules:
  0.0 430.1 jit_solution(4568803669256448303)
XLA Ops:
  3.2 1.6 broadcast.108
  4.8 13.7 %scatter_fusion = bf16[256,4,8,128]{3,2,1,0:T(8,128)(2,1)} fusion(bf16[256,4,8,128]{3,2,1,0:T(8,128)(2,1)} %broadcast.108, s32[128]{0:T(128)S(1)} %fusion.68, bf16[128,4,8,128]{3,2,1,0:T(8,128)(2,1)S(1)} %bitcast.279), kind=kCustom, calls=%fused_computation.2 | custom fusion | bytes 3146240 | tf_op jit(solution)/shard_map/scatter | solution.py:98
  18.5 19.1 %all-to-all-start = ((bf16[64,2,2,4,1,8,128]{6,5,3,2,1,4,0:T(8,128)(2,1)}), bf16[64,2,2,4,1,8,128]{6,5,3,2,1,4,0:T(8,128)(2,1)S(1)}, u32[]{:S(2)}, u32[]{:S(2)}) async-start(bf16[64,2,2,4,1,8,128]{6,5,3,2,1,4,0:T(8,128)(2,1)} %bitcast.40), calls=%async_computation | async-start | bytes 4194304 | tf_op jit(solution)/shard_map/all_to_all | solution.py:100
  37.6 94.9 %all-to-all-done = bf16[64,2,2,4,1,8,128]{6,5,3,2,1,4,0:T(8,128)(2,1)S(1)} async-done(((bf16[64,2,2,4,1,8,128]{6,5,3,2,1,4,0:T(8,128)(2,1)}), bf16[64,2,2,4,1,8,128]{6,5,3,2,1,4,0:T(8,128)(2,1)S(1)}, u32[]{:S(2)}, u32[]{:S(2)}) %all-to-all-start) | async-done | bytes 2097184 | tf_op jit(solution)/shard_map/all_to_all | solution.py:100
  132.4 1.9 fusion.71
  134.3 1.6 broadcast.104.clone.1
  136.0 26.1 %while.24 = (s32[]{:T(128)}, f32[8,16,4,1,8,128]{5,4,2,1,3,0:T(8,128)}, f32[8,16,4,1,8]{4,1,0,2,3:T(8,128)S(1)}, bf16[8,16,4,1,8,128]{5,4,2,1,3,0:T(8,128)(2,1)}...) while((s32[]{:T(128)}, f32[8,16,4,1,8,128]{5,4,2,1,3,0:T(8,128)}, ...), condition=%wide.region_5.6_spmd, body=%wide.region_2.5_spmd.sunk | while | flops 272694784 | bytes 7353425 | solution.py:112
  136.0 1.4 bitcast_reduce_fusion.4
  139.2 1.4 bitcast_reduce_fusion.4
  142.5 1.4 bitcast_reduce_fusion.4
  149.0 1.4 bitcast_reduce_fusion.4
  152.3 1.4 bitcast_reduce_fusion.4
  155.5 1.4 bitcast_reduce_fusion.4
  158.8 1.4 bitcast_reduce_fusion.4
  162.1 1.6 broadcast.104.clone
  163.7 26.1 %while.25 = (s32[]{:T(128)}, f32[8,16,4,1,8,128]{5,4,2,1,3,0:T(8,128)}, f32[8,16,4,1,8]{4,1,0,2,3:T(8,128)S(1)}, bf16[8,16,4,1,8,128]{5,4,2,1,3,0:T(8,128)(2,1)}...) while((s32[]{:T(128)}, ...), condition=%wide.region_9.10_spmd, body=%wide.region_6.9_spmd.sunk | while | flops 272694784 | bytes 7353425 | solution.py:112
  163.7 1.4 bitcast_reduce_fusion.5
  167.0 1.4 bitcast_reduce_fusion.5
  170.2 1.4 bitcast_reduce_fusion.5
  173.5 1.4 bitcast_reduce_fusion.5
  176.8 1.4 bitcast_reduce_fusion.5
  180.0 1.4 bitcast_reduce_fusion.5
  186.5 1.4 bitcast_reduce_fusion.5
  191.5 10.7 %all-to-all-start.1 = ((f32[64,1,128]{2,1,0:T(1,128)}), f32[64,1,128]{2,1,0:T(1,128)S(1)}, u32[]{:S(2)}, u32[]{:S(2)}) async-start(f32[64,1,128]{2,1,0:T(1,128)} %reshape.363), calls=%async_computation.1 | async-start | bytes 65536 | tf_op jit(solution)/shard_map/all_to_all | solution.py:118
  202.2 5.0 %pad_maximum_fusion = f32[64,2,2,4,1,8,128]{6,5,3,2,1,4,0:T(8,128)} fusion(f32[64,1,2,4,1,8,128]{6,5,3,2,1,4,0:T(8,128)} %bitcast.62, f32[64,1,2,4,1,8,128]{6,5,3,2,1,4,0:T(8,128)} %bitcast.61), kind=kLoop, calls=%fused_computation.49 | loop fusion | flops 1048576 | bytes 8388608 | tf_op jit(solution)/shard_map/stack | solution.py:115
  207.2 8.4 %all-to-all-done.1 = f32[64,1,128]{2,1,0:T(1,128)S(1)} async-done(((f32[64,1,128]{2,1,0:T(1,128)}), f32[64,1,128]{2,1,0:T(1,128)S(1)}, u32[]{:S(2)}, u32[]{:S(2)}) %all-to-all-start.1) | async-done | bytes 32800 | tf_op jit(solution)/shard_map/all_to_all | solution.py:118
  215.6 6.7 %all-to-all-start.2 = ((f32[64,2,2,4,1,8,128]{6,5,3,2,1,4,0:T(8,128)}), f32[64,2,2,4,1,8,128]{6,5,3,2,1,4,0:T(8,128)}, u32[]{:S(2)}, u32[]{:S(2)}) async-start(f32[64,2,2,4,1,8,128]{6,5,3,2,1,4,0:T(8,128)} %pad_maximum_fusion), calls=%async_computation.2 | async-start | bytes 8388608 | tf_op jit(solution)/shard_map/all_to_all | solution.py:117
  229.6 2.5 fusion.47
  232.2 173.4 %all-to-all-done.2 = f32[64,2,2,4,1,8,128]{6,5,3,2,1,4,0:T(8,128)} async-done(((f32[64,2,2,4,1,8,128]{6,5,3,2,1,4,0:T(8,128)}), f32[64,2,2,4,1,8,128]{6,5,3,2,1,4,0:T(8,128)}, u32[]{:S(2)}, u32[]{:S(2)}) %all-to-all-start.2) | async-done | bytes 4194336 | tf_op jit(solution)/shard_map/all_to_all | solution.py:117
  405.6 2.9 gather_fusion.1
  408.5 1.8 fusion.39
  410.8 18.2 %all_to_all.33 = bf16[4,8,4,1024]{3,0,2,1:T(4,128)(2,1)S(1)} all-to-all(bf16[4,8,4,1024]{3,0,2,1:T(4,128)(2,1)S(1)} %copy.114), channel_id=1, replica_groups=mesh['kv'=8,'req'=64] {'kv'}, dimensions={1} | all-to-all | bytes 524288 | tf_op jit(solution)/shard_map/all_to_all | solution.py:134
  (121 shorter events, 45.3 us)
Async XLA Ops:
  0.0 223.7 %copy-start = (bf16[32,128,1,128]{3,1,2,0:T(8,128)(2,1)S(1)}, bf16[32,128,1,128]{3,1,2,0:T(8,128)(2,1)}, u32[]{:S(2)}) copy-start(bf16[32,128,1,128]{3,1,2,0:T(8,128)(2,1)} %param.16) | copy-start | bytes 3145732
  18.5 113.9 %all-to-all-start = ((bf16[64,2,2,4,1,8,128]{6,5,3,2,1,4,0:T(8,128)(2,1)}), bf16[64,2,2,4,1,8,128]{6,5,3,2,1,4,0:T(8,128)(2,1)S(1)}, u32[]{:S(2)}, u32[]{:S(2)}) async-start(bf16[64,2,2,4,1,8,128]{6,5,3,2,1,4,0:T(8,128)(2,1)} %bitcast.40), calls=%async_computation | async-start | bytes 4194304 | tf_op jit(solution)/shard_map/all_to_all | solution.py:100
  134.3 1.6 copy-start.1
  134.3 1.6 copy-start.5
  191.5 24.1 %all-to-all-start.1 = ((f32[64,1,128]{2,1,0:T(1,128)}), f32[64,1,128]{2,1,0:T(1,128)S(1)}, u32[]{:S(2)}, u32[]{:S(2)}) async-start(f32[64,1,128]{2,1,0:T(1,128)} %reshape.363), calls=%async_computation.1 | async-start | bytes 65536 | tf_op jit(solution)/shard_map/all_to_all | solution.py:118
  207.2 15.2 %copy-start.4 = (s32[32]{0:T(128)S(1)}, s32[32]{0:T(128)}, u32[]{:S(2)}) copy-start(s32[32]{0:T(128)} %param.18) | copy-start | bytes 388
  207.2 15.2 %copy-start.2 = (bf16[32,4,8,128]{3,2,1,0:T(8,128)(2,1)S(1)}, bf16[32,4,8,128]{3,2,1,0:T(8,128)(2,1)}, u32[]{:S(2)}) copy-start(bf16[32,4,8,128]{3,2,1,0:T(8,128)(2,1)} %param.13) | copy-start | bytes 786436
  207.2 15.2 %copy-start.6 = (bf16[32,4,1,128]{3,1,2,0:T(4,128)(2,1)S(1)}, bf16[32,4,1,128]{3,1,2,0:T(4,128)(2,1)}, u32[]{:S(2)}) copy-start(bf16[32,4,1,128]{3,1,2,0:T(4,128)(2,1)} %param.14) | copy-start | bytes 98308
  215.6 190.0 %all-to-all-start.2 = ((f32[64,2,2,4,1,8,128]{6,5,3,2,1,4,0:T(8,128)}), f32[64,2,2,4,1,8,128]{6,5,3,2,1,4,0:T(8,128)}, u32[]{:S(2)}, u32[]{:S(2)}) async-start(f32[64,2,2,4,1,8,128]{6,5,3,2,1,4,0:T(8,128)} %pad_maximum_fusion), calls=%async_computation.2 | async-start | bytes 8388608 | tf_op jit(solution)/shard_map/all_to_all | solution.py:117
  222.3 2.9 copy-start.3
where the time goes:
time: 431 us; the launch traced here: 430 us
  waiting for transfers between devices  277 us (64%)
  matrix products  47.5 us (11%)
  starting transfers between devices  36.5 us (8%)
  local copies, waits for them, and re-layouts  31.5 us (7%)
  other arithmetic  18.9 us (4%)
  blocking collectives  18.2 us (4%)
    all_to_all x1, waiting for transfers between devices, local(): lax.all_to_all(partial_out, 'req', split_axis=0, concat_axis=0, tiled=True)  173 us
    all_to_all x1, waiting for transfers between devices, local(): lax.all_to_all(outgoing, 'req', split_axis=0, concat_axis=0, tiled=True)  94.9 us
    dot_general x16, matrix products, span_states(): jnp.einsum('bsngd,tnd->bsngt', queries_in, key_block, preferred_element_t...  22.9 us
    dot_general x16, matrix products, span_states(): jnp.einsum('bsngt,tnd->bsngd', weights.astype(jnp.bfloat16), value_block,...  19.8 us
    all_to_all x1, starting transfers between devices, local(): lax.all_to_all(outgoing, 'req', split_axis=0, concat_axis=0, tiled=True)  19.1 us
    all_to_all x1, blocking collectives, local(): return lax.all_to_all(merged, 'kv', split_axis=1, concat_axis=3, tiled=True)  18.2 us
    scatter x1, local copies, waits for them, and re-layouts, local(): outgoing.at[slot_ids].set(jnp.repeat(grouped, depth_count, axis=0))  13.7 us
    all_to_all x1, starting transfers between devices, local(): lax.all_to_all(log_out, 'req', split_axis=0, concat_axis=0, tiled=True)  10.7 us
  transfers between devices with their start and end apart: 3, of which 3 were waited for; matrix products, arithmetic and copies ran while one was open for 3% of the time, Pallas kernels for 0%

commit v1 on v0

v1 whole, which is shorter than its diff:
```python
import jax
import jax.numpy as jnp
from jax import lax
from jax.experimental import pallas as pl
from jax.experimental.pallas import tpu as pltpu
from jax.sharding import PartitionSpec as P

NX = 4
CAP = 2
CHUNKS = 2
TILE = 256
PAD = 16
EMPTY = -1e30


def dot(a, b, dims):
    return lax.dot_general(a, b, (dims, ((), ())), preferred_element_type=jnp.float32)


def three_parts(line):
    parts = []
    for _ in range(3):
        piece = line.astype(jnp.bfloat16)
        line = line - piece.astype(jnp.float32)
        parts.append(piece)
    return parts


def span_kernel(q_ref, k_ref, v_ref, out_ref, logs_ref):
    spans, rows, width = q_ref.shape[1:]
    scale = width ** (-0.5)
    tile = min(TILE, rows)
    base = spans * rows
    blocks, lanes = logs_ref.shape[0] // 2, logs_ref.shape[1]
    per = rows // blocks
    logs_ref[...] = jnp.zeros_like(logs_ref)
    for s in range(spans):
        for t in range(0, rows, tile):
            q = q_ref[0, s, t : t + tile, :]
            scores = dot(k_ref[s], q, ((1,), (1,)))
            top = jnp.max(scores, axis=0, keepdims=True)
            weights = jnp.exp((scores - top) * scale)
            total = jnp.sum(weights, axis=0, keepdims=True)
            mixed = dot(v_ref[s], weights.astype(jnp.bfloat16), ((1,), (0,)))
            mixed = mixed / total
            at = s * rows + t
            out_ref[0, at : at + tile, :] = mixed.T.astype(jnp.bfloat16)
            parts = three_parts(top * scale + jnp.log(total))
            for u in range(0, tile, per):
                block = (t + u) // per
                for p in range(3):
                    line = blocks * (p // 2) + block
                    lane = (p % 2) * spans * per + s * per
                    logs_ref[line : line + 1, lane : lane + per] = parts[p][
                        :, u : u + per
                    ].astype(jnp.float32)
    out_ref[0, base : base + 2 * blocks, :] = logs_ref[...].astype(jnp.bfloat16)


def span_states(q, keys, values, blocks):
    peers, spans, rows, width = q.shape
    lines = spans * rows + 2 * blocks
    return pl.pallas_call(
        span_kernel,
        grid=(peers,),
        in_specs=[
            pl.BlockSpec((1, spans, rows, width), lambda i: (i, 0, 0, 0)),
            pl.BlockSpec(keys.shape, lambda i: (0, 0, 0)),
            pl.BlockSpec(values.shape, lambda i: (0, 0, 0)),
        ],
        out_specs=pl.BlockSpec((1, lines, width), lambda i: (i, 0, 0)),
        out_shape=jax.ShapeDtypeStruct((peers, lines, width), jnp.bfloat16),
        scratch_shapes=[pltpu.VMEM((2 * blocks, width), jnp.float32)],
        compiler_params=pltpu.CompilerParams(vmem_limit_bytes=48 * 1024 * 1024),
        cost_estimate=pl.CostEstimate(
            flops=4 * peers * spans * rows * keys.shape[1] * width,
            bytes_accessed=4 * peers * lines * width + 4 * keys.size,
            transcendentals=peers * spans * rows * keys.shape[1],
        ),
    )(q, keys, values)


def as_columns(line):
    count = line.shape[1]
    return jnp.concatenate(
        [
            jnp.broadcast_to(line[:, u : u + 128], (128, 128)).T
            for u in range(0, count, 128)
        ],
        axis=0,
    )


def merge_slots(data_refs, logs, targets, arrived):
    peers = data_refs[0].shape[0]
    data = jnp.concatenate([ref[x] for x in range(peers) for ref in data_refs], axis=0)
    rows = arrived_rows(arrived)
    slots = data.shape[0]
    column = as_columns(logs)
    column = jnp.concatenate([column] * (rows // 128), axis=1)
    mask = lax.broadcasted_iota(jnp.int32, (slots, rows), 1) == targets
    top = jnp.max(jnp.where(mask, column, EMPTY), axis=0, keepdims=True)
    states = []
    for ref in arrived[1]:
        width = ref.shape[0] - PAD
        log = jnp.sum(ref[width:, :].astype(jnp.float32), axis=0, keepdims=True)
        states.append((ref[:width, :].astype(jnp.float32), log))
        top = jnp.maximum(top, log)
    weights = jnp.where(mask, jnp.exp(column - top), 0.0)
    total = jnp.sum(weights, axis=0, keepdims=True)
    high = weights.astype(jnp.bfloat16)
    low = (weights - high.astype(jnp.float32)).astype(jnp.bfloat16)
    out = dot(data, high, ((0,), (0,))) + dot(data, low, ((0,), (0,)))
    for state, log in states:
        factor = jnp.exp(log - top)
        total = total + factor
        out = out + state * factor
    total = jnp.where(total == 0.0, 1.0, total)
    return out * (1.0 / total), top + jnp.log(total)


def arrived_rows(arrived):
    return arrived[0]


def step_kernel(rows, count, *refs):
    data_refs, logs_ref, targets_ref = refs[:2], refs[2], refs[3]
    out_ref = refs[-1]
    out, log = merge_slots(data_refs, logs_ref[0], targets_ref[0], (rows, refs[4 : 4 + count]))
    width = out.shape[0]
    out_ref[:width, :] = out.astype(jnp.bfloat16)
    parts = three_parts(log)
    rest = jnp.zeros((PAD - 3, rows), jnp.bfloat16)
    out_ref[width:, :] = jnp.concatenate(parts + [rest], axis=0)


def last_kernel(rows, count, *refs):
    data_refs, logs_ref, targets_ref = refs[:2], refs[2], refs[3]
    own_ref, own_log_ref, out_ref = refs[-3:]
    out, log = merge_slots(data_refs, logs_ref[0], targets_ref[0], (rows, refs[4 : 4 + count]))
    out = out.T
    log = as_columns(log)
    own_log = own_log_ref[...]
    top = jnp.maximum(log, own_log)
    far, near = jnp.exp(log - top), jnp.exp(own_log - top)
    merged = (far * out + near * own_ref[...]) / (far + near)
    out_ref[...] = merged.astype(jnp.bfloat16)


def merge_call(kernel, place, states, logs, targets, arrived, extra, rows, out_shape):
    peers, lines, width = states.shape
    blocks, _, slots = logs.shape
    group = slots // (2 * peers)

    def whole(a):
        return pl.BlockSpec(a.shape, lambda i, n=a.ndim: (0,) * n)

    return pl.pallas_call(
        lambda *refs: kernel(rows, len(arrived), *refs),
        grid=(1,),
        in_specs=[
            pl.BlockSpec((peers, group, width), lambda i: (0, place, 0)),
            pl.BlockSpec((peers, group, width), lambda i: (0, blocks + place, 0)),
            pl.BlockSpec((1, 1, slots), lambda i: (place, 0, 0)),
            pl.BlockSpec((1, slots, 1), lambda i: (place, 0, 0)),
        ]
        + [whole(a) for a in arrived + extra],
        out_specs=pl.BlockSpec(out_shape, lambda i: (0, 0)),
        out_shape=jax.ShapeDtypeStruct(out_shape, jnp.bfloat16),
        compiler_params=pltpu.CompilerParams(vmem_limit_bytes=32 * 1024 * 1024),
        cost_estimate=pl.CostEstimate(
            flops=4 * rows * slots * width,
            bytes_accessed=4 * rows * width,
            transcendentals=rows * slots,
        ),
    )(states, states, logs, targets, *arrived, *extra)


def own_states(grouped, cache_keys, cache_values, fresh_keys, fresh_values, live_len):
    scaling = grouped.shape[-1] ** (-0.5)
    step_count = grouped.shape[1]
    cache_slots = cache_keys.shape[1]
    cache_scores = (
        jnp.einsum("rsngd,rtnd->rsngt", grouped, cache_keys, preferred_element_type=jnp.float32)
        * scaling
    )
    fresh_scores = (
        jnp.einsum("rsngd,rtnd->rsngt", grouped, fresh_keys, preferred_element_type=jnp.float32)
        * scaling
    )
    cache_live = jnp.arange(cache_slots, dtype=jnp.int32)[None, :] < live_len[:, None]
    cache_scores = jnp.where(cache_live[:, None, None, None, :], cache_scores, EMPTY)
    causal = (
        jnp.arange(step_count, dtype=jnp.int32)[None, :]
        <= jnp.arange(step_count, dtype=jnp.int32)[:, None]
    )
    fresh_scores = jnp.where(causal[None, :, None, None, :], fresh_scores, EMPTY)
    highest = jnp.maximum(jnp.max(cache_scores, axis=-1), jnp.max(fresh_scores, axis=-1))
    cache_w = jnp.exp(cache_scores - highest[..., None])
    fresh_w = jnp.exp(fresh_scores - highest[..., None])
    summed = jnp.sum(cache_w, axis=-1) + jnp.sum(fresh_w, axis=-1)
    product = jnp.einsum(
        "rsngt,rtnd->rsngd",
        cache_w.astype(jnp.bfloat16),
        cache_values,
        preferred_element_type=jnp.float32,
    )
    product = product + jnp.einsum(
        "rsngt,rtnd->rsngd",
        fresh_w.astype(jnp.bfloat16),
        fresh_values,
        preferred_element_type=jnp.float32,
    )
    return (product / summed[..., None], highest + jnp.log(summed))


def local(
    queries,
    new_keys,
    new_values,
    suffix_keys,
    suffix_values,
    suffix_len,
    block_table,
    prefix_keys,
    prefix_values,
):
    requests, steps, heads, width = queries.shape
    span_count, span_len = prefix_keys.shape[:2]
    depth = block_table.shape[1]
    owners = lax.axis_size("req")
    nz = owners // NX
    half = nz // 2
    row = lax.axis_index("req") // NX
    z_groups = [[z * NX + x for z in range(nz)] for x in range(NX)]
    x_groups = [[z * NX + x for x in range(NX)] for z in range(nz)]
    keys = prefix_keys.reshape(span_count, span_len, width)
    values = prefix_values.reshape(span_count, span_len, width).transpose(0, 2, 1)

    def shift(array, by):
        pairs = [(z * NX + x, (z + by) % nz * NX + x) for z in range(nz) for x in range(NX)]
        return lax.ppermute(array, "req", pairs)

    per = steps // CHUNKS
    rows = per * heads
    pieces = []
    for c in range(CHUNKS):
        part = queries[:, c * per : (c + 1) * per].reshape(requests, rows, width)
        pieces.append({0: part})
    for k in range(1, half + 1):
        for c in range(CHUNKS):
            pieces[c][k] = shift(pieces[c][k - 1], -1)
            if k < half:
                pieces[c][nz - k] = shift(pieces[c][(nz - k + 1) % nz], 1)

    table = jnp.broadcast_to(block_table.reshape(1, -1), (nz, requests * depth))
    table = lax.all_to_all(
        table, "req", split_axis=0, concat_axis=0, tiled=True, axis_index_groups=z_groups
    )
    table = jnp.concatenate([table, table], axis=0)
    table = lax.dynamic_slice_in_dim(table, row, nz, 0).reshape(nz, requests, depth)
    here = row * NX * span_count + jnp.arange(NX * span_count, dtype=jnp.int32)
    match = jnp.any(table[None] == here[:, None, None, None], axis=-1)
    who = jnp.arange(requests, dtype=jnp.int32)
    first = jnp.min(jnp.where(match, who, requests), axis=-1)
    last = jnp.max(jnp.where(match, who, -1), axis=-1)
    chosen = jnp.stack(
        [jnp.where(last >= 0, first, -1), jnp.where(last > first, last, -1)], axis=-1
    )
    block_at = (jnp.arange(nz, dtype=jnp.int32) * requests)[None, :, None]
    pick = (jnp.maximum(chosen, 0) + block_at).reshape(NX, span_count, nz, CAP)
    slot_req = chosen.transpose(1, 0, 2).reshape(nz, NX * span_count * CAP)
    slots = NX * span_count * CAP * rows
    targets = slot_req[:, :, None] * rows + jnp.arange(rows, dtype=jnp.int32)
    targets = jnp.where(slot_req[:, :, None] >= 0, targets, -1).reshape(nz, slots, 1)

    kv_local = new_keys.shape[2]
    grouped = queries.reshape(requests, steps, kv_local, heads // kv_local, width)
    own_part, own_log = own_states(
        grouped, suffix_keys, suffix_values, new_keys, new_values, suffix_len
    )
    own_part = own_part.reshape(requests, steps, heads, width)
    own_log = jnp.broadcast_to(
        own_log.reshape(requests, steps, heads, 1), (requests, steps, heads, width)
    )

    state_shape = (width + PAD, requests * rows)
    flat = requests * rows
    all_states = []
    all_logs = []
    for c in range(CHUNKS):
        pool = jnp.concatenate([pieces[c][g] for g in range(nz)], axis=0)
        outgoing = pool[pick].reshape(NX, span_count * nz * CAP * rows, width)
        incoming = lax.all_to_all(
            outgoing, "req", split_axis=0, concat_axis=0, tiled=True, axis_index_groups=x_groups
        )
        incoming = incoming.reshape(NX, span_count, nz * CAP * rows, width)
        states = span_states(incoming, keys, values, nz)
        states = lax.all_to_all(
            states, "req", split_axis=0, concat_axis=0, tiled=True, axis_index_groups=x_groups
        )
        base = span_count * nz * CAP * rows
        lanes = span_count * CAP * rows
        logs = states[:, base:].reshape(NX, 2, nz, width).astype(jnp.float32)
        logs = logs[:, 0, :, :lanes] + logs[:, 0, :, lanes : 2 * lanes] + logs[:, 1, :, :lanes]
        logs = logs.transpose(1, 0, 2).reshape(nz, 1, slots)
        all_states.append(states)
        all_logs.append(logs)

    def step(c, place, arrived):
        return merge_call(
            step_kernel, place, all_states[c], all_logs[c], targets, arrived, [], flat, state_shape
        )

    down = [step(c, half, []) for c in range(CHUNKS)]
    up = [step(c, half - 1, []) for c in range(CHUNKS)]
    for k in range(half - 1, -1, -1):
        for c in range(CHUNKS):
            down[c] = shift(down[c], -1)
            if k > 0:
                down[c] = step(c, nz - k, [down[c]])
                up[c] = shift(up[c], 1)
                if k > 1:
                    up[c] = step(c, k - 1, [up[c]])
    kv_count = lax.axis_size("kv")
    results = []
    for c in range(CHUNKS):
        own_p = own_part[:, c * per : (c + 1) * per].reshape(flat, width)
        own_l = own_log[:, c * per : (c + 1) * per].reshape(flat, width)
        merged = merge_call(
            last_kernel, 0, all_states[c], all_logs[c], targets,
            [down[c], up[c]], [own_p, own_l], flat, (flat, width),
        )
        results.append(merged.reshape(requests // kv_count, kv_count, per, heads * width))
    merged = jnp.concatenate(results, axis=2)
    return lax.all_to_all(merged, "kv", split_axis=1, concat_axis=3, tiled=True)


def solution(mesh):
    placed = (
        P("req", None, "kv", None),
        P("req", None, "kv", None),
        P("req", None, "kv", None),
        P("req", None, "kv", None),
        P("req", None, "kv", None),
        P("req"),
        P("req", None),
        P("req", None, "kv", None),
        P("req", None, "kv", None),
    )
    return jax.shard_map(
        local, mesh=mesh, in_specs=placed, out_specs=P("req", "kv", None, None), check_vma=False
    )
```

time: 431 us -> 395 us (0.916)
  waiting for transfers between devices: 277 us -> 11.3 us
  starting transfers between devices: 36.5 us -> 215 us
  Pallas kernels: 0 us -> 64.3 us
  matrix products: 47.5 us -> 4.33 us
  local copies, waits for them, and re-layouts: 31.5 us -> 51.9 us
  blocking collectives: 18.2 us -> 37.4 us
  other arithmetic: 18.9 us -> 5.39 us
    all_to_all x3 -> x5, waiting for transfers between devices: 277 us -> 10.7 us  [the longest x1 9.51 us: local(): lax.all_to_all(table, 'req', split_axis=0, concat_axis=0, tiled=True, axi...]
    ppermute x0 -> x60, starting transfers between devices: none -> 192 us  [shift(): return lax.ppermute(array, 'req', pairs)]
    pallas_call x0 -> x34, Pallas kernels: none -> 64.3 us  [the longest x32 37.3 us: merge_call(): pl.pallas_call(lambda *refs: kernel(rows, len(arrived), *refs), grid=(1,)...]
    dot_general x32 -> x0, matrix products: 42.7 us -> none  [the longest x16 22.9 us: span_states(): jnp.einsum('bsngd,tnd->bsngt', queries_in, key_block, preferred_element_t...]
    unnamed x18 -> x71, local copies, waits for them, and re-layouts: 3.07 us -> 30.9 us
    all_to_all x1, blocking collectives: 18.2 us -> 37.4 us  [local(): return lax.all_to_all(merged, 'kv', split_axis=1, concat_axis=3, tiled=True)]
    scatter x1 -> x0, local copies, waits for them, and re-layouts: 13.7 us -> none  [local(): outgoing.at[slot_ids].set(jnp.repeat(grouped, depth_count, axis=0))]
    all_to_all x3 -> x5, starting transfers between devices: 36.5 us -> 23.3 us  [the longest x2 8.76 us: local(): lax.all_to_all(states, 'req', split_axis=0, concat_axis=0, tiled=True, ax...]
  transfers between devices with their start and end apart: 3 -> 65, of which waited for: 3 -> 3; matrix products, arithmetic and copies ran while one was open for 3% -> 13% of each run, Pallas kernels for 0% -> 16%
where the time goes in v1:
time: 395 us; the launch traced here: 391 us
  starting transfers between devices  215 us (54%)
  Pallas kernels  64.3 us (16%)
  local copies, waits for them, and re-layouts  51.9 us (13%)
  blocking collectives  37.4 us (9%)
  waiting for transfers between devices  11.3 us (3%)
  other arithmetic  5.39 us (1%)
  matrix products  4.33 us (1%)
    ppermute x60, starting transfers between devices, shift(): return lax.ppermute(array, 'req', pairs)  192 us
    all_to_all x1, blocking collectives, local(): return lax.all_to_all(merged, 'kv', split_axis=1, concat_axis=3, tiled=True)  37.4 us
    pallas_call x32, Pallas kernels, merge_call(): pl.pallas_call(lambda *refs: kernel(rows, len(arrived), *refs), grid=(1,)...  37.3 us
    unnamed x71, local copies, waits for them, and re-layouts  30.9 us
    pallas_call x2, Pallas kernels, span_states(): pl.pallas_call(span_kernel, grid=(peers,), in_specs=[pl.BlockSpec((1, spa...  27 us
    all_to_all x1, waiting for transfers between devices, local(): lax.all_to_all(table, 'req', split_axis=0, concat_axis=0, tiled=True, axi...  9.51 us
    all_to_all x2, starting transfers between devices, local(): lax.all_to_all(states, 'req', split_axis=0, concat_axis=0, tiled=True, ax...  8.76 us
  transfers between devices with their start and end apart: 65, of which 3 were waited for; matrix products, arithmetic and copies ran while one was open for 13% of the time, Pallas kernels for 16%

profile of v1, /device:TPU:1, one launch (start us, length us, event | category | flops | bytes accessed | tf_op | source)
XLA Modules:
  0.0 391.2 jit_solution(16618113165884363532)
XLA Ops:
  1.1 12.0 %collective-permute-start = (bf16[32,16,128]{2,1,0:T(8,128)(2,1)S(1)}, bf16[32,16,128]{2,1,0:T(8,128)(2,1)S(1)}, u32[]{:S(2)}, u32[]{:S(2)}) collective-permute-start(bf16[32,16,128]{2,1,0:T(8,128)(2,1)S(1)} %get-tuple-element.11), channel_id=1, source_target_pairs={{0,60},{1,61},{2,62},{3,63},{4,0},{5,1},{6,2},{7,3},{8,4},{9,5},{1... | collective-permute-start | bytes 393224 | tf_op jit(solution)/shard_map/ppermute | solution.py:242
  15.0 4.6 %collective-permute-start.30 = (bf16[32,16,128]{2,1,0:T(8,128)(2,1)S(1)}, bf16[32,16,128]{2,1,0:T(8,128)(2,1)S(1)}, u32[]{:S(2)}, u32[]{:S(2)}) collective-permute-start(bf16[32,16,128]{2,1,0:T(8,128)(2,1)S(1)} %get-tuple-element.12), channel_id=1, source_target_pairs={{0,60},{1,61},{2,62},{3,63},{4,0},{5,1},{6,2},{7,3},{8,4},{9,5},{1... | collective-permute-start | bytes 393224 | tf_op jit(solution)/shard_map/ppermute | solution.py:242
  23.0 7.0 %all-to-all-start = ((s32[16,1,128]{2,1,0:T(1,128)}), s32[16,1,128]{2,1,0:T(1,128)S(1)}, u32[]{:S(2)}, u32[]{:S(2)}) async-start(s32[16,1,128]{2,1,0:T(1,128)} %broadcast_in_dim.92), calls=%async_computation | async-start | bytes 16384 | tf_op jit(solution)/shard_map/all_to_all | solution.py:257
  31.7 9.5 %all-to-all-done = s32[16,1,128]{2,1,0:T(1,128)S(1)} async-done(((s32[16,1,128]{2,1,0:T(1,128)}), s32[16,1,128]{2,1,0:T(1,128)S(1)}, u32[]{:S(2)}, u32[]{:S(2)}) %all-to-all-start) | async-done | bytes 8224 | tf_op jit(solution)/shard_map/all_to_all | solution.py:257
  48.2 3.5 collective-permute-start.31
  54.2 4.6 %collective-permute-start.2 = (bf16[32,16,128]{2,1,0:T(8,128)(2,1)S(1)}, bf16[32,16,128]{2,1,0:T(8,128)(2,1)S(1)}, u32[]{:S(2)}, u32[]{:S(2)}) collective-permute-start(bf16[32,16,128]{2,1,0:T(8,128)(2,1)S(1)} %collective-permute-done.1), channel_id=1, source_target_pairs={{0,60},{1,61},{2,62},{3,63},{4,0},{5,1},{6,2},{7,3},{8,4},{9,5},{1... | collective-permute-start | bytes 393224 | tf_op jit(solution)/shard_map/ppermute | solution.py:242
  61.4 4.6 %collective-permute-start.32 = (bf16[32,16,128]{2,1,0:T(8,128)(2,1)S(1)}, bf16[32,16,128]{2,1,0:T(8,128)(2,1)S(1)}, u32[]{:S(2)}, u32[]{:S(2)}) collective-permute-start(bf16[32,16,128]{2,1,0:T(8,128)(2,1)S(1)} %collective-permute-done.31), channel_id=1, source_target_pairs={{0,60},{1,61},{2,62},{3,63},{4,0},{5,1},{6,2},{7,3},{8,4},{9,5},{1... | collective-permute-start | bytes 393224 | tf_op jit(solution)/shard_map/ppermute | solution.py:242
  68.6 4.6 %collective-permute-start.3 = (bf16[32,16,128]{2,1,0:T(8,128)(2,1)S(1)}, bf16[32,16,128]{2,1,0:T(8,128)(2,1)S(1)}, u32[]{:S(2)}, u32[]{:S(2)}) collective-permute-start(bf16[32,16,128]{2,1,0:T(8,128)(2,1)S(1)} %collective-permute-done.2), channel_id=1, source_target_pairs={{0,60},{1,61},{2,62},{3,63},{4,0},{5,1},{6,2},{7,3},{8,4},{9,5},{1... | collective-permute-start | bytes 393224 | tf_op jit(solution)/shard_map/ppermute | solution.py:242
  75.8 4.6 %collective-permute-start.33 = (bf16[32,16,128]{2,1,0:T(8,128)(2,1)S(1)}, bf16[32,16,128]{2,1,0:T(8,128)(2,1)S(1)}, u32[]{:S(2)}, u32[]{:S(2)}) collective-permute-start(bf16[32,16,128]{2,1,0:T(8,128)(2,1)S(1)} %collective-permute-done.32), channel_id=1, source_target_pairs={{0,60},{1,61},{2,62},{3,63},{4,0},{5,1},{6,2},{7,3},{8,4},{9,5},{1... | collective-permute-start | bytes 393224 | tf_op jit(solution)/shard_map/ppermute | solution.py:242
  82.9 4.6 %collective-permute-start.4 = (bf16[32,16,128]{2,1,0:T(8,128)(2,1)S(1)}, bf16[32,16,128]{2,1,0:T(8,128)(2,1)S(1)}, u32[]{:S(2)}, u32[]{:S(2)}) collective-permute-start(bf16[32,16,128]{2,1,0:T(8,128)(2,1)S(1)} %collective-permute-done.3), channel_id=1, source_target_pairs={{0,60},{1,61},{2,62},{3,63},{4,0},{5,1},{6,2},{7,3},{8,4},{9,5},{1... | collective-permute-start | bytes 393224 | tf_op jit(solution)/shard_map/ppermute | solution.py:242
  90.1 4.6 %collective-permute-start.34 = (bf16[32,16,128]{2,1,0:T(8,128)(2,1)S(1)}, bf16[32,16,128]{2,1,0:T(8,128)(2,1)S(1)}, u32[]{:S(2)}, u32[]{:S(2)}) collective-permute-start(bf16[32,16,128]{2,1,0:T(8,128)(2,1)S(1)} %collective-permute-done.33), channel_id=1, source_target_pairs={{0,60},{1,61},{2,62},{3,63},{4,0},{5,1},{6,2},{7,3},{8,4},{9,5},{1... | collective-permute-start | bytes 393224 | tf_op jit(solution)/shard_map/ppermute | solution.py:242
  97.3 4.6 %collective-permute-start.5 = (bf16[32,16,128]{2,1,0:T(8,128)(2,1)S(1)}, bf16[32,16,128]{2,1,0:T(8,128)(2,1)S(1)}, u32[]{:S(2)}, u32[]{:S(2)}) collective-permute-start(bf16[32,16,128]{2,1,0:T(8,128)(2,1)S(1)} %collective-permute-done.4), channel_id=1, source_target_pairs={{0,60},{1,61},{2,62},{3,63},{4,0},{5,1},{6,2},{7,3},{8,4},{9,5},{1... | collective-permute-start | bytes 393224 | tf_op jit(solution)/shard_map/ppermute | solution.py:242
  104.5 4.6 %collective-permute-start.35 = (bf16[32,16,128]{2,1,0:T(8,128)(2,1)S(1)}, bf16[32,16,128]{2,1,0:T(8,128)(2,1)S(1)}, u32[]{:S(2)}, u32[]{:S(2)}) collective-permute-start(bf16[32,16,128]{2,1,0:T(8,128)(2,1)S(1)} %collective-permute-done.34), channel_id=1, source_target_pairs={{0,60},{1,61},{2,62},{3,63},{4,0},{5,1},{6,2},{7,3},{8,4},{9,5},{1... | collective-permute-start | bytes 393224 | tf_op jit(solution)/shard_map/ppermute | solution.py:242
  111.6 4.6 %collective-permute-start.6 = (bf16[32,16,128]{2,1,0:T(8,128)(2,1)S(1)}, bf16[32,16,128]{2,1,0:T(8,128)(2,1)S(1)}, u32[]{:S(2)}, u32[]{:S(2)}) collective-permute-start(bf16[32,16,128]{2,1,0:T(8,128)(2,1)S(1)} %collective-permute-done.5), channel_id=1, source_target_pairs={{0,60},{1,61},{2,62},{3,63},{4,0},{5,1},{6,2},{7,3},{8,4},{9,5},{1... | collective-permute-start | bytes 393224 | tf_op jit(solution)/shard_map/ppermute | solution.py:242
  118.8 4.6 %collective-permute-start.36 = (bf16[32,16,128]{2,1,0:T(8,128)(2,1)S(1)}, bf16[32,16,128]{2,1,0:T(8,128)(2,1)S(1)}, u32[]{:S(2)}, u32[]{:S(2)}) collective-permute-start(bf16[32,16,128]{2,1,0:T(8,128)(2,1)S(1)} %collective-permute-done.35), channel_id=1, source_target_pairs={{0,60},{1,61},{2,62},{3,63},{4,0},{5,1},{6,2},{7,3},{8,4},{9,5},{1... | collective-permute-start | bytes 393224 | tf_op jit(solution)/shard_map/ppermute | solution.py:242
  126.0 4.6 %collective-permute-start.7 = (bf16[32,16,128]{2,1,0:T(8,128)(2,1)S(1)}, bf16[32,16,128]{2,1,0:T(8,128)(2,1)S(1)}, u32[]{:S(2)}, u32[]{:S(2)}) collective-permute-start(bf16[32,16,128]{2,1,0:T(8,128)(2,1)S(1)} %collective-permute-done.6), channel_id=1, source_target_pairs={{0,60},{1,61},{2,62},{3,63},{4,0},{5,1},{6,2},{7,3},{8,4},{9,5},{1... | collective-permute-start | bytes 393224 | tf_op jit(solution)/shard_map/ppermute | solution.py:242
  139.1 3.4 gather_fusion
  142.5 4.0 %all-to-all-start.1 = ((bf16[4,1024,128]{2,1,0:T(8,128)(2,1)}), bf16[4,1024,128]{2,1,0:T(8,128)(2,1)S(1)}, u32[]{:S(2)}, u32[]{:S(2)}) async-start(bf16[4,1024,128]{2,1,0:T(8,128)(2,1)} %bitcast.7), calls=%async_computation.1 | async-start | bytes 2097152 | tf_op jit(solution)/shard_map/all_to_all | solution.py:294
  156.2 3.5 all-to-all-start.3
  163.9 13.5 %shard_map.91 = bf16[4,1056,128]{2,1,0:T(8,128)(2,1)} custom-call(bf16[4,2,512,128]{3,2,1,0:T(8,128)(2,1)S(1)} %bitcast.132, bf16[2,1024,128]{2,1,0:T(8,128)(2,1)S(1)} %bitcast.138, bf16[2,128,1024]{2,1,0:T(8,128)(2,1)S(1)} %bitcast.136), custom_call_target="tpu_custom_call" | custom-call | flops 2147483648 | bytes 3211264 | tf_op jit(solution)/shard_map/pallas_call | solution.py:63
  177.4 4.3 %all-to-all-start.2 = ((bf16[4,1056,128]{2,1,0:T(8,128)(2,1)}), bf16[4,1056,128]{2,1,0:T(8,128)(2,1)S(1)}, u32[]{:S(2)}, u32[]{:S(2)}) async-start(bf16[4,1056,128]{2,1,0:T(8,128)(2,1)} %shard_map.91), calls=%async_computation.2 | async-start | bytes 2162688 | tf_op jit(solution)/shard_map/all_to_all | solution.py:299
  185.5 13.5 %shard_map.108 = bf16[4,1056,128]{2,1,0:T(8,128)(2,1)} custom-call(bf16[4,2,512,128]{3,2,1,0:T(8,128)(2,1)S(1)} %bitcast.133, bf16[2,1024,128]{2,1,0:T(8,128)(2,1)S(1)} %bitcast.139, bf16[2,128,1024]{2,1,0:T(8,128)(2,1)S(1)} %bitcast.137), custom_call_target="tpu_custom_call" | custom-call | flops 2147483648 | bytes 3211264 | tf_op jit(solution)/shard_map/pallas_call | solution.py:63
  198.9 4.4 %all-to-all-start.4 = ((bf16[4,1056,128]{2,1,0:T(8,128)(2,1)}), bf16[4,1056,128]{2,1,0:T(8,128)(2,1)}, u32[]{:S(2)}, u32[]{:S(2)}) async-start(bf16[4,1056,128]{2,1,0:T(8,128)(2,1)} %shard_map.108), calls=%async_computation.4 | async-start | bytes 2162688 | tf_op jit(solution)/shard_map/all_to_all | solution.py:299
  212.5 3.7 collective-permute-start.15
  231.3 4.6 %collective-permute-start.16 = (bf16[144,512]{1,0:T(8,128)(2,1)S(1)}, bf16[144,512]{1,0:T(8,128)(2,1)S(1)}, u32[]{:S(2)}, u32[]{:S(2)}) collective-permute-start(bf16[144,512]{1,0:T(8,128)(2,1)S(1)} %shard_map.93), channel_id=1, source_target_pairs={{0,60},{1,61},{2,62},{3,63},{4,0},{5,1},{6,2},{7,3},{8,4},{9,5},{1... | collective-permute-start | bytes 442376 | tf_op jit(solution)/shard_map/ppermute | solution.py:242
  247.5 4.7 %collective-permute-start.17 = (bf16[144,512]{1,0:T(8,128)(2,1)S(1)}, bf16[144,512]{1,0:T(8,128)(2,1)S(1)}, u32[]{:S(2)}, u32[]{:S(2)}) collective-permute-start(bf16[144,512]{1,0:T(8,128)(2,1)S(1)} %shard_map.94), channel_id=1, source_target_pairs={{0,60},{1,61},{2,62},{3,63},{4,0},{5,1},{6,2},{7,3},{8,4},{9,5},{1... | collective-permute-start | bytes 442376 | tf_op jit(solution)/shard_map/ppermute | solution.py:242
  264.0 4.6 %collective-permute-start.18 = (bf16[144,512]{1,0:T(8,128)(2,1)S(1)}, bf16[144,512]{1,0:T(8,128)(2,1)S(1)}, u32[]{:S(2)}, u32[]{:S(2)}) collective-permute-start(bf16[144,512]{1,0:T(8,128)(2,1)S(1)} %shard_map.95), channel_id=1, source_target_pairs={{0,60},{1,61},{2,62},{3,63},{4,0},{5,1},{6,2},{7,3},{8,4},{9,5},{1... | collective-permute-start | bytes 442376 | tf_op jit(solution)/shard_map/ppermute | solution.py:242
  280.4 4.6 %collective-permute-start.19 = (bf16[144,512]{1,0:T(8,128)(2,1)S(1)}, bf16[144,512]{1,0:T(8,128)(2,1)S(1)}, u32[]{:S(2)}, u32[]{:S(2)}) collective-permute-start(bf16[144,512]{1,0:T(8,128)(2,1)S(1)} %shard_map.96), channel_id=1, source_target_pairs={{0,60},{1,61},{2,62},{3,63},{4,0},{5,1},{6,2},{7,3},{8,4},{9,5},{1... | collective-permute-start | bytes 442376 | tf_op jit(solution)/shard_map/ppermute | solution.py:242
  296.3 4.7 %collective-permute-start.20 = (bf16[144,512]{1,0:T(8,128)(2,1)S(1)}, bf16[144,512]{1,0:T(8,128)(2,1)S(1)}, u32[]{:S(2)}, u32[]{:S(2)}) collective-permute-start(bf16[144,512]{1,0:T(8,128)(2,1)S(1)} %shard_map.97), channel_id=1, source_target_pairs={{0,60},{1,61},{2,62},{3,63},{4,0},{5,1},{6,2},{7,3},{8,4},{9,5},{1... | collective-permute-start | bytes 442376 | tf_op jit(solution)/shard_map/ppermute | solution.py:242
  314.9 4.6 %collective-permute-start.21 = (bf16[144,512]{1,0:T(8,128)(2,1)}, bf16[144,512]{1,0:T(8,128)(2,1)}, u32[]{:S(2)}, u32[]{:S(2)}) collective-permute-start(bf16[144,512]{1,0:T(8,128)(2,1)} %shard_map.98), channel_id=1, source_target_pairs={{0,60},{1,61},{2,62},{3,63},{4,0},{5,1},{6,2},{7,3},{8,4},{9,5},{1... | collective-permute-start | bytes 442376 | tf_op jit(solution)/shard_map/ppermute | solution.py:242
  334.8 4.7 %collective-permute-start.22 = (bf16[144,512]{1,0:T(8,128)(2,1)S(1)}, bf16[144,512]{1,0:T(8,128)(2,1)S(1)}, u32[]{:S(2)}, u32[]{:S(2)}) collective-permute-start(bf16[144,512]{1,0:T(8,128)(2,1)S(1)} %shard_map.99), channel_id=1, source_target_pairs={{0,60},{1,61},{2,62},{3,63},{4,0},{5,1},{6,2},{7,3},{8,4},{9,5},{1... | collective-permute-start | bytes 442376 | tf_op jit(solution)/shard_map/ppermute | solution.py:242
  353.1 37.4 %all_to_all.47 = bf16[4,8,4,1024]{3,2,0,1:T(4,128)(2,1)S(1)} all-to-all(bf16[4,8,4,1024]{3,2,0,1:T(4,128)(2,1)S(1)} %copy.101), channel_id=1, replica_groups=mesh['kv'=8,'req'=64] {'kv'}, dimensions={1} | all-to-all | bytes 524288 | tf_op jit(solution)/shard_map/all_to_all | solution.py:336
  (268 shorter events, 182.9 us)
Async XLA Ops:
  1.1 41.1 %collective-permute-start = (bf16[32,16,128]{2,1,0:T(8,128)(2,1)S(1)}, bf16[32,16,128]{2,1,0:T(8,128)(2,1)S(1)}, u32[]{:S(2)}, u32[]{:S(2)}) collective-permute-start(bf16[32,16,128]{2,1,0:T(8,128)(2,1)S(1)} %get-tuple-element.11), channel_id=1, source_target_pairs={{0,60},{1,61},{2,62},{3,63},{4,0},{5,1},{6,2},{7,3},{8,4},{9,5},{1... | collective-permute-start | bytes 393224 | tf_op jit(solution)/shard_map/ppermute | solution.py:242
  13.0 32.1 %collective-permute-start.8 = (bf16[32,16,128]{2,1,0:T(8,128)(2,1)S(1)}, bf16[32,16,128]{2,1,0:T(8,128)(2,1)S(1)}, u32[]{:S(2)}, u32[]{:S(2)}) collective-permute-start(bf16[32,16,128]{2,1,0:T(8,128)(2,1)S(1)} %get-tuple-element.11), channel_id=1, source_target_pairs={{0,4},{1,5},{2,6},{3,7},{4,8},{5,9},{6,10},{7,11},{8,12},{9,13},{1... | collective-permute-start | bytes 393224 | tf_op jit(solution)/shard_map/ppermute | solution.py:242
  15.0 33.2 %collective-permute-start.30 = (bf16[32,16,128]{2,1,0:T(8,128)(2,1)S(1)}, bf16[32,16,128]{2,1,0:T(8,128)(2,1)S(1)}, u32[]{:S(2)}, u32[]{:S(2)}) collective-permute-start(bf16[32,16,128]{2,1,0:T(8,128)(2,1)S(1)} %get-tuple-element.12), channel_id=1, source_target_pairs={{0,60},{1,61},{2,62},{3,63},{4,0},{5,1},{6,2},{7,3},{8,4},{9,5},{1... | collective-permute-start | bytes 393224 | tf_op jit(solution)/shard_map/ppermute | solution.py:242
  19.5 32.8 %collective-permute-start.38 = (bf16[32,16,128]{2,1,0:T(8,128)(2,1)S(1)}, bf16[32,16,128]{2,1,0:T(8,128)(2,1)S(1)}, u32[]{:S(2)}, u32[]{:S(2)}) collective-permute-start(bf16[32,16,128]{2,1,0:T(8,128)(2,1)S(1)} %get-tuple-element.12), channel_id=1, source_target_pairs={{0,4},{1,5},{2,6},{3,7},{4,8},{5,9},{6,10},{7,11},{8,12},{9,13},{1... | collective-permute-start | bytes 393224 | tf_op jit(solution)/shard_map/ppermute | solution.py:242
  23.0 18.3 %all-to-all-start = ((s32[16,1,128]{2,1,0:T(1,128)}), s32[16,1,128]{2,1,0:T(1,128)S(1)}, u32[]{:S(2)}, u32[]{:S(2)}) async-start(s32[16,1,128]{2,1,0:T(1,128)} %broadcast_in_dim.92), calls=%async_computation | async-start | bytes 16384 | tf_op jit(solution)/shard_map/all_to_all | solution.py:257
  116.9 17.6 %collective-permute-start.14 = (bf16[32,16,128]{2,1,0:T(8,128)(2,1)S(1)}, bf16[32,16,128]{2,1,0:T(8,128)(2,1)S(1)}, u32[]{:S(2)}, u32[]{:S(2)}) collective-permute-start(bf16[32,16,128]{2,1,0:T(8,128)(2,1)S(1)} %collective-permute-done.13), channel_id=1, source_target_pairs={{0,4},{1,5},{2,6},{3,7},{4,8},{5,9},{6,10},{7,11},{8,12},{9,13},{1... | collective-permute-start | bytes 393224 | tf_op jit(solution)/shard_map/ppermute | solution.py:242
  124.0 23.1 %collective-permute-start.44 = (bf16[32,16,128]{2,1,0:T(8,128)(2,1)S(1)}, bf16[32,16,128]{2,1,0:T(8,128)(2,1)S(1)}, u32[]{:S(2)}, u32[]{:S(2)}) collective-permute-start(bf16[32,16,128]{2,1,0:T(8,128)(2,1)S(1)} %collective-permute-done.43), channel_id=1, source_target_pairs={{0,4},{1,5},{2,6},{3,7},{4,8},{5,9},{6,10},{7,11},{8,12},{9,13},{1... | collective-permute-start | bytes 393224 | tf_op jit(solution)/shard_map/ppermute | solution.py:242
  131.2 15.3 %collective-permute-start.37 = (bf16[32,16,128]{2,1,0:T(8,128)(2,1)S(1)}, bf16[32,16,128]{2,1,0:T(8,128)(2,1)S(1)}, u32[]{:S(2)}, u32[]{:S(2)}) collective-permute-start(bf16[32,16,128]{2,1,0:T(8,128)(2,1)S(1)} %collective-permute-done.36), channel_id=1, source_target_pairs={{0,60},{1,61},{2,62},{3,63},{4,0},{5,1},{6,2},{7,3},{8,4},{9,5},{1... | collective-permute-start | bytes 393224 | tf_op jit(solution)/shard_map/ppermute | solution.py:242
  156.2 21.2 %all-to-all-start.3 = ((bf16[4,1024,128]{2,1,0:T(8,128)(2,1)}), bf16[4,1024,128]{2,1,0:T(8,128)(2,1)S(1)}, u32[]{:S(2)}, u32[]{:S(2)}) async-start(bf16[4,1024,128]{2,1,0:T(8,128)(2,1)} %bitcast.140), calls=%async_computation.3 | async-start | bytes 2097152 | tf_op jit(solution)/shard_map/all_to_all | solution.py:294
  177.4 21.5 %all-to-all-start.2 = ((bf16[4,1056,128]{2,1,0:T(8,128)(2,1)}), bf16[4,1056,128]{2,1,0:T(8,128)(2,1)S(1)}, u32[]{:S(2)}, u32[]{:S(2)}) async-start(bf16[4,1056,128]{2,1,0:T(8,128)(2,1)} %shard_map.91), calls=%async_computation.2 | async-start | bytes 2162688 | tf_op jit(solution)/shard_map/all_to_all | solution.py:299
  198.9 17.3 %all-to-all-start.4 = ((bf16[4,1056,128]{2,1,0:T(8,128)(2,1)}), bf16[4,1056,128]{2,1,0:T(8,128)(2,1)}, u32[]{:S(2)}, u32[]{:S(2)}) async-start(bf16[4,1056,128]{2,1,0:T(8,128)(2,1)} %shard_map.108), calls=%async_computation.4 | async-start | bytes 2162688 | tf_op jit(solution)/shard_map/all_to_all | solution.py:299
  212.5 18.1 %collective-permute-start.15 = (bf16[144,512]{1,0:T(8,128)(2,1)S(1)}, bf16[144,512]{1,0:T(8,128)(2,1)S(1)}, u32[]{:S(2)}, u32[]{:S(2)}) collective-permute-start(bf16[144,512]{1,0:T(8,128)(2,1)S(1)} %shard_map.92), channel_id=1, source_target_pairs={{0,60},{1,61},{2,62},{3,63},{4,0},{5,1},{6,2},{7,3},{8,4},{9,5},{1... | collective-permute-start | bytes 442376 | tf_op jit(solution)/shard_map/ppermute | solution.py:242
  220.1 15.8 %collective-permute-start.45 = (bf16[144,512]{1,0:T(8,128)(2,1)S(1)}, bf16[144,512]{1,0:T(8,128)(2,1)S(1)}, u32[]{:S(2)}, u32[]{:S(2)}) collective-permute-start(bf16[144,512]{1,0:T(8,128)(2,1)S(1)} %shard_map.109), channel_id=1, source_target_pairs={{0,60},{1,61},{2,62},{3,63},{4,0},{5,1},{6,2},{7,3},{8,4},{9,5},{1... | collective-permute-start | bytes 442376 | tf_op jit(solution)/shard_map/ppermute | solution.py:242
  224.8 15.6 %collective-permute-start.23 = (bf16[144,512]{1,0:T(8,128)(2,1)S(1)}, bf16[144,512]{1,0:T(8,128)(2,1)S(1)}, u32[]{:S(2)}, u32[]{:S(2)}) collective-permute-start(bf16[144,512]{1,0:T(8,128)(2,1)S(1)} %shard_map.100), channel_id=1, source_target_pairs={{0,4},{1,5},{2,6},{3,7},{4,8},{5,9},{6,10},{7,11},{8,12},{9,13},{1... | collective-permute-start | bytes 442376 | tf_op jit(solution)/shard_map/ppermute | solution.py:242
  231.3 15.6 %collective-permute-start.16 = (bf16[144,512]{1,0:T(8,128)(2,1)S(1)}, bf16[144,512]{1,0:T(8,128)(2,1)S(1)}, u32[]{:S(2)}, u32[]{:S(2)}) collective-permute-start(bf16[144,512]{1,0:T(8,128)(2,1)S(1)} %shard_map.93), channel_id=1, source_target_pairs={{0,60},{1,61},{2,62},{3,63},{4,0},{5,1},{6,2},{7,3},{8,4},{9,5},{1... | collective-permute-start | bytes 442376 | tf_op jit(solution)/shard_map/ppermute | solution.py:242
  241.0 15.8 %collective-permute-start.24 = (bf16[144,512]{1,0:T(8,128)(2,1)S(1)}, bf16[144,512]{1,0:T(8,128)(2,1)S(1)}, u32[]{:S(2)}, u32[]{:S(2)}) collective-permute-start(bf16[144,512]{1,0:T(8,128)(2,1)S(1)} %shard_map.101), channel_id=1, source_target_pairs={{0,4},{1,5},{2,6},{3,7},{4,8},{5,9},{6,10},{7,11},{8,12},{9,13},{1... | collective-permute-start | bytes 442376 | tf_op jit(solution)/shard_map/ppermute | solution.py:242
  244.9 15.1 %collective-permute-start.54 = (bf16[144,512]{1,0:T(8,128)(2,1)S(1)}, bf16[144,512]{1,0:T(8,128)(2,1)S(1)}, u32[]{:S(2)}, u32[]{:S(2)}) collective-permute-start(bf16[144,512]{1,0:T(8,128)(2,1)S(1)} %shard_map.118), channel_id=1, source_target_pairs={{0,4},{1,5},{2,6},{3,7},{4,8},{5,9},{6,10},{7,11},{8,12},{9,13},{1... | collective-permute-start | bytes 442376 | tf_op jit(solution)/shard_map/ppermute | solution.py:242
  247.5 15.8 %collective-permute-start.17 = (bf16[144,512]{1,0:T(8,128)(2,1)S(1)}, bf16[144,512]{1,0:T(8,128)(2,1)S(1)}, u32[]{:S(2)}, u32[]{:S(2)}) collective-permute-start(bf16[144,512]{1,0:T(8,128)(2,1)S(1)} %shard_map.94), channel_id=1, source_target_pairs={{0,60},{1,61},{2,62},{3,63},{4,0},{5,1},{6,2},{7,3},{8,4},{9,5},{1... | collective-permute-start | bytes 442376 | tf_op jit(solution)/shard_map/ppermute | solution.py:242
  257.5 15.5 %collective-permute-start.25 = (bf16[144,512]{1,0:T(8,128)(2,1)S(1)}, bf16[144,512]{1,0:T(8,128)(2,1)S(1)}, u32[]{:S(2)}, u32[]{:S(2)}) collective-permute-start(bf16[144,512]{1,0:T(8,128)(2,1)S(1)} %shard_map.102), channel_id=1, source_target_pairs={{0,4},{1,5},{2,6},{3,7},{4,8},{5,9},{6,10},{7,11},{8,12},{9,13},{1... | collective-permute-start | bytes 442376 | tf_op jit(solution)/shard_map/ppermute | solution.py:242
  264.0 15.7 %collective-permute-start.18 = (bf16[144,512]{1,0:T(8,128)(2,1)S(1)}, bf16[144,512]{1,0:T(8,128)(2,1)S(1)}, u32[]{:S(2)}, u32[]{:S(2)}) collective-permute-start(bf16[144,512]{1,0:T(8,128)(2,1)S(1)} %shard_map.95), channel_id=1, source_target_pairs={{0,60},{1,61},{2,62},{3,63},{4,0},{5,1},{6,2},{7,3},{8,4},{9,5},{1... | collective-permute-start | bytes 442376 | tf_op jit(solution)/shard_map/ppermute | solution.py:242
  273.6 15.5 %collective-permute-start.26 = (bf16[144,512]{1,0:T(8,128)(2,1)S(1)}, bf16[144,512]{1,0:T(8,128)(2,1)S(1)}, u32[]{:S(2)}, u32[]{:S(2)}) collective-permute-start(bf16[144,512]{1,0:T(8,128)(2,1)S(1)} %shard_map.103), channel_id=1, source_target_pairs={{0,4},{1,5},{2,6},{3,7},{4,8},{5,9},{6,10},{7,11},{8,12},{9,13},{1... | collective-permute-start | bytes 442376 | tf_op jit(solution)/shard_map/ppermute | solution.py:242
  280.4 15.3 %collective-permute-start.19 = (bf16[144,512]{1,0:T(8,128)(2,1)S(1)}, bf16[144,512]{1,0:T(8,128)(2,1)S(1)}, u32[]{:S(2)}, u32[]{:S(2)}) collective-permute-start(bf16[144,512]{1,0:T(8,128)(2,1)S(1)} %shard_map.96), channel_id=1, source_target_pairs={{0,60},{1,61},{2,62},{3,63},{4,0},{5,1},{6,2},{7,3},{8,4},{9,5},{1... | collective-permute-start | bytes 442376 | tf_op jit(solution)/shard_map/ppermute | solution.py:242
  289.7 16.7 %collective-permute-start.27 = (bf16[144,512]{1,0:T(8,128)(2,1)S(1)}, bf16[144,512]{1,0:T(8,128)(2,1)S(1)}, u32[]{:S(2)}, u32[]{:S(2)}) collective-permute-start(bf16[144,512]{1,0:T(8,128)(2,1)S(1)} %shard_map.104), channel_id=1, source_target_pairs={{0,4},{1,5},{2,6},{3,7},{4,8},{5,9},{6,10},{7,11},{8,12},{9,13},{1... | collective-permute-start | bytes 442376 | tf_op jit(solution)/shard_map/ppermute | solution.py:242
  293.7 15.9 %collective-permute-start.57 = (bf16[144,512]{1,0:T(8,128)(2,1)S(1)}, bf16[144,512]{1,0:T(8,128)(2,1)S(1)}, u32[]{:S(2)}, u32[]{:S(2)}) collective-permute-start(bf16[144,512]{1,0:T(8,128)(2,1)S(1)} %shard_map.121), channel_id=1, source_target_pairs={{0,4},{1,5},{2,6},{3,7},{4,8},{5,9},{6,10},{7,11},{8,12},{9,13},{1... | collective-permute-start | bytes 442376 | tf_op jit(solution)/shard_map/ppermute | solution.py:242
  296.3 17.3 %collective-permute-start.20 = (bf16[144,512]{1,0:T(8,128)(2,1)S(1)}, bf16[144,512]{1,0:T(8,128)(2,1)S(1)}, u32[]{:S(2)}, u32[]{:S(2)}) collective-permute-start(bf16[144,512]{1,0:T(8,128)(2,1)S(1)} %shard_map.97), channel_id=1, source_target_pairs={{0,60},{1,61},{2,62},{3,63},{4,0},{5,1},{6,2},{7,3},{8,4},{9,5},{1... | collective-permute-start | bytes 442376 | tf_op jit(solution)/shard_map/ppermute | solution.py:242
  302.4 17.1 %collective-permute-start.50 = (bf16[144,512]{1,0:T(8,128)(2,1)S(1)}, bf16[144,512]{1,0:T(8,128)(2,1)S(1)}, u32[]{:S(2)}, u32[]{:S(2)}) collective-permute-start(bf16[144,512]{1,0:T(8,128)(2,1)S(1)} %shard_map.114), channel_id=1, source_target_pairs={{0,60},{1,61},{2,62},{3,63},{4,0},{5,1},{6,2},{7,3},{8,4},{9,5},{1... | collective-permute-start | bytes 442376 | tf_op jit(solution)/shard_map/ppermute | solution.py:242
  307.1 17.5 %collective-permute-start.28 = (bf16[144,512]{1,0:T(8,128)(2,1)S(1)}, bf16[144,512]{1,0:T(8,128)(2,1)S(1)}, u32[]{:S(2)}, u32[]{:S(2)}) collective-permute-start(bf16[144,512]{1,0:T(8,128)(2,1)S(1)} %shard_map.105), channel_id=1, source_target_pairs={{0,4},{1,5},{2,6},{3,7},{4,8},{5,9},{6,10},{7,11},{8,12},{9,13},{1... | collective-permute-start | bytes 442376 | tf_op jit(solution)/shard_map/ppermute | solution.py:242
  311.7 17.4 %collective-permute-start.58 = (bf16[144,512]{1,0:T(8,128)(2,1)}, bf16[144,512]{1,0:T(8,128)(2,1)}, u32[]{:S(2)}, u32[]{:S(2)}) collective-permute-start(bf16[144,512]{1,0:T(8,128)(2,1)} %shard_map.122), channel_id=1, source_target_pairs={{0,4},{1,5},{2,6},{3,7},{4,8},{5,9},{6,10},{7,11},{8,12},{9,13},{1... | collective-permute-start | bytes 442376 | tf_op jit(solution)/shard_map/ppermute | solution.py:242
  314.9 18.3 %collective-permute-start.21 = (bf16[144,512]{1,0:T(8,128)(2,1)}, bf16[144,512]{1,0:T(8,128)(2,1)}, u32[]{:S(2)}, u32[]{:S(2)}) collective-permute-start(bf16[144,512]{1,0:T(8,128)(2,1)} %shard_map.98), channel_id=1, source_target_pairs={{0,60},{1,61},{2,62},{3,63},{4,0},{5,1},{6,2},{7,3},{8,4},{9,5},{1... | collective-permute-start | bytes 442376 | tf_op jit(solution)/shard_map/ppermute | solution.py:242
  321.5 18.0 %collective-permute-start.51 = (bf16[144,512]{1,0:T(8,128)(2,1)}, bf16[144,512]{1,0:T(8,128)(2,1)}, u32[]{:S(2)}, u32[]{:S(2)}) collective-permute-start(bf16[144,512]{1,0:T(8,128)(2,1)} %shard_map.115), channel_id=1, source_target_pairs={{0,60},{1,61},{2,62},{3,63},{4,0},{5,1},{6,2},{7,3},{8,4},{9,5},{1... | collective-permute-start | bytes 442376 | tf_op jit(solution)/shard_map/ppermute | solution.py:242
  326.4 18.1 %collective-permute-start.29 = (bf16[144,512]{1,0:T(8,128)(2,1)S(1)}, bf16[144,512]{1,0:T(8,128)(2,1)S(1)}, u32[]{:S(2)}, u32[]{:S(2)}) collective-permute-start(bf16[144,512]{1,0:T(8,128)(2,1)S(1)} %shard_map.106), channel_id=1, source_target_pairs={{0,4},{1,5},{2,6},{3,7},{4,8},{5,9},{6,10},{7,11},{8,12},{9,13},{1... | collective-permute-start | bytes 442376 | tf_op jit(solution)/shard_map/ppermute | solution.py:242
  331.3 16.4 %collective-permute-start.59 = (bf16[144,512]{1,0:T(8,128)(2,1)}, bf16[144,512]{1,0:T(8,128)(2,1)}, u32[]{:S(2)}, u32[]{:S(2)}) collective-permute-start(bf16[144,512]{1,0:T(8,128)(2,1)} %shard_map.123), channel_id=1, source_target_pairs={{0,4},{1,5},{2,6},{3,7},{4,8},{5,9},{6,10},{7,11},{8,12},{9,13},{1... | collective-permute-start | bytes 442376 | tf_op jit(solution)/shard_map/ppermute | solution.py:242
  (54 other events, 719.2 us)

commit v2 on v0

v2 whole, which is shorter than its diff:
```python
import jax
import jax.numpy as jnp
from jax import lax
from jax.experimental import pallas as pl
from jax.experimental.pallas import tpu as pltpu
from jax.sharding import PartitionSpec as P

NX = 4
CAP = 2
PLAN = ("direct", "direct")
TILE = 256
PAD = 8
LOG2E = 1.4426950408889634
EMPTY = -1e30


def dot(a, b, dims):
    return lax.dot_general(a, b, (dims, ((), ())), preferred_element_type=jnp.float32)


def three_parts(line):
    parts = []
    for _ in range(3):
        piece = line.astype(jnp.bfloat16).astype(jnp.float32)
        line = line - piece
        parts.append(piece)
    return parts


def span_kernel(axis, q_ref, k_ref, v_ref, out_ref, logs_ref):
    blocks, lines = out_ref.shape[0], out_ref.shape[2]
    spans, per, width = q_ref.shape[2:]
    scale = width ** (-0.5)
    group = max(1, min(TILE // per, blocks))
    logs_ref[...] = jnp.zeros_like(logs_ref)
    for s in range(spans):
        for b in range(0, blocks, group):
            if axis == 0:
                q = q_ref[0, b : b + group, s]
            else:
                q = q_ref[b : b + group, 0, s]
            scores = dot(k_ref[s], q.reshape(group * per, width), ((1,), (1,)))
            top = jnp.max(scores, axis=0, keepdims=True)
            weights = jnp.exp2((scores - top) * (scale * LOG2E))
            total = jnp.sum(weights, axis=0, keepdims=True)
            mixed = dot(v_ref[s], weights.astype(jnp.bfloat16), ((1,), (0,)))
            mixed = (mixed * (1.0 / total)).T.astype(jnp.bfloat16)
            out_ref[b : b + group, 0, s * per : (s + 1) * per, :] = mixed.reshape(
                group, per, width
            )
            parts = three_parts(top * scale + jnp.log(total))
            for u in range(group):
                for p in range(3):
                    lane = (p % 2) * spans * per + s * per
                    logs_ref[b + u, p // 2 : p // 2 + 1, lane : lane + per] = parts[p][
                        :, u * per : (u + 1) * per
                    ]
    out_ref[:, 0, spans * per :, :] = logs_ref[...].astype(jnp.bfloat16)


def span_states(q, keys, values, axis):
    peers, blocks = (q.shape[0], q.shape[1]) if axis == 0 else (q.shape[1], q.shape[0])
    spans, per, width = q.shape[2:]
    lines = spans * per + PAD
    if axis == 0:
        q_spec = pl.BlockSpec((1, blocks, spans, per, width), lambda i: (i, 0, 0, 0, 0))
    else:
        q_spec = pl.BlockSpec((blocks, 1, spans, per, width), lambda i: (0, i, 0, 0, 0))
    return pl.pallas_call(
        lambda *refs: span_kernel(axis, *refs),
        grid=(peers,),
        in_specs=[
            q_spec,
            pl.BlockSpec(keys.shape, lambda i: (0, 0, 0)),
            pl.BlockSpec(values.shape, lambda i: (0, 0, 0)),
        ],
        out_specs=pl.BlockSpec((blocks, 1, lines, width), lambda i: (0, i, 0, 0)),
        out_shape=jax.ShapeDtypeStruct((blocks, peers, lines, width), jnp.bfloat16),
        scratch_shapes=[pltpu.VMEM((blocks, PAD, width), jnp.float32)],
        compiler_params=pltpu.CompilerParams(vmem_limit_bytes=48 * 1024 * 1024),
        cost_estimate=pl.CostEstimate(
            flops=4 * q.size * keys.shape[1],
            bytes_accessed=4 * q.size + 4 * keys.size,
            transcendentals=q.size // width * keys.shape[1],
        ),
    )(q, keys, values)


def named_by(table, spans):
    requests = table.shape[-2]
    match = jnp.any(table[None] == spans.reshape((-1,) + (1,) * table.ndim), axis=-1)
    who = jnp.arange(requests, dtype=jnp.int32)
    first = jnp.min(jnp.where(match, who, requests), axis=-1)
    last = jnp.max(jnp.where(match, who, -1), axis=-1)
    return jnp.stack(
        [jnp.where(last >= 0, first, -1), jnp.where(last > first, last, -1)], axis=-1
    )


def own_states(grouped, cache_keys, cache_values, fresh_keys, fresh_values, live_len):
    scaling = grouped.shape[-1] ** (-0.5)
    step_count = grouped.shape[1]
    cache_slots = cache_keys.shape[1]
    cache_scores = (
        jnp.einsum("rsngd,rtnd->rsngt", grouped, cache_keys, preferred_element_type=jnp.float32)
        * scaling
    )
    fresh_scores = (
        jnp.einsum("rsngd,rtnd->rsngt", grouped, fresh_keys, preferred_element_type=jnp.float32)
        * scaling
    )
    cache_live = jnp.arange(cache_slots, dtype=jnp.int32)[None, :] < live_len[:, None]
    cache_scores = jnp.where(cache_live[:, None, None, None, :], cache_scores, EMPTY)
    causal = (
        jnp.arange(step_count, dtype=jnp.int32)[None, :]
        <= jnp.arange(step_count, dtype=jnp.int32)[:, None]
    )
    fresh_scores = jnp.where(causal[None, :, None, None, :], fresh_scores, EMPTY)
    highest = jnp.maximum(jnp.max(cache_scores, axis=-1), jnp.max(fresh_scores, axis=-1))
    cache_w = jnp.exp(cache_scores - highest[..., None])
    fresh_w = jnp.exp(fresh_scores - highest[..., None])
    summed = jnp.sum(cache_w, axis=-1) + jnp.sum(fresh_w, axis=-1)
    product = jnp.einsum(
        "rsngt,rtnd->rsngd",
        cache_w.astype(jnp.bfloat16),
        cache_values,
        preferred_element_type=jnp.float32,
    )
    product = product + jnp.einsum(
        "rsngt,rtnd->rsngd",
        fresh_w.astype(jnp.bfloat16),
        fresh_values,
        preferred_element_type=jnp.float32,
    )
    return (product / summed[..., None], highest + jnp.log(summed))


def local(
    queries,
    new_keys,
    new_values,
    suffix_keys,
    suffix_values,
    suffix_len,
    block_table,
    prefix_keys,
    prefix_values,
):
    requests, steps, heads, width = queries.shape
    span_count, span_len = prefix_keys.shape[:2]
    depth = block_table.shape[1]
    owners = lax.axis_size("req")
    nz = owners // NX
    row = lax.axis_index("req") // NX
    z_groups = [[z * NX + x for z in range(nz)] for x in range(NX)]
    x_groups = [[z * NX + x for x in range(NX)] for z in range(nz)]
    keys = prefix_keys.reshape(span_count, span_len, width)
    values = prefix_values.reshape(span_count, span_len, width).transpose(0, 2, 1)
    per = steps // len(PLAN)
    rows = per * heads
    lines = span_count * CAP * rows

    chosen = named_by(block_table, jnp.arange(owners * span_count, dtype=jnp.int32))
    own_pick = jnp.maximum(chosen, 0).reshape(-1)
    second = chosen[:, 0][block_table] != jnp.arange(requests, dtype=jnp.int32)[:, None]
    slot_ids = block_table * CAP + second.astype(jnp.int32)

    arrived = []
    for c, how in enumerate(PLAN):
        part = queries[:, c * per : (c + 1) * per].reshape(requests, rows, width)
        if how == "direct":
            outgoing = part[own_pick].reshape(owners, lines, width)
            incoming = lax.all_to_all(
                outgoing, "req", split_axis=0, concat_axis=0, tiled=True
            )
            incoming = incoming.reshape(nz, NX, span_count, CAP * rows, width)
            arrived.append((incoming, 1))
            continue
        line = block_table.astype(jnp.bfloat16).reshape(1, -1)
        line = jnp.pad(line, ((0, rows - 1), (0, width - requests * depth)))
        pool = jnp.concatenate([part.reshape(-1, width), line], axis=0)
        pool = lax.all_gather(pool, "req", axis_index_groups=z_groups, tiled=True)
        pool = pool.reshape(nz, requests + 1, rows, width)
        table = pool[:, requests, 0, : requests * depth].astype(jnp.int32)
        here = row * NX * span_count + jnp.arange(NX * span_count, dtype=jnp.int32)
        picked = jnp.maximum(named_by(table.reshape(nz, requests, depth), here), 0)
        block_at = jnp.arange(nz, dtype=jnp.int32) * (requests + 1)
        picked = picked + block_at[None, :, None]
        picked = picked.reshape(NX, span_count, nz, CAP).transpose(0, 2, 1, 3).reshape(-1)
        outgoing = pool.reshape(nz * (requests + 1), rows, width)[picked]
        outgoing = outgoing.reshape(NX, nz * lines, width)
        incoming = lax.all_to_all(
            outgoing, "req", split_axis=0, concat_axis=0, tiled=True, axis_index_groups=x_groups
        )
        arrived.append((incoming.reshape(NX, nz, span_count, CAP * rows, width), 0))

    kv_local = new_keys.shape[2]
    grouped = queries.reshape(requests, steps, kv_local, heads // kv_local, width)
    own_part, own_log = own_states(
        grouped, suffix_keys, suffix_values, new_keys, new_values, suffix_len
    )
    own_part = own_part.reshape(requests, steps, heads, width)
    own_log = own_log.reshape(requests, steps, heads)

    kv_count = lax.axis_size("kv")
    results = []
    for c, (incoming, axis) in enumerate(arrived):
        states = span_states(incoming, keys, values, axis)
        states = states.reshape(owners, lines + PAD, width)
        if c + 1 < len(arrived) and PLAN[c + 1] == "direct":
            states, following = lax.optimization_barrier((states, arrived[c + 1][0]))
            arrived[c + 1] = (following, arrived[c + 1][1])
        states = lax.all_to_all(states, "req", split_axis=0, concat_axis=0, tiled=True)
        logs = states[:, lines : lines + 2].astype(jnp.float32)
        logs = logs[:, 0, :lines] + logs[:, 0, lines : 2 * lines] + logs[:, 1, :lines]
        logs = logs.reshape(owners * span_count * CAP, rows)[slot_ids]
        parts = states[:, :lines].reshape(owners * span_count * CAP, rows, width)[slot_ids]
        own_l = own_log[:, c * per : (c + 1) * per].reshape(requests, 1, rows)
        own_p = own_part[:, c * per : (c + 1) * per].reshape(requests, rows, width)
        top = jnp.maximum(jnp.max(logs, axis=1, keepdims=True), own_l)
        factors = jnp.exp(logs - top)
        own_f = jnp.exp(own_l - top)[:, 0]
        total = jnp.sum(factors, axis=1) + own_f
        merged = jnp.sum(factors[..., None] * parts.astype(jnp.float32), axis=1)
        merged = (merged + own_f[..., None] * own_p) / total[..., None]
        merged = merged.astype(jnp.bfloat16)
        merged = merged.reshape(requests // kv_count, kv_count, per, heads * width)
        results.append(lax.all_to_all(merged, "kv", split_axis=1, concat_axis=3, tiled=True))
    return jnp.concatenate(results, axis=2)


def solution(mesh):
    placed = (
        P("req", None, "kv", None),
        P("req", None, "kv", None),
        P("req", None, "kv", None),
        P("req", None, "kv", None),
        P("req", None, "kv", None),
        P("req"),
        P("req", None),
        P("req", None, "kv", None),
        P("req", None, "kv", None),
    )
    return jax.shard_map(
        local, mesh=mesh, in_specs=placed, out_specs=P("req", "kv", None, None), check_vma=False
    )
```

time: 431 us -> 297 us (0.69)
  waiting for transfers between devices: 277 us -> 178 us
  matrix products: 47.5 us -> 4.05 us
  Pallas kernels: 0 us -> 25.5 us
  starting transfers between devices: 36.5 us -> 61.6 us
  blocking collectives: 18.2 us -> 0 us
  other arithmetic: 18.9 us -> 5.46 us
  local copies, waits for them, and re-layouts: 31.5 us -> 21.3 us
    all_to_all x2 -> x4, waiting for transfers between devices: 182 us -> 94 us  [the longest x2 84.8 us: local(): lax.all_to_all(states, 'req', split_axis=0, concat_axis=0, tiled=True)]
    dot_general x32 -> x0, matrix products: 42.7 us -> none  [the longest x16 22.9 us: span_states(): jnp.einsum('bsngd,tnd->bsngt', queries_in, key_block, preferred_element_t...]
    pallas_call x0 -> x2, Pallas kernels: none -> 25.5 us  [span_states(): pl.pallas_call(lambda *refs: span_kernel(axis, *refs), grid=(peers,), in_...]
    all_to_all x1 -> x0, blocking collectives: 18.2 us -> none  [local(): return lax.all_to_all(merged, 'kv', split_axis=1, concat_axis=3, tiled=True)]
    all_to_all x2 -> x4, starting transfers between devices: 17.5 us -> 33.4 us  [the longest x2 18.7 us: local(): lax.all_to_all(states, 'req', split_axis=0, concat_axis=0, tiled=True)]
    scatter x1 -> x0, local copies, waits for them, and re-layouts: 13.7 us -> none  [local(): outgoing.at[slot_ids].set(jnp.repeat(grouped, depth_count, axis=0))]
    all_to_all x1 -> x2, waiting for transfers between devices: 94.9 us -> 83.8 us  [local(): lax.all_to_all(outgoing, 'req', split_axis=0, concat_axis=0, tiled=True)]
    reduce_sum x19 -> x3, other arithmetic: 10.7 us -> 0.8 us  [the longest x2 0.67 us: local(): merged = jnp.sum(factors[..., None] * parts.astype(jnp.float32), axis=1)]
  transfers between devices with their start and end apart: 3 -> 6, of which waited for: 3 -> 6; matrix products, arithmetic and copies ran while one was open for 3% -> 6% of each run, Pallas kernels for 0% -> 9%
where the time goes in v2:
time: 297 us; the launch traced here: 296 us
  waiting for transfers between devices  178 us (60%)
  starting transfers between devices  61.6 us (21%)
  Pallas kernels  25.5 us (9%)
  local copies, waits for them, and re-layouts  21.3 us (7%)
  other arithmetic  5.46 us (2%)
  matrix products  4.05 us (1%)
    all_to_all x2, waiting for transfers between devices, local(): lax.all_to_all(states, 'req', split_axis=0, concat_axis=0, tiled=True)  84.8 us
    all_to_all x2, waiting for transfers between devices, local(): lax.all_to_all(outgoing, 'req', split_axis=0, concat_axis=0, tiled=True)  83.8 us
    all_to_all x2, starting transfers between devices, local(): lax.all_to_all(outgoing, 'req', split_axis=0, concat_axis=0, tiled=True)  28.1 us
    pallas_call x2, Pallas kernels, span_states(): pl.pallas_call(lambda *refs: span_kernel(axis, *refs), grid=(peers,), in_...  25.5 us
    all_to_all x2, starting transfers between devices, local(): lax.all_to_all(states, 'req', split_axis=0, concat_axis=0, tiled=True)  18.7 us
    all_to_all x2, starting transfers between devices, local(): lax.all_to_all(merged, 'kv', split_axis=1, concat_axis=3, tiled=True)  14.7 us
    all_to_all x2, waiting for transfers between devices, local(): lax.all_to_all(merged, 'kv', split_axis=1, concat_axis=3, tiled=True)  9.18 us
  transfers between devices with their start and end apart: 6, of which 6 were waited for; matrix products, arithmetic and copies ran while one was open for 6% of the time, Pallas kernels for 9%

profile of v2, /device:TPU:1, one launch (start us, length us, event | category | flops | bytes accessed | tf_op | source)
XLA Modules:
  0.0 296.0 jit_solution(16923293001480192842)
XLA Ops:
  0.0 0.9 fusion.25
  1.2 1.0 slice_bitcast_fusion
  2.2 1.8 gather_fusion
  4.0 19.1 %all-to-all-start = ((bf16[64,64,128]{2,1,0:T(8,128)(2,1)}), bf16[64,64,128]{2,1,0:T(8,128)(2,1)S(1)}, u32[]{:S(2)}, u32[]{:S(2)}) async-start(bf16[64,64,128]{2,1,0:T(8,128)(2,1)} %bitcast.3), calls=%async_computation | async-start | bytes 2097152 | tf_op jit(solution)/shard_map/all_to_all | solution.py:173
  23.1 1.8 gather_fusion.1
  24.9 49.7 %all-to-all-done = bf16[64,64,128]{2,1,0:T(8,128)(2,1)S(1)} async-done(((bf16[64,64,128]{2,1,0:T(8,128)(2,1)}), bf16[64,64,128]{2,1,0:T(8,128)(2,1)S(1)}, u32[]{:S(2)}, u32[]{:S(2)}) %all-to-all-start) | async-done | bytes 1048608 | tf_op jit(solution)/shard_map/all_to_all | solution.py:173
  74.6 9.0 %all-to-all-start.1 = ((bf16[64,64,128]{2,1,0:T(8,128)(2,1)}), bf16[64,64,128]{2,1,0:T(8,128)(2,1)S(1)}, u32[]{:S(2)}, u32[]{:S(2)}) async-start(bf16[64,64,128]{2,1,0:T(8,128)(2,1)} %bitcast.121), calls=%async_computation.1 | async-start | bytes 2097152 | tf_op jit(solution)/shard_map/all_to_all | solution.py:173
  83.6 2.1 copy.107
  85.6 1.0 copy-done.1
  86.7 1.0 copy-done.3
  87.7 12.7 %shard_map.91 = bf16[16,4,72,128]{3,2,1,0:T(8,128)(2,1)} custom-call(bf16[16,4,2,32,128]{4,3,2,1,0:T(8,128)(2,1)S(1)} %bitcast.115, bf16[2,1024,128]{2,1,0:T(8,128)(2,1)S(1)} %bitcast.119, bf16[2,128,1024]{2,1,0:T(8,128)(2,1)S(1)} %bitcast.117), custom_call_target="tpu_custom_call" | custom-call | flops 2147483648 | bytes 3145728 | tf_op jit(solution)/shard_map/pallas_call | solution.py:69
  100.5 34.1 %all-to-all-done.1 = bf16[64,64,128]{2,1,0:T(8,128)(2,1)S(1)} async-done(((bf16[64,64,128]{2,1,0:T(8,128)(2,1)}), bf16[64,64,128]{2,1,0:T(8,128)(2,1)S(1)}, u32[]{:S(2)}, u32[]{:S(2)}) %all-to-all-start.1) | async-done | bytes 1048608 | tf_op jit(solution)/shard_map/all_to_all | solution.py:173
  134.6 8.9 %all-to-all-start.2 = ((bf16[64,72,128]{2,1,0:T(8,128)(2,1)}), bf16[64,72,128]{2,1,0:T(8,128)(2,1)}, u32[]{:S(2)}, u32[]{:S(2)}) async-start(bf16[64,72,128]{2,1,0:T(8,128)(2,1)} %bitcast.8), calls=%async_computation.2 | async-start | bytes 2359296 | tf_op jit(solution)/shard_map/all_to_all | solution.py:213
  143.5 12.7 %shard_map.92 = bf16[16,4,72,128]{3,2,1,0:T(8,128)(2,1)} custom-call(bf16[16,4,2,32,128]{4,3,2,1,0:T(8,128)(2,1)S(1)} %bitcast.116, bf16[2,1024,128]{2,1,0:T(8,128)(2,1)S(1)} %bitcast.120, bf16[2,128,1024]{2,1,0:T(8,128)(2,1)S(1)} %bitcast.118), custom_call_target="tpu_custom_call" | custom-call | flops 2147483648 | bytes 3145728 | tf_op jit(solution)/shard_map/pallas_call | solution.py:69
  156.3 42.8 %all-to-all-done.2 = bf16[64,72,128]{2,1,0:T(8,128)(2,1)} async-done(((bf16[64,72,128]{2,1,0:T(8,128)(2,1)}), bf16[64,72,128]{2,1,0:T(8,128)(2,1)}, u32[]{:S(2)}, u32[]{:S(2)}) %all-to-all-start.2) | async-done | bytes 1179680 | tf_op jit(solution)/shard_map/all_to_all | solution.py:213
  199.0 9.7 %all-to-all-start.4 = ((bf16[64,72,128]{2,1,0:T(8,128)(2,1)}), bf16[64,72,128]{2,1,0:T(8,128)(2,1)S(1)}, u32[]{:S(2)}, u32[]{:S(2)}) async-start(bf16[64,72,128]{2,1,0:T(8,128)(2,1)} %bitcast.41), calls=%async_computation.4 | async-start | bytes 2359296 | tf_op jit(solution)/shard_map/all_to_all | solution.py:213
  209.1 1.2 gather_fusion.2
  210.8 1.3 fusion.37
  212.1 0.8 fusion.36
  214.3 1.7 fusion.7
  216.0 0.8 reshape.331
  216.8 0.8 reshape.335
  217.7 0.9 slice_convert_fusion.1
  218.9 1.3 slice.83
  220.2 1.5 gather_fusion.4
  222.3 42.0 %all-to-all-done.4 = bf16[64,72,128]{2,1,0:T(8,128)(2,1)S(1)} async-done(((bf16[64,72,128]{2,1,0:T(8,128)(2,1)}), bf16[64,72,128]{2,1,0:T(8,128)(2,1)S(1)}, u32[]{:S(2)}, u32[]{:S(2)}) %all-to-all-start.4) | async-done | bytes 1179680 | tf_op jit(solution)/shard_map/all_to_all | solution.py:213
  268.9 0.8 copy.119
  269.6 10.6 %all-to-all-start.5 = ((bf16[4,8,2,1024]{3,2,0,1:T(2,128)(2,1)}), bf16[4,8,2,1024]{3,2,0,1:T(2,128)(2,1)S(1)}, u32[]{:S(2)}, u32[]{:S(2)}) async-start(bf16[4,8,2,1024]{3,2,0,1:T(2,128)(2,1)} %copy.119), calls=%async_computation.5 | async-start | bytes 262144 | tf_op jit(solution)/shard_map/all_to_all | solution.py:228
  281.5 4.0 %all-to-all-done.5 = bf16[4,8,2,1024]{3,2,0,1:T(2,128)(2,1)S(1)} async-done(((bf16[4,8,2,1024]{3,2,0,1:T(2,128)(2,1)}), bf16[4,8,2,1024]{3,2,0,1:T(2,128)(2,1)S(1)}, u32[]{:S(2)}, u32[]{:S(2)}) %all-to-all-start.5) | async-done | bytes 131104 | tf_op jit(solution)/shard_map/all_to_all | solution.py:228
  285.5 4.1 %all-to-all-start.3 = ((bf16[4,8,2,1024]{3,2,0,1:T(2,128)(2,1)}), bf16[4,8,2,1024]{3,2,0,1:T(2,128)(2,1)S(1)}, u32[]{:S(2)}, u32[]{:S(2)}) async-start(bf16[4,8,2,1024]{3,2,0,1:T(2,128)(2,1)} %copy.114), calls=%async_computation.3 | async-start | bytes 262144 | tf_op jit(solution)/shard_map/all_to_all | solution.py:228
  289.8 5.2 %all-to-all-done.3 = bf16[4,8,2,1024]{3,2,0,1:T(2,128)(2,1)S(1)} async-done(((bf16[4,8,2,1024]{3,2,0,1:T(2,128)(2,1)}), bf16[4,8,2,1024]{3,2,0,1:T(2,128)(2,1)S(1)}, u32[]{:S(2)}, u32[]{:S(2)}) %all-to-all-start.3) | async-done | bytes 131104 | tf_op jit(solution)/shard_map/all_to_all | solution.py:228
  295.1 1.0 maximum_bitcast_fusion
  (87 shorter events, 9.2 us)
Async XLA Ops:
  0.0 212.1 %copy-start = (bf16[32,128,1,128]{3,1,2,0:T(8,128)(2,1)S(1)}, bf16[32,128,1,128]{3,1,2,0:T(8,128)(2,1)}, u32[]{:S(2)}) copy-start(bf16[32,128,1,128]{3,1,2,0:T(8,128)(2,1)} %param.12) | copy-start | bytes 3145732
  4.0 70.6 %all-to-all-start = ((bf16[64,64,128]{2,1,0:T(8,128)(2,1)}), bf16[64,64,128]{2,1,0:T(8,128)(2,1)S(1)}, u32[]{:S(2)}, u32[]{:S(2)}) async-start(bf16[64,64,128]{2,1,0:T(8,128)(2,1)} %bitcast.3), calls=%async_computation | async-start | bytes 2097152 | tf_op jit(solution)/shard_map/all_to_all | solution.py:173
  74.6 60.0 %all-to-all-start.1 = ((bf16[64,64,128]{2,1,0:T(8,128)(2,1)}), bf16[64,64,128]{2,1,0:T(8,128)(2,1)S(1)}, u32[]{:S(2)}, u32[]{:S(2)}) async-start(bf16[64,64,128]{2,1,0:T(8,128)(2,1)} %bitcast.121), calls=%async_computation.1 | async-start | bytes 2097152 | tf_op jit(solution)/shard_map/all_to_all | solution.py:173
  85.6 1.0 copy-start.1
  86.7 1.0 copy-start.3
  134.6 9.0 %copy-start.2 = (bf16[2,1024,1,128]{1,3,0,2:T(8,128)(2,1)S(1)}, bf16[2,1024,1,128]{1,3,0,2:T(8,128)(2,1)}, u32[]{:S(2)}) copy-start(bf16[2,1024,1,128]{1,3,0,2:T(8,128)(2,1)} %copy.107) | copy-start | bytes 1572868
  134.6 9.0 %copy-start.4 = (bf16[2,1024,1,128]{3,1,2,0:T(8,128)(2,1)S(1)}, bf16[2,1024,1,128]{3,1,2,0:T(8,128)(2,1)}, u32[]{:S(2)}) copy-start(bf16[2,1024,1,128]{3,1,2,0:T(8,128)(2,1)} %param.16) | copy-start | bytes 1572868
  134.6 64.4 %all-to-all-start.2 = ((bf16[64,72,128]{2,1,0:T(8,128)(2,1)}), bf16[64,72,128]{2,1,0:T(8,128)(2,1)}, u32[]{:S(2)}, u32[]{:S(2)}) async-start(bf16[64,72,128]{2,1,0:T(8,128)(2,1)} %bitcast.8), calls=%async_computation.2 | async-start | bytes 2359296 | tf_op jit(solution)/shard_map/all_to_all | solution.py:213
  199.0 9.8 %copy-start.10 = (s32[32,4]{0,1:T(4,128)S(1)}, s32[32,4]{0,1:T(4,128)}, u32[]{:S(2)}) copy-start(s32[32,4]{0,1:T(4,128)} %param.15) | copy-start | bytes 1540
  199.0 65.3 %all-to-all-start.4 = ((bf16[64,72,128]{2,1,0:T(8,128)(2,1)}), bf16[64,72,128]{2,1,0:T(8,128)(2,1)S(1)}, u32[]{:S(2)}, u32[]{:S(2)}) async-start(bf16[64,72,128]{2,1,0:T(8,128)(2,1)} %bitcast.41), calls=%async_computation.4 | async-start | bytes 2359296 | tf_op jit(solution)/shard_map/all_to_all | solution.py:213
  209.0 1.7 copy-start.11
  209.0 1.8 copy-start.8
  209.0 1.7 copy-start.12
  212.9 1.1 copy-start.9
  266.1 1.0 copy-start.5
  267.7 1.0 copy-start.7
  268.6 11.9 %copy-start.6 = (f32[4,8,2,1024]{3,2,1,0:T(2,128)S(1)}, f32[4,8,2,1024]{3,2,1,0:T(2,128)}, u32[]{:S(2)}) copy-start(f32[4,8,2,1024]{3,2,1,0:T(2,128)} %reshape.331) | copy-start | bytes 786436
  269.6 15.9 %all-to-all-start.5 = ((bf16[4,8,2,1024]{3,2,0,1:T(2,128)(2,1)}), bf16[4,8,2,1024]{3,2,0,1:T(2,128)(2,1)S(1)}, u32[]{:S(2)}, u32[]{:S(2)}) async-start(bf16[4,8,2,1024]{3,2,0,1:T(2,128)(2,1)} %copy.119), calls=%async_computation.5 | async-start | bytes 262144 | tf_op jit(solution)/shard_map/all_to_all | solution.py:228
  285.5 9.4 %all-to-all-start.3 = ((bf16[4,8,2,1024]{3,2,0,1:T(2,128)(2,1)}), bf16[4,8,2,1024]{3,2,0,1:T(2,128)(2,1)S(1)}, u32[]{:S(2)}, u32[]{:S(2)}) async-start(bf16[4,8,2,1024]{3,2,0,1:T(2,128)(2,1)} %copy.114), calls=%async_computation.3 | async-start | bytes 262144 | tf_op jit(solution)/shard_map/all_to_all | solution.py:228

commit v3 on v0

v3 whole, which is shorter than its diff:
```python
import jax
import jax.numpy as jnp
from jax import lax
from jax.experimental import pallas as pl
from jax.experimental.pallas import tpu as pltpu
from jax.sharding import PartitionSpec as P

NX = 4
CAP = 2
ROOM = 11
CHUNKS = 2
TILE = 256
PAD = 8
LOG2E = 1.4426950408889634
EMPTY = -1e30


def dot(a, b, dims):
    return lax.dot_general(a, b, (dims, ((), ())), preferred_element_type=jnp.float32)


def row_kernel(tiles_ref, span_ref, block_ref, line_ref, q_ref, kv_ref, out_ref, logs_ref):
    blocks, slots, width = logs_ref.shape
    per = out_ref.shape[1] // slots
    length = kv_ref.shape[1] // 2
    items = TILE // per
    scale = width ** (-0.5)
    out_ref[...] = jnp.zeros_like(out_ref)
    logs_ref[...] = jnp.zeros_like(logs_ref)

    def one_tile(t, carry):
        span = span_ref[t]
        spots = []
        for u in range(items):
            line = pl.multiple_of(line_ref[t * items + u] * per, per)
            spots.append((block_ref[t * items + u], line, line_ref[t * items + u]))
        q = jnp.concatenate([q_ref[b, pl.ds(line, per), :] for b, line, _ in spots], axis=0)
        scores = dot(kv_ref[span, :length, :], q, ((1,), (1,)))
        top = jnp.max(scores, axis=0, keepdims=True)
        weights = jnp.exp2((scores - top) * (scale * LOG2E))
        total = jnp.sum(weights, axis=0, keepdims=True)
        mixed = dot(kv_ref[span, length : 2 * length, :], weights.astype(jnp.bfloat16), ((0,), (0,)))
        mixed = (mixed * (1.0 / total)).T.astype(jnp.bfloat16)
        logs = top * scale + jnp.log(total)
        for u, (b, line, slot) in enumerate(spots):
            out_ref[b, pl.ds(line, per), :] = mixed[u * per : (u + 1) * per, :]
            logs_ref[b, pl.ds(slot, 1), 0:per] = logs[:, u * per : (u + 1) * per]
        return carry

    lax.fori_loop(0, tiles_ref[0], one_tile, 0)


def row_states(plan, q, kv, slots, per):
    blocks, _, width = q.shape
    lines = slots * per
    return pl.pallas_call(
        row_kernel,
        grid_spec=pltpu.PrefetchScalarGridSpec(
            num_scalar_prefetch=4,
            grid=(1,),
            in_specs=[
                pl.BlockSpec((blocks, lines, width), lambda i, *_: (0, 0, 0)),
                pl.BlockSpec(kv.shape, lambda i, *_: (0, 0, 0)),
            ],
            out_specs=[
                pl.BlockSpec((blocks, lines, width), lambda i, *_: (0, 0, 0)),
                pl.BlockSpec((blocks, slots, width), lambda i, *_: (0, 0, 0)),
            ],
        ),
        out_shape=[
            jax.ShapeDtypeStruct((blocks, lines, width), jnp.bfloat16),
            jax.ShapeDtypeStruct((blocks, slots, width), jnp.float32),
        ],
        compiler_params=pltpu.CompilerParams(vmem_limit_bytes=48 * 1024 * 1024),
        cost_estimate=pl.CostEstimate(
            flops=2 * q.size * kv.shape[1],
            bytes_accessed=6 * q.size + 2 * kv.size,
            transcendentals=q.size // width * kv.shape[1] // 2,
        ),
    )(*plan, q, kv)


def tile_plan(spans, count, per):
    blocks, slots = spans.shape
    items = TILE // per
    most = blocks * CAP
    rounds = -(-most // items)
    flat = spans.reshape(-1)
    names = jnp.arange(count, dtype=jnp.int32)
    equal = (flat[None, :] == names[:, None]).astype(jnp.int32)
    place = jnp.cumsum(equal, axis=1) - 1
    spot = jnp.arange(rounds * items, dtype=jnp.int32)
    hit = (place[:, None, :] == spot[None, :, None]) & (equal[:, None, :] > 0)
    lists = jnp.sum(jnp.where(hit, jnp.arange(flat.shape[0], dtype=jnp.int32), 0), axis=2)
    amount = jnp.sum(equal, axis=1)
    lists = jnp.where(spot[None, :] < amount[:, None], lists, lists[:, :1])
    tiles = jnp.minimum((amount + items - 1) // items, rounds)
    ends = jnp.cumsum(tiles)
    each = jnp.arange(count * rounds, dtype=jnp.int32)
    span = jnp.minimum(jnp.sum((ends[None, :] <= each[:, None]).astype(jnp.int32), axis=1), count - 1)
    turn = jnp.clip(each - (ends - tiles)[span], 0, rounds - 1)
    picked = lists.reshape(count * rounds, items)[span * rounds + turn].reshape(-1)
    return ends[-1:], span, picked // slots, picked % slots


def own_states(grouped, cache_keys, cache_values, fresh_keys, fresh_values, live_len):
    scaling = grouped.shape[-1] ** (-0.5)
    step_count = grouped.shape[1]
    cache_slots = cache_keys.shape[1]
    cache_scores = (
        jnp.einsum("rsngd,rtnd->rsngt", grouped, cache_keys, preferred_element_type=jnp.float32)
        * scaling
    )
    fresh_scores = (
        jnp.einsum("rsngd,rtnd->rsngt", grouped, fresh_keys, preferred_element_type=jnp.float32)
        * scaling
    )
    cache_live = jnp.arange(cache_slots, dtype=jnp.int32)[None, :] < live_len[:, None]
    cache_scores = jnp.where(cache_live[:, None, None, None, :], cache_scores, EMPTY)
    causal = (
        jnp.arange(step_count, dtype=jnp.int32)[None, :]
        <= jnp.arange(step_count, dtype=jnp.int32)[:, None]
    )
    fresh_scores = jnp.where(causal[None, :, None, None, :], fresh_scores, EMPTY)
    highest = jnp.maximum(jnp.max(cache_scores, axis=-1), jnp.max(fresh_scores, axis=-1))
    cache_w = jnp.exp(cache_scores - highest[..., None])
    fresh_w = jnp.exp(fresh_scores - highest[..., None])
    summed = jnp.sum(cache_w, axis=-1) + jnp.sum(fresh_w, axis=-1)
    product = jnp.einsum(
        "rsngt,rtnd->rsngd",
        cache_w.astype(jnp.bfloat16),
        cache_values,
        preferred_element_type=jnp.float32,
    )
    product = product + jnp.einsum(
        "rsngt,rtnd->rsngd",
        fresh_w.astype(jnp.bfloat16),
        fresh_values,
        preferred_element_type=jnp.float32,
    )
    return (product / summed[..., None], highest + jnp.log(summed))


def merge_own(parts, logs, own_part, own_log, c, per):
    requests, _, heads, width = own_part.shape
    rows = per * heads
    own_l = own_log[:, c * per : (c + 1) * per].reshape(requests, 1, rows)
    own_p = own_part[:, c * per : (c + 1) * per].reshape(requests, rows, width)
    top = jnp.maximum(jnp.max(logs, axis=1, keepdims=True), own_l)
    factors = jnp.exp(logs - top)
    own_f = jnp.exp(own_l - top)[:, 0]
    total = jnp.sum(factors, axis=1) + own_f
    merged = jnp.sum(factors[..., None] * parts.astype(jnp.float32), axis=1)
    merged = (merged + own_f[..., None] * own_p) / total[..., None]
    return merged.astype(jnp.bfloat16).reshape(requests, per, heads, width)


def local(
    queries,
    new_keys,
    new_values,
    suffix_keys,
    suffix_values,
    suffix_len,
    block_table,
    prefix_keys,
    prefix_values,
):
    requests, steps, heads, width = queries.shape
    span_count, span_len = prefix_keys.shape[:2]
    depth = block_table.shape[1]
    owners = lax.axis_size("req")
    nz = owners // NX
    in_row = NX * span_count
    column = lax.axis_index("req") % NX
    z_groups = [[z * NX + x for z in range(nz)] for x in range(NX)]
    keys = prefix_keys.reshape(span_count, span_len, width)
    values = prefix_values.reshape(span_count, span_len, width)
    per = steps // CHUNKS
    rows = per * heads

    named = block_table.reshape(-1)
    number = jnp.arange(named.shape[0], dtype=jnp.int32)
    goal = named // in_row
    before = (goal[:, None] == goal[None, :]) & (number[None, :] < number[:, None])
    rank = jnp.sum(before.astype(jnp.int32), axis=1)
    over = jnp.max((rank >= ROOM).astype(jnp.bfloat16))
    local_span = (named - column * span_count) % in_row

    def seats(low, room):
        inside = (rank >= low) & (rank < low + room)
        seat = jnp.where(inside, goal * room + rank - low, -1)
        taken = seat[None, :] == jnp.arange(nz * room, dtype=jnp.int32)[:, None]
        sender = jnp.sum(jnp.where(taken, number // depth, 0), axis=1)
        span_at = jnp.sum(jnp.where(taken, local_span + 1, 0), axis=1) - 1
        span_at = span_at.reshape(nz, room).astype(jnp.bfloat16)
        return sender, span_at, jnp.maximum(seat, 0).reshape(requests, depth)

    def along_z(array):
        return lax.all_to_all(
            array, "req", split_axis=0, concat_axis=0, tiled=True, axis_index_groups=z_groups
        )

    def send(part, sender, span_at):
        lines = sender.shape[0] // nz * part.shape[1]
        outgoing = part[sender].reshape(nz, lines, width)
        if span_at is not None:
            extra = ((0, 0), (0, PAD - 1), (0, width - span_at.shape[1]))
            outgoing = jnp.concatenate([outgoing, jnp.pad(span_at[:, None, :], extra)], axis=1)
        return along_z(outgoing)

    def packed(states, logs, note):
        lines = states.shape[1]
        logs = logs[:, :, : lines // logs.shape[1]].reshape(nz, lines)
        high = lax.reduce_precision(logs, 8, 7)
        middle = lax.reduce_precision(logs - high, 8, 7)
        logs = jnp.concatenate([high, middle, logs - high - middle], axis=1).astype(jnp.bfloat16)
        note = jnp.broadcast_to(note, (nz, PAD * width - 3 * lines))
        logs = jnp.concatenate([logs, note], axis=1).reshape(nz, PAD, width)
        return jnp.concatenate([states, logs], axis=1)

    def opened(states, slot_ids, rows):
        lines = states.shape[1] - PAD
        logs = states[:, lines:].reshape(nz, PAD * width).astype(jnp.float32)
        note = jnp.max(logs[:, -1])
        logs = logs[:, :lines] + logs[:, lines : 2 * lines] + logs[:, 2 * lines : 3 * lines]
        logs = logs.reshape(-1, rows)[slot_ids]
        parts = states[:, :lines].reshape(-1, rows, width)[slot_ids]
        return parts, logs, note

    sender, span_at, slot_ids = seats(0, ROOM)
    arrived = []
    for c in range(CHUNKS):
        part = queries[:, c * per : (c + 1) * per].reshape(requests, rows, width)
        arrived.append(send(part, sender, span_at if c == 0 else None))
    spans_named = arrived[0][:, ROOM * rows, :ROOM].astype(jnp.int32)
    plan = tile_plan(spans_named, in_row, rows)

    def along_x(array, by):
        pairs = [(z * NX + x, z * NX + (x + by) % NX) for z in range(nz) for x in range(NX)]
        return lax.ppermute(array, "req", pairs)

    note = jnp.broadcast_to(over, (span_count, 2 * PAD, width))
    mine = jnp.concatenate([keys, values, note], axis=1)
    left = along_x(mine, 1)
    right = along_x(mine, -1)
    far_keys = along_x(left[:, :span_len], 1)
    far_rest = along_x(right[:, span_len:], -1)
    lacking = jnp.maximum(over, jnp.maximum(left[0, -1, 0], right[0, -1, 0]))
    lacking = jnp.maximum(lacking, far_rest[0, -1, 0])
    both = 2 * span_len
    far = jnp.concatenate([far_keys, far_rest[:, :span_len]], axis=1)
    spans = jnp.concatenate([mine[:, :both], right[:, :both], far, left[:, :both]], axis=0)

    kv_local = new_keys.shape[2]
    grouped = queries.reshape(requests, steps, kv_local, heads // kv_local, width)
    own_part, own_log = own_states(
        grouped, suffix_keys, suffix_values, new_keys, new_values, suffix_len
    )
    own_part = own_part.reshape(requests, steps, heads, width)
    own_log = own_log.reshape(requests, steps, heads)

    results = []
    held = []
    for c in range(CHUNKS):
        states, logs = row_states(plan, arrived[c], spans, ROOM, rows)
        states = packed(states, logs, lacking)
        if c + 1 < CHUNKS:
            states, arrived[c + 1] = lax.optimization_barrier((states, arrived[c + 1]))
        states = along_z(states)
        if c > 0:
            states, results[-1] = lax.optimization_barrier((states, results[-1]))
        parts, logs, note = opened(states, slot_ids, rows)
        held.append((parts, logs))
        results.append(merge_own(parts, logs, own_part, own_log, c, per))

    def one_more_round(merged):
        room = in_row * CAP - ROOM
        all_rows = steps * heads
        sender, span_at, more_ids = seats(ROOM, room)
        incoming = send(queries.reshape(requests, all_rows, width), sender, span_at)
        named_more = incoming[:, room * all_rows, :room].astype(jnp.int32)
        plan = tile_plan(named_more, in_row, all_rows)
        states, logs = row_states(plan, incoming, spans, room, all_rows)
        states = along_z(packed(states, logs, lacking))
        more, more_logs, _ = opened(states, more_ids, all_rows)
        late = (rank >= ROOM).reshape(requests, depth, 1)
        results = []
        for c, (parts, logs) in enumerate(held):
            cut = slice(c * rows, (c + 1) * rows)
            parts = jnp.where(late[..., None], more[:, :, cut], parts)
            logs = jnp.where(late, more_logs[:, :, cut], logs)
            results.append(merge_own(parts, logs, own_part, own_log, c, per))
        return jnp.concatenate(results, axis=1)

    merged = jnp.concatenate(results, axis=1)
    merged = lax.cond(note > 0.0, one_more_round, lambda m: m, merged)
    kv_count = lax.axis_size("kv")
    merged = merged.reshape(requests // kv_count, kv_count, steps, heads * width)
    return lax.all_to_all(merged, "kv", split_axis=1, concat_axis=3, tiled=True)


def solution(mesh):
    placed = (
        P("req", None, "kv", None),
        P("req", None, "kv", None),
        P("req", None, "kv", None),
        P("req", None, "kv", None),
        P("req", None, "kv", None),
        P("req"),
        P("req", None),
        P("req", None, "kv", None),
        P("req", None, "kv", None),
    )
    return jax.shard_map(
        local, mesh=mesh, in_specs=placed, out_specs=P("req", "kv", None, None), check_vma=False
    )
```

time: 431 us -> 235 us (0.55)
  waiting for transfers between devices: 277 us -> 71.5 us
  matrix products: 47.5 us -> 7.2 us
  starting transfers between devices: 36.5 us -> 67.6 us
  Pallas kernels: 0 us -> 22.7 us
  local copies, waits for them, and re-layouts: 31.5 us -> 23.9 us
    all_to_all x3 -> x4, waiting for transfers between devices: 277 us -> 49.6 us  [along_z(): lax.all_to_all(array, 'req', split_axis=0, concat_axis=0, tiled=True, axi...]
    dot_general x32 -> x0, matrix products: 42.7 us -> none  [the longest x16 22.9 us: span_states(): jnp.einsum('bsngd,tnd->bsngt', queries_in, key_block, preferred_element_t...]
    pallas_call x0 -> x2, Pallas kernels: none -> 22.7 us  [row_states(): pl.pallas_call(row_kernel, grid_spec=pltpu.PrefetchScalarGridSpec(num_sca...]
    ppermute x0 -> x4, waiting for transfers between devices: none -> 21.9 us  [along_x(): return lax.ppermute(array, 'req', pairs)]
    all_to_all x3 -> x4, starting transfers between devices: 36.5 us -> 54.1 us  [along_z(): lax.all_to_all(array, 'req', split_axis=0, concat_axis=0, tiled=True, axi...]
    scatter x1 -> x0, local copies, waits for them, and re-layouts: 13.7 us -> none  [local(): outgoing.at[slot_ids].set(jnp.repeat(grouped, depth_count, axis=0))]
    ppermute x0 -> x4, starting transfers between devices: none -> 13.5 us  [along_x(): return lax.ppermute(array, 'req', pairs)]
    concatenate x0 -> x6, other arithmetic: none -> 12.2 us  [the longest x1 7.99 us: local(): jnp.concatenate([mine[:, :both], right[:, :both], far, left[:, :both]], a...]
  transfers between devices with their start and end apart: 3 -> 8, of which waited for: 3 -> 5; matrix products, arithmetic and copies ran while one was open for 3% -> 17% of each run, Pallas kernels for 0% -> 10%
where the time goes in v3:
time: 235 us; the launch traced here: 234 us
  waiting for transfers between devices  71.5 us (30%)
  starting transfers between devices  67.6 us (29%)
  local copies, waits for them, and re-layouts  23.9 us (10%)
  Pallas kernels  22.7 us (10%)
  other arithmetic  20.9 us (9%)
  blocking collectives  16.3 us (7%)
  matrix products  7.2 us (3%)
  between operations  3.95 us (2%)
    all_to_all x4, starting transfers between devices, along_z(): lax.all_to_all(array, 'req', split_axis=0, concat_axis=0, tiled=True, axi...  54.1 us
    all_to_all x4, waiting for transfers between devices, along_z(): lax.all_to_all(array, 'req', split_axis=0, concat_axis=0, tiled=True, axi...  49.6 us
    pallas_call x2, Pallas kernels, row_states(): pl.pallas_call(row_kernel, grid_spec=pltpu.PrefetchScalarGridSpec(num_sca...  22.7 us
    ppermute x4, waiting for transfers between devices, along_x(): return lax.ppermute(array, 'req', pairs)  21.9 us
    all_to_all x1, blocking collectives, local(): return lax.all_to_all(merged, 'kv', split_axis=1, concat_axis=3, tiled=True)  16.3 us
    ppermute x4, starting transfers between devices, along_x(): return lax.ppermute(array, 'req', pairs)  13.5 us
    concatenate x1, other arithmetic, local(): jnp.concatenate([mine[:, :both], right[:, :both], far, left[:, :both]], a...  7.99 us
  transfers between devices with their start and end apart: 8, of which 5 were waited for; matrix products, arithmetic and copies ran while one was open for 17% of the time, Pallas kernels for 10%

profile of v3, /device:TPU:1, one launch (start us, length us, event | category | flops | bytes accessed | tf_op | source)
XLA Modules:
  0.0 234.0 jit_solution(14215434506986823071)
XLA Ops:
  2.0 1.0 slice_bitcast_fusion.2
  4.8 15.7 %all-to-all-start.2 = ((bf16[16,184,128]{2,1,0:T(8,128)(2,1)}), bf16[16,184,128]{2,1,0:T(8,128)(2,1)S(1)}, u32[]{:S(2)}, u32[]{:S(2)}) async-start(bf16[16,184,128]{2,1,0:T(8,128)(2,1)} %fusion.39), calls=%async_computation.2 | async-start | bytes 1507328 | tf_op jit(solution)/shard_map/all_to_all | solution.py:200
  21.8 1.4 maximum_maximum_fusion
  23.2 4.4 %collective-permute-start = (bf16[2,2064,128]{2,1,0:T(8,128)(2,1)S(1)}, bf16[2,2064,128]{2,1,0:T(8,128)(2,1)S(1)}, u32[]{:S(2)}, u32[]{:S(2)}) collective-permute-start(bf16[2,2064,128]{2,1,0:T(8,128)(2,1)S(1)} %maximum_maximum_fusion), channel_id=1, source_target_pairs={{0,3},{1,0},{2,1},{3,2},{4,7},{5,4},{6,5},{7,6},{8,11},{9,8},{10,9... | collective-permute-start | bytes 3170312 | tf_op jit(solution)/shard_map/ppermute | solution.py:241
  27.6 1.9 collective-permute-start.1
  29.5 19.7 %collective-permute-done = bf16[2,2064,128]{2,1,0:T(8,128)(2,1)S(1)} collective-permute-done((bf16[2,2064,128]{2,1,0:T(8,128)(2,1)S(1)}, bf16[2,2064,128]{2,1,0:T(8,128)(2,1)S(1)}, u32[]{:S(2)}, u32[]{:S(2)}) %collective-permute-start) | collective-permute-done | bytes 1056800 | tf_op jit(solution)/shard_map/ppermute | solution.py:241
  50.2 5.3 %collective-permute-start.3 = (bf16[2,1040,128]{2,1,0:T(8,128)(2,1)}, bf16[2,1040,128]{2,1,0:T(8,128)(2,1)}, u32[]{:S(2)}, u32[]{:S(2)}) collective-permute-start(bf16[2,1040,128]{2,1,0:T(8,128)(2,1)} %slice.233), channel_id=1, source_target_pairs={{0,3},{1,0},{2,1},{3,2},{4,7},{5,4},{6,5},{7,6},{8,11},{9,8},{10,9... | collective-permute-start | bytes 1597448 | tf_op jit(solution)/shard_map/ppermute | solution.py:241
  56.4 1.9 collective-permute-start.2
  58.3 1.6 gather_fusion.8
  60.5 1.2 slice.237
  63.7 1.2 copy-done.7
  64.9 1.0 slice.231
  65.9 1.3 slice.238
  67.9 1.1 slice.234
  68.9 2.1 collective-permute-done.2
  71.1 8.0 %pad_maximum_fusion.2.kv_ref = bf16[8,2048,128]{2,1,0:T(8,128)(2,1)} fusion(bf16[2,2048,128]{2,1,0:T(8,128)(2,1)S(1)} %slice-done, bf16[2,1024,128]{2,1,0:T(8,128)(2,1)S(1)} %slice.234, bf16[2,1024,128]{2,1,0:T(8,128)(2,1)} %collective-permute-done.2, bf16[2,2048,128]{2,1,0:T(8,128)(2,1)} %slice.231, bf16[2,1024,128]{2,1,0:T(8,128)(2,1)S(1)} %bitcast.258, ...), kind=kLoop, calls=%fused_computation.120 | loop fusion | flops 25165824 | bytes 8388608 | tf_op jit(solution)/shard_map/concatenate | solution.py:253
  79.1 10.9 %all-to-all-start.3 = ((bf16[16,176,128]{2,1,0:T(8,128)(2,1)}), bf16[16,176,128]{2,1,0:T(8,128)(2,1)S(1)}, u32[]{:S(2)}, u32[]{:S(2)}) async-start(bf16[16,176,128]{2,1,0:T(8,128)(2,1)} %bitcast.252), calls=%async_computation.3 | async-start | bytes 1441792 | tf_op jit(solution)/shard_map/all_to_all | solution.py:200
  94.5 11.3 %shard_map.91 = (bf16[16,176,128]{2,1,0:T(8,128)(2,1)S(1)}, f32[16,11,128]{2,1,0:T(8,128)S(1)}) custom-call(s32[1]{0:T(128)} %bitcast.28.tiles_ref, s32[16]{0:T(128)S(1)} %broadcast_minimum_fusion.1.span_ref, s32[256]{0:T(256)S(1)} %get-tuple-element.230.block_ref, s32[256]{0:T(256)S(1)} %get-tuple-element.229.line_ref, ...), custom_call_target="tpu_custom_call" | custom-call | flops 1543503872 | bytes 6455296 | tf_op jit(solution)/shard_map/pallas_call | solution.py:56
  107.0 11.2 %all-to-all-done.3.q_ref = bf16[16,176,128]{2,1,0:T(8,128)(2,1)S(1)} async-done(((bf16[16,176,128]{2,1,0:T(8,128)(2,1)}), bf16[16,176,128]{2,1,0:T(8,128)(2,1)S(1)}, u32[]{:S(2)}, u32[]{:S(2)}) %all-to-all-start.3) | async-done | bytes 720928 | tf_op jit(solution)/shard_map/all_to_all | solution.py:200
  118.2 14.8 %all-to-all-start.5 = ((bf16[16,184,128]{2,1,0:T(8,128)(2,1)}), bf16[16,184,128]{2,1,0:T(8,128)(2,1)S(1)}, u32[]{:S(2)}, u32[]{:S(2)}) async-start(bf16[16,184,128]{2,1,0:T(8,128)(2,1)} %pad_maximum_fusion.3), calls=%async_computation.5 | async-start | bytes 1507328 | tf_op jit(solution)/shard_map/all_to_all | solution.py:200
  133.1 2.0 fusion.103
  135.3 1.5 fusion.102
  137.0 11.3 %shard_map.92 = (bf16[16,176,128]{2,1,0:T(8,128)(2,1)S(1)}, f32[16,11,128]{2,1,0:T(8,128)S(1)}) custom-call(s32[1]{0:T(128)} %bitcast.28.tiles_ref, s32[16]{0:T(128)S(1)} %broadcast_minimum_fusion.1.span_ref, s32[256]{0:T(256)S(1)} %get-tuple-element.230.block_ref, s32[256]{0:T(256)S(1)} %get-tuple-element.229.line_ref, ...), custom_call_target="tpu_custom_call" | custom-call | flops 1476395008 | bytes 6356992 | tf_op jit(solution)/shard_map/pallas_call | solution.py:56
  149.5 16.1 %all-to-all-done.5 = bf16[16,184,128]{2,1,0:T(8,128)(2,1)S(1)} async-done(((bf16[16,184,128]{2,1,0:T(8,128)(2,1)}), bf16[16,184,128]{2,1,0:T(8,128)(2,1)S(1)}, u32[]{:S(2)}, u32[]{:S(2)}) %all-to-all-start.5) | async-done | bytes 753696 | tf_op jit(solution)/shard_map/all_to_all | solution.py:200
  165.5 12.7 %all-to-all-start.4 = ((bf16[16,184,128]{2,1,0:T(8,128)(2,1)}), bf16[16,184,128]{2,1,0:T(8,128)(2,1)S(1)}, u32[]{:S(2)}, u32[]{:S(2)}) async-start(bf16[16,184,128]{2,1,0:T(8,128)(2,1)} %pad_maximum_fusion.4), calls=%async_computation.4 | async-start | bytes 1507328 | tf_op jit(solution)/shard_map/all_to_all | solution.py:200
  178.2 1.2 fusion.53
  180.8 1.2 fusion.55
  182.1 2.5 %fusion.36 = f32[32,4,8,128]{3,2,1,0:T(8,128)} fusion(f32[32,4,8,128]{3,2,1,0:T(8,128)S(1)} %fusion.55, bf16[32,128,1,128]{3,1,2,0:T(8,128)(2,1)} %param.15, f32[32,4,1,8,128]{4,3,1,0,2:T(8,128)S(1)} %copy-done.9, f32[32,4,8]{2,1,0:T(4,128)S(1)} %copy.206, f32[32,4,8]{2,1,0:T(4,128)S(1)} %copy.199), kind=kOutput, calls=%fused_computation.134 | convolution fusion | flops 34078720 | bytes 2629632 | tf_op jit(solution)/shard_map/rsngt,rtnd->rsngd/dot_general | solution.py:129
  185.7 1.9 gather_fusion.10
  189.3 22.4 %all-to-all-done.4 = bf16[16,184,128]{2,1,0:T(8,128)(2,1)S(1)} async-done(((bf16[16,184,128]{2,1,0:T(8,128)(2,1)}), bf16[16,184,128]{2,1,0:T(8,128)(2,1)S(1)}, u32[]{:S(2)}, u32[]{:S(2)}) %all-to-all-start.4) | async-done | bytes 753696 | tf_op jit(solution)/shard_map/all_to_all | solution.py:200
  215.5 1.2 fusion.50
  217.0 16.3 %all_to_all.46 = bf16[4,8,4,1024]{3,2,0,1:T(4,128)(2,1)S(1)} all-to-all(bf16[4,8,4,1024]{3,2,0,1:T(4,128)(2,1)S(1)} %copy.215), channel_id=1, replica_groups=mesh['kv'=8,'req'=64] {'kv'}, dimensions={1} | all-to-all | bytes 524288 | tf_op jit(solution)/shard_map/all_to_all | solution.py:300
  (164 shorter events, 22.8 us)
Async XLA Ops:
  0.0 135.3 %copy-start = (bf16[32,128,1,128]{3,1,2,0:T(8,128)(2,1)S(1)}, bf16[32,128,1,128]{3,1,2,0:T(8,128)(2,1)}, u32[]{:S(2)}) copy-start(bf16[32,128,1,128]{3,1,2,0:T(8,128)(2,1)} %param.14) | copy-start | bytes 3145732
  3.8 18.0 %copy-start.8 = (bf16[2,1024,1,128]{3,1,2,0:T(8,128)(2,1)S(1)}, bf16[2,1024,1,128]{3,1,2,0:T(8,128)(2,1)}, u32[]{:S(2)}) copy-start(bf16[2,1024,1,128]{3,1,2,0:T(8,128)(2,1)} %param.19) | copy-start | bytes 1572868
  4.8 74.3 %all-to-all-start.2 = ((bf16[16,184,128]{2,1,0:T(8,128)(2,1)}), bf16[16,184,128]{2,1,0:T(8,128)(2,1)S(1)}, u32[]{:S(2)}, u32[]{:S(2)}) async-start(bf16[16,184,128]{2,1,0:T(8,128)(2,1)} %fusion.39), calls=%async_computation.2 | async-start | bytes 1507328 | tf_op jit(solution)/shard_map/all_to_all | solution.py:200
  23.2 26.1 %collective-permute-start = (bf16[2,2064,128]{2,1,0:T(8,128)(2,1)S(1)}, bf16[2,2064,128]{2,1,0:T(8,128)(2,1)S(1)}, u32[]{:S(2)}, u32[]{:S(2)}) collective-permute-start(bf16[2,2064,128]{2,1,0:T(8,128)(2,1)S(1)} %maximum_maximum_fusion), channel_id=1, source_target_pairs={{0,3},{1,0},{2,1},{3,2},{4,7},{5,4},{6,5},{7,6},{8,11},{9,8},{10,9... | collective-permute-start | bytes 3170312 | tf_op jit(solution)/shard_map/ppermute | solution.py:241
  27.6 27.9 %collective-permute-start.1 = (bf16[2,2064,128]{2,1,0:T(8,128)(2,1)S(1)}, bf16[2,2064,128]{2,1,0:T(8,128)(2,1)S(1)}, u32[]{:S(2)}, u32[]{:S(2)}) collective-permute-start(bf16[2,2064,128]{2,1,0:T(8,128)(2,1)S(1)} %maximum_maximum_fusion), channel_id=1, source_target_pairs={{0,1},{1,2},{2,3},{3,0},{4,5},{5,6},{6,7},{7,4},{8,9},{9,10},{10,1... | collective-permute-start | bytes 3170312 | tf_op jit(solution)/shard_map/ppermute | solution.py:241
  49.3 6.3 %copy-start.6 = (bf16[2,2064,128]{2,1,0:T(8,128)(2,1)}, bf16[2,2064,128]{2,1,0:T(8,128)(2,1)S(1)}, u32[]{:S(2)}) copy-start(bf16[2,2064,128]{2,1,0:T(8,128)(2,1)S(1)} %collective-permute-done) | copy-start | bytes 3170308
  50.2 15.7 %collective-permute-start.3 = (bf16[2,1040,128]{2,1,0:T(8,128)(2,1)}, bf16[2,1040,128]{2,1,0:T(8,128)(2,1)}, u32[]{:S(2)}, u32[]{:S(2)}) collective-permute-start(bf16[2,1040,128]{2,1,0:T(8,128)(2,1)} %slice.233), channel_id=1, source_target_pairs={{0,3},{1,0},{2,1},{3,2},{4,7},{5,4},{6,5},{7,6},{8,11},{9,8},{10,9... | collective-permute-start | bytes 1597448 | tf_op jit(solution)/shard_map/ppermute | solution.py:241
  55.5 8.1 %copy-start.5 = (bf16[2,2064,128]{2,1,0:T(8,128)(2,1)}, bf16[2,2064,128]{2,1,0:T(8,128)(2,1)S(1)}, u32[]{:S(2)}) copy-start(bf16[2,2064,128]{2,1,0:T(8,128)(2,1)S(1)} %collective-permute-done.1) | copy-start | bytes 3170308
  56.4 14.7 %collective-permute-start.2 = (bf16[2,1024,128]{2,1,0:T(8,128)(2,1)}, bf16[2,1024,128]{2,1,0:T(8,128)(2,1)}, u32[]{:S(2)}, u32[]{:S(2)}) collective-permute-start(bf16[2,1024,128]{2,1,0:T(8,128)(2,1)} %slice.232), channel_id=1, source_target_pairs={{0,1},{1,2},{2,3},{3,0},{4,5},{5,6},{6,7},{7,4},{8,9},{9,10},{10,1... | collective-permute-start | bytes 1572872 | tf_op jit(solution)/shard_map/ppermute | solution.py:241
  63.6 1.2 copy-start.7
  65.9 5.2 %slice-start = ((bf16[2,2064,128]{2,1,0:T(8,128)(2,1)}), bf16[2,2048,128]{2,1,0:T(8,128)(2,1)S(1)}, s32[]{:S(2)}) async-start(bf16[2,2064,128]{2,1,0:T(8,128)(2,1)} %copy-done.5), calls=%async_computation.7 | async-start | bytes 2097152 | tf_op jit(solution)/shard_map/slice | solution.py:253
  79.1 39.1 %all-to-all-start.3 = ((bf16[16,176,128]{2,1,0:T(8,128)(2,1)}), bf16[16,176,128]{2,1,0:T(8,128)(2,1)S(1)}, u32[]{:S(2)}, u32[]{:S(2)}) async-start(bf16[16,176,128]{2,1,0:T(8,128)(2,1)} %bitcast.252), calls=%async_computation.3 | async-start | bytes 1441792 | tf_op jit(solution)/shard_map/all_to_all | solution.py:200
  106.0 27.1 %copy-start.1 = (bf16[32,4,8,128]{3,2,1,0:T(8,128)(2,1)S(1)}, bf16[32,4,8,128]{3,2,1,0:T(8,128)(2,1)}, u32[]{:S(2)}) copy-start(bf16[32,4,8,128]{3,2,1,0:T(8,128)(2,1)} %param.11) | copy-start | bytes 786436
  106.0 27.1 %copy-start.26 = (bf16[32,4,1,128]{3,1,2,0:T(4,128)(2,1)S(1)}, bf16[32,4,1,128]{3,1,2,0:T(4,128)(2,1)}, u32[]{:S(2)}) copy-start(bf16[32,4,1,128]{3,1,2,0:T(4,128)(2,1)} %param.12) | copy-start | bytes 98308
  107.0 28.2 %copy-start.23 = (s32[32]{0:T(128)S(1)}, s32[32]{0:T(128)}, u32[]{:S(2)}) copy-start(s32[32]{0:T(128)} %param.16) | copy-start | bytes 388
  118.2 47.4 %all-to-all-start.5 = ((bf16[16,184,128]{2,1,0:T(8,128)(2,1)}), bf16[16,184,128]{2,1,0:T(8,128)(2,1)S(1)}, u32[]{:S(2)}, u32[]{:S(2)}) async-start(bf16[16,184,128]{2,1,0:T(8,128)(2,1)} %pad_maximum_fusion.3), calls=%async_computation.5 | async-start | bytes 1507328 | tf_op jit(solution)/shard_map/all_to_all | solution.py:200
  149.4 30.2 %copy-start.9 = (f32[32,4,1,8,128]{4,3,1,0,2:T(8,128)S(1)}, f32[32,4,1,8,128]{4,3,1,0,2:T(8,128)}, u32[]{:S(2)}) copy-start(f32[32,4,1,8,128]{4,3,1,0,2:T(8,128)} %get-tuple-element.237) | copy-start | bytes 1572868
  149.4 31.4 %copy-start.20 = (bf16[32,4,1,128]{3,1,2,0:T(4,128)(2,1)S(1)}, bf16[32,4,1,128]{3,1,2,0:T(4,128)(2,1)}, u32[]{:S(2)}) copy-start(bf16[32,4,1,128]{3,1,2,0:T(4,128)(2,1)} %param.13) | copy-start | bytes 98308
  165.5 46.1 %all-to-all-start.4 = ((bf16[16,184,128]{2,1,0:T(8,128)(2,1)}), bf16[16,184,128]{2,1,0:T(8,128)(2,1)S(1)}, u32[]{:S(2)}, u32[]{:S(2)}) async-start(bf16[16,184,128]{2,1,0:T(8,128)(2,1)} %pad_maximum_fusion.4), calls=%async_computation.4 | async-start | bytes 1507328 | tf_op jit(solution)/shard_map/all_to_all | solution.py:200
  185.7 3.3 %copy-start.10 = (f32[32,4,8,128]{3,2,1,0:T(8,128)S(1)}, f32[32,4,8,128]{3,2,1,0:T(8,128)}, u32[]{:S(2)}) copy-start(f32[32,4,8,128]{3,2,1,0:T(8,128)} %fusion.36) | copy-start | bytes 1572868
  214.0 2.8 %copy-start.2 = (bf16[32,4,8,128]{3,2,1,0:T(8,128)(2,1)S(1)}, bf16[32,4,8,128]{3,2,1,0:T(8,128)(2,1)}, u32[]{:S(2)}) copy-start(bf16[32,4,8,128]{3,2,1,0:T(8,128)(2,1)} %param.11) | copy-start | bytes 786436
  214.0 2.8 %copy-start.21 = (s32[128]{0:T(128)S(1)}, s32[128]{0:T(128)}, u32[]{:S(2)}) copy-start(s32[128]{0:T(128)} %get-tuple-element.233) | copy-start | bytes 1540
  214.0 2.8 %copy-start.22 = (s32[128]{0:T(128)S(1)}, s32[128]{0:T(128)}, u32[]{:S(2)}) copy-start(s32[128]{0:T(128)} %get-tuple-element.234) | copy-start | bytes 1540
  214.0 2.8 %copy-start.24 = (s32[128]{0:T(128)S(1)}, s32[128]{0:T(128)}, u32[]{:S(2)}) copy-start(s32[128]{0:T(128)} %get-tuple-element.199) | copy-start | bytes 1540
  214.0 2.8 %copy-start.25 = (pred[128]{0:T(512)(128)(4,1)S(1)}, pred[128]{0:T(512)(128)(4,1)}, u32[]{:S(2)}) copy-start(pred[128]{0:T(512)(128)(4,1)} %broadcast_compare_fusion.3) | copy-start | bytes 388

commit v4 on v3

--- a/solution.py
+++ b/solution.py
@@ -19,14 +19,34 @@
     return lax.dot_general(a, b, (dims, ((), ())), preferred_element_type=jnp.float32)
 
 
-def row_kernel(tiles_ref, span_ref, block_ref, line_ref, q_ref, kv_ref, out_ref, logs_ref):
+def row_kernel(
+    tiles_ref, span_ref, block_ref, line_ref,
+    q_ref, mine_ref, right_ref, far_keys_ref, far_rest_ref, left_ref,
+    out_ref, logs_ref, kv_ref, sems,
+):
     blocks, slots, width = logs_ref.shape
     per = out_ref.shape[1] // slots
     length = kv_ref.shape[1] // 2
     items = TILE // per
     scale = width ** (-0.5)
+    each = mine_ref.shape[0]
+    both = 2 * length
+    pieces = (
+        (mine_ref.at[:, :both], kv_ref.at[:each]),
+        (right_ref.at[:, :both], kv_ref.at[each : 2 * each]),
+        (far_keys_ref, kv_ref.at[2 * each : 3 * each, :length]),
+        (far_rest_ref.at[:, :length], kv_ref.at[2 * each : 3 * each, length:]),
+        (left_ref.at[:, :both], kv_ref.at[3 * each :]),
+    )
+    copies = [
+        pltpu.make_async_copy(piece, place, sems.at[i]) for i, (piece, place) in enumerate(pieces)
+    ]
+    for copy in copies:
+        copy.start()
     out_ref[...] = jnp.zeros_like(out_ref)
     logs_ref[...] = jnp.zeros_like(logs_ref)
+    for copy in copies:
+        copy.wait()
 
     def one_tile(t, carry):
         span = span_ref[t]
@@ -50,9 +70,10 @@
     lax.fori_loop(0, tiles_ref[0], one_tile, 0)
 
 
-def row_states(plan, q, kv, slots, per):
+def row_states(plan, q, spans, slots, per):
     blocks, _, width = q.shape
     lines = slots * per
+    each, length = spans[2].shape[:2]
     return pl.pallas_call(
         row_kernel,
         grid_spec=pltpu.PrefetchScalarGridSpec(
@@ -60,11 +81,15 @@
             grid=(1,),
             in_specs=[
                 pl.BlockSpec((blocks, lines, width), lambda i, *_: (0, 0, 0)),
-                pl.BlockSpec(kv.shape, lambda i, *_: (0, 0, 0)),
-            ],
+            ]
+            + [pl.BlockSpec(memory_space=pl.ANY)] * len(spans),
             out_specs=[
                 pl.BlockSpec((blocks, lines, width), lambda i, *_: (0, 0, 0)),
                 pl.BlockSpec((blocks, slots, width), lambda i, *_: (0, 0, 0)),
+            ],
+            scratch_shapes=[
+                pltpu.VMEM((NX * each, 2 * length, width), jnp.bfloat16),
+                pltpu.SemaphoreType.DMA((len(spans),)),
             ],
         ),
         out_shape=[
@@ -73,11 +98,9 @@
         ],
         compiler_params=pltpu.CompilerParams(vmem_limit_bytes=48 * 1024 * 1024),
         cost_estimate=pl.CostEstimate(
-            flops=2 * q.size * kv.shape[1],
-            bytes_accessed=6 * q.size + 2 * kv.size,
-            transcendentals=q.size // width * kv.shape[1] // 2,
+            flops=q.size, bytes_accessed=4 * q.size, transcendentals=0
         ),
-    )(*plan, q, kv)
+    )(*plan, q, *spans)
 
 
 def tile_plan(spans, count, per):
@@ -248,9 +271,7 @@
     far_rest = along_x(right[:, span_len:], -1)
     lacking = jnp.maximum(over, jnp.maximum(left[0, -1, 0], right[0, -1, 0]))
     lacking = jnp.maximum(lacking, far_rest[0, -1, 0])
-    both = 2 * span_len
-    far = jnp.concatenate([far_keys, far_rest[:, :span_len]], axis=1)
-    spans = jnp.concatenate([mine[:, :both], right[:, :both], far, left[:, :both]], axis=0)
+    spans = (mine, right, far_keys, far_rest, left)
 
     kv_local = new_keys.shape[2]
     grouped = queries.reshape(requests, steps, kv_local, heads // kv_local, width)

time: 235 us -> 231 us (0.983)
  local copies, waits for them, and re-layouts: 23.9 us -> 28.9 us
  waiting for transfers between devices: 71.5 us -> 68.3 us
    concatenate x1 -> x0, other arithmetic: 7.99 us -> none  [local(): jnp.concatenate([mine[:, :both], right[:, :both], far, left[:, :both]], a...]
  transfers between devices with their start and end apart: 8 -> 8, of which waited for: 5 -> 4; matrix products, arithmetic and copies ran while one was open for 17% -> 16% of each run, Pallas kernels for 10% -> 9%
where the time goes in v4:
time: 231 us; the launch traced here: 230 us
  waiting for transfers between devices  68.3 us (30%)
  starting transfers between devices  65.9 us (29%)
  local copies, waits for them, and re-layouts  28.9 us (13%)
  Pallas kernels  20.7 us (9%)
  other arithmetic  18.7 us (8%)
  blocking collectives  16.3 us (7%)
  matrix products  7.27 us (3%)
  between operations  3.94 us (2%)
    all_to_all x4, starting transfers between devices, along_z(): lax.all_to_all(array, 'req', split_axis=0, concat_axis=0, tiled=True, axi...  52.4 us
    all_to_all x4, waiting for transfers between devices, along_z(): lax.all_to_all(array, 'req', split_axis=0, concat_axis=0, tiled=True, axi...  48.5 us
    pallas_call x2, Pallas kernels, row_states(): pl.pallas_call(row_kernel, grid_spec=pltpu.PrefetchScalarGridSpec(num_sca...  20.7 us
    ppermute x4, waiting for transfers between devices, along_x(): return lax.ppermute(array, 'req', pairs)  19.7 us
    all_to_all x1, blocking collectives, local(): return lax.all_to_all(merged, 'kv', split_axis=1, concat_axis=3, tiled=True)  16.3 us
    ppermute x4, starting transfers between devices, along_x(): return lax.ppermute(array, 'req', pairs)  13.5 us
  transfers between devices with their start and end apart: 8, of which 4 were waited for; matrix products, arithmetic and copies ran while one was open for 16% of the time, Pallas kernels for 9%

profile of v4, /device:TPU:1, one launch (start us, length us, event | category | flops | bytes accessed | tf_op | source)
XLA Modules:
  0.0 230.2 jit_solution(7130009763029094306)
XLA Ops:
  4.7 15.9 %all-to-all-start.2 = ((bf16[16,184,128]{2,1,0:T(8,128)(2,1)}), bf16[16,184,128]{2,1,0:T(8,128)(2,1)S(1)}, u32[]{:S(2)}, u32[]{:S(2)}) async-start(bf16[16,184,128]{2,1,0:T(8,128)(2,1)} %fusion.39), calls=%async_computation.2 | async-start | bytes 1507328 | tf_op jit(solution)/shard_map/all_to_all | solution.py:223
  21.8 1.4 maximum_maximum_fusion.mine_ref
  23.2 4.4 %collective-permute-start = (bf16[2,2064,128]{2,1,0:T(8,128)(2,1)S(1)}, bf16[2,2064,128]{2,1,0:T(8,128)(2,1)S(1)}, u32[]{:S(2)}, u32[]{:S(2)}) collective-permute-start(bf16[2,2064,128]{2,1,0:T(8,128)(2,1)S(1)} %maximum_maximum_fusion.mine_ref), channel_id=1, source_target_pairs={{0,3},{1,0},{2,1},{3,2},{4,7},{5,4},{6,5},{7,6},{8,11},{9,8},{10,9... | collective-permute-start | bytes 3170312 | tf_op jit(solution)/shard_map/ppermute | solution.py:264
  27.6 1.9 collective-permute-start.1
  29.6 19.7 %collective-permute-done.right_ref = bf16[2,2064,128]{2,1,0:T(8,128)(2,1)S(1)} collective-permute-done((bf16[2,2064,128]{2,1,0:T(8,128)(2,1)S(1)}, bf16[2,2064,128]{2,1,0:T(8,128)(2,1)S(1)}, u32[]{:S(2)}, u32[]{:S(2)}) %collective-permute-start) | collective-permute-done | bytes 1056800 | tf_op jit(solution)/shard_map/ppermute | solution.py:264
  51.1 5.3 %collective-permute-start.3 = (bf16[2,1040,128]{2,1,0:T(8,128)(2,1)}, bf16[2,1040,128]{2,1,0:T(8,128)(2,1)S(1)}, u32[]{:S(2)}, u32[]{:S(2)}) collective-permute-start(bf16[2,1040,128]{2,1,0:T(8,128)(2,1)} %slice.218), channel_id=1, source_target_pairs={{0,3},{1,0},{2,1},{3,2},{4,7},{5,4},{6,5},{7,6},{8,11},{9,8},{10,9... | collective-permute-start | bytes 1597448 | tf_op jit(solution)/shard_map/ppermute | solution.py:264
  56.5 1.6 gather_fusion.8
  58.1 1.9 slice.217
  59.9 1.9 collective-permute-start.2
  61.9 1.3 slice.219
  63.1 1.2 slice.220
  67.6 11.2 %all-to-all-start.3 = ((bf16[16,176,128]{2,1,0:T(8,128)(2,1)}), bf16[16,176,128]{2,1,0:T(8,128)(2,1)S(1)}, u32[]{:S(2)}, u32[]{:S(2)}) async-start(bf16[16,176,128]{2,1,0:T(8,128)(2,1)} %bitcast.252), calls=%async_computation.3 | async-start | bytes 1441792 | tf_op jit(solution)/shard_map/all_to_all | solution.py:223
  83.3 10.4 %shard_map.91 = (bf16[16,176,128]{2,1,0:T(8,128)(2,1)S(1)}, f32[16,11,128]{2,1,0:T(8,128)S(1)}) custom-call(s32[1]{0:T(128)} %bitcast.28.tiles_ref, s32[16]{0:T(128)S(1)} %broadcast_minimum_fusion.1.span_ref, s32[256]{0:T(256)S(1)} %get-tuple-element.258.block_ref, s32[256]{0:T(256)S(1)} %get-tuple-element.257.line_ref, ...), custom_call_target="tpu_custom_call" | custom-call | flops 376832 | bytes 1507328 | tf_op jit(solution)/shard_map/pallas_call | solution.py:77
  94.9 14.3 %all-to-all-done.3.q_ref = bf16[16,176,128]{2,1,0:T(8,128)(2,1)S(1)} async-done(((bf16[16,176,128]{2,1,0:T(8,128)(2,1)}), bf16[16,176,128]{2,1,0:T(8,128)(2,1)S(1)}, u32[]{:S(2)}, u32[]{:S(2)}) %all-to-all-start.3) | async-done | bytes 720928 | tf_op jit(solution)/shard_map/all_to_all | solution.py:223
  109.2 12.7 %all-to-all-start.5 = ((bf16[16,184,128]{2,1,0:T(8,128)(2,1)}), bf16[16,184,128]{2,1,0:T(8,128)(2,1)}, u32[]{:S(2)}, u32[]{:S(2)}) async-start(bf16[16,184,128]{2,1,0:T(8,128)(2,1)} %pad_maximum_fusion.2), calls=%async_computation.5 | async-start | bytes 1507328 | tf_op jit(solution)/shard_map/all_to_all | solution.py:223
  122.0 2.0 fusion.103
  124.2 1.5 fusion.102
  127.0 10.3 %shard_map.92 = (bf16[16,176,128]{2,1,0:T(8,128)(2,1)S(1)}, f32[16,11,128]{2,1,0:T(8,128)S(1)}) custom-call(s32[1]{0:T(128)} %bitcast.28.tiles_ref, s32[16]{0:T(128)S(1)} %broadcast_minimum_fusion.1.span_ref, s32[256]{0:T(256)S(1)} %get-tuple-element.258.block_ref, s32[256]{0:T(256)S(1)} %get-tuple-element.257.line_ref, ...), custom_call_target="tpu_custom_call" | custom-call | flops 360448 | bytes 1441792 | tf_op jit(solution)/shard_map/pallas_call | solution.py:77
  138.4 16.1 %all-to-all-done.5 = bf16[16,184,128]{2,1,0:T(8,128)(2,1)} async-done(((bf16[16,184,128]{2,1,0:T(8,128)(2,1)}), bf16[16,184,128]{2,1,0:T(8,128)(2,1)}, u32[]{:S(2)}, u32[]{:S(2)}) %all-to-all-start.5) | async-done | bytes 753696 | tf_op jit(solution)/shard_map/all_to_all | solution.py:223
  154.5 12.7 %all-to-all-start.4 = ((bf16[16,184,128]{2,1,0:T(8,128)(2,1)}), bf16[16,184,128]{2,1,0:T(8,128)(2,1)S(1)}, u32[]{:S(2)}, u32[]{:S(2)}) async-start(bf16[16,184,128]{2,1,0:T(8,128)(2,1)} %pad_maximum_fusion.3), calls=%async_computation.4 | async-start | bytes 1507328 | tf_op jit(solution)/shard_map/all_to_all | solution.py:223
  167.2 1.2 fusion.53
  170.5 1.3 fusion.55
  171.8 2.5 %fusion.36 = f32[32,4,8,128]{3,2,1,0:T(8,128)} fusion(f32[32,4,8,128]{3,2,1,0:T(8,128)S(1)} %fusion.55, bf16[32,128,1,128]{3,1,2,0:T(8,128)(2,1)} %param.15, f32[32,4,1,8,128]{4,3,1,0,2:T(8,128)S(1)} %copy-done.11, f32[32,4,8]{2,1,0:T(4,128)S(1)} %copy.206, f32[32,4,8]{2,1,0:T(4,128)S(1)} %copy.199), kind=kOutput, calls=%fused_computation.133 | convolution fusion | flops 34078720 | bytes 2629632 | tf_op jit(solution)/shard_map/rsngt,rtnd->rsngd/dot_general | solution.py:152
  175.3 2.0 slice.227
  177.3 1.8 gather_fusion.10
  180.6 1.8 fusion.49
  182.4 18.1 %all-to-all-done.4 = bf16[16,184,128]{2,1,0:T(8,128)(2,1)S(1)} async-done(((bf16[16,184,128]{2,1,0:T(8,128)(2,1)}), bf16[16,184,128]{2,1,0:T(8,128)(2,1)S(1)}, u32[]{:S(2)}, u32[]{:S(2)}) %all-to-all-start.4) | async-done | bytes 753696 | tf_op jit(solution)/shard_map/all_to_all | solution.py:223
  202.3 2.6 %gather_fusion.12 = bf16[128,16,128]{2,1,0:T(8,128)(2,1)} fusion(bf16[176,16,128]{2,1,0:T(8,128)(2,1)} %bitcast.255, s32[1024]{0:T(1024)S(1)} %pad_clamp_fusion.4), kind=kCustom, calls=%fused_computation.12 | custom fusion | bytes 1049088 | tf_op jit(solution)/shard_map/gather | solution.py:251
  207.4 1.5 multiply_reduce_fusion.2
  208.9 1.2 fusion.50
  210.1 1.6 pad_maximum_fusion.4
  213.1 16.3 %all_to_all.46 = bf16[4,8,4,1024]{3,2,0,1:T(4,128)(2,1)S(1)} all-to-all(bf16[4,8,4,1024]{3,2,0,1:T(4,128)(2,1)S(1)} %copy.215), channel_id=1, replica_groups=mesh['kv'=8,'req'=64] {'kv'}, dimensions={1} | all-to-all | bytes 524288 | tf_op jit(solution)/shard_map/all_to_all | solution.py:321
  (169 shorter events, 26.7 us)
Async XLA Ops:
  0.0 124.1 %copy-start = (bf16[32,128,1,128]{3,1,2,0:T(8,128)(2,1)S(1)}, bf16[32,128,1,128]{3,1,2,0:T(8,128)(2,1)}, u32[]{:S(2)}) copy-start(bf16[32,128,1,128]{3,1,2,0:T(8,128)(2,1)} %param.14) | copy-start | bytes 3145732
  4.7 17.2 %copy-start.17 = (bf16[2,1024,1,128]{3,1,2,0:T(8,128)(2,1)S(1)}, bf16[2,1024,1,128]{3,1,2,0:T(8,128)(2,1)}, u32[]{:S(2)}) copy-start(bf16[2,1024,1,128]{3,1,2,0:T(8,128)(2,1)} %param.19) | copy-start | bytes 1572868
  4.7 62.9 %all-to-all-start.2 = ((bf16[16,184,128]{2,1,0:T(8,128)(2,1)}), bf16[16,184,128]{2,1,0:T(8,128)(2,1)S(1)}, u32[]{:S(2)}, u32[]{:S(2)}) async-start(bf16[16,184,128]{2,1,0:T(8,128)(2,1)} %fusion.39), calls=%async_computation.2 | async-start | bytes 1507328 | tf_op jit(solution)/shard_map/all_to_all | solution.py:223
  23.2 34.8 %copy-start.1 = (bf16[2,2064,128]{2,1,0:T(8,128)(2,1)}, bf16[2,2064,128]{2,1,0:T(8,128)(2,1)S(1)}, u32[]{:S(2)}) copy-start(bf16[2,2064,128]{2,1,0:T(8,128)(2,1)S(1)} %maximum_maximum_fusion.mine_ref) | copy-start | bytes 3170308
  23.2 26.1 %collective-permute-start = (bf16[2,2064,128]{2,1,0:T(8,128)(2,1)S(1)}, bf16[2,2064,128]{2,1,0:T(8,128)(2,1)S(1)}, u32[]{:S(2)}, u32[]{:S(2)}) collective-permute-start(bf16[2,2064,128]{2,1,0:T(8,128)(2,1)S(1)} %maximum_maximum_fusion.mine_ref), channel_id=1, source_target_pairs={{0,3},{1,0},{2,1},{3,2},{4,7},{5,4},{6,5},{7,6},{8,11},{9,8},{10,9... | collective-permute-start | bytes 3170312 | tf_op jit(solution)/shard_map/ppermute | solution.py:264
  27.6 30.4 %collective-permute-start.1 = (bf16[2,2064,128]{2,1,0:T(8,128)(2,1)S(1)}, bf16[2,2064,128]{2,1,0:T(8,128)(2,1)}, u32[]{:S(2)}, u32[]{:S(2)}) collective-permute-start(bf16[2,2064,128]{2,1,0:T(8,128)(2,1)S(1)} %maximum_maximum_fusion.mine_ref), channel_id=1, source_target_pairs={{0,1},{1,2},{2,3},{3,0},{4,5},{5,6},{6,7},{7,4},{8,9},{9,10},{10,1... | collective-permute-start | bytes 3170312 | tf_op jit(solution)/shard_map/ppermute | solution.py:264
  49.3 1.0 copy-start.3
  51.1 15.2 %collective-permute-start.3 = (bf16[2,1040,128]{2,1,0:T(8,128)(2,1)}, bf16[2,1040,128]{2,1,0:T(8,128)(2,1)S(1)}, u32[]{:S(2)}, u32[]{:S(2)}) collective-permute-start(bf16[2,1040,128]{2,1,0:T(8,128)(2,1)} %slice.218), channel_id=1, source_target_pairs={{0,3},{1,0},{2,1},{3,2},{4,7},{5,4},{6,5},{7,6},{8,11},{9,8},{10,9... | collective-permute-start | bytes 1597448 | tf_op jit(solution)/shard_map/ppermute | solution.py:264
  59.9 23.3 %collective-permute-start.2 = (bf16[2,1024,128]{2,1,0:T(8,128)(2,1)}, bf16[2,1024,128]{2,1,0:T(8,128)(2,1)}, u32[]{:S(2)}, u32[]{:S(2)}) collective-permute-start(bf16[2,1024,128]{2,1,0:T(8,128)(2,1)} %slice.217), channel_id=1, source_target_pairs={{0,1},{1,2},{2,3},{3,0},{4,5},{5,6},{6,7},{7,4},{8,9},{9,10},{10,1... | collective-permute-start | bytes 1572872 | tf_op jit(solution)/shard_map/ppermute | solution.py:264
  66.4 16.9 %copy-start.5 = (bf16[2,1040,128]{2,1,0:T(8,128)(2,1)}, bf16[2,1040,128]{2,1,0:T(8,128)(2,1)S(1)}, u32[]{:S(2)}) copy-start(bf16[2,1040,128]{2,1,0:T(8,128)(2,1)S(1)} %collective-permute-done.3.far_rest_ref) | copy-start | bytes 1597444
  67.6 41.6 %all-to-all-start.3 = ((bf16[16,176,128]{2,1,0:T(8,128)(2,1)}), bf16[16,176,128]{2,1,0:T(8,128)(2,1)S(1)}, u32[]{:S(2)}, u32[]{:S(2)}) async-start(bf16[16,176,128]{2,1,0:T(8,128)(2,1)} %bitcast.252), calls=%async_computation.3 | async-start | bytes 1441792 | tf_op jit(solution)/shard_map/all_to_all | solution.py:223
  94.9 27.1 %copy-start.4 = (bf16[32,4,8,128]{3,2,1,0:T(8,128)(2,1)S(1)}, bf16[32,4,8,128]{3,2,1,0:T(8,128)(2,1)}, u32[]{:S(2)}) copy-start(bf16[32,4,8,128]{3,2,1,0:T(8,128)(2,1)} %param.11) | copy-start | bytes 786436
  94.9 27.1 %copy-start.28 = (bf16[32,4,1,128]{3,1,2,0:T(4,128)(2,1)S(1)}, bf16[32,4,1,128]{3,1,2,0:T(4,128)(2,1)}, u32[]{:S(2)}) copy-start(bf16[32,4,1,128]{3,1,2,0:T(4,128)(2,1)} %param.12) | copy-start | bytes 98308
  94.9 29.2 %copy-start.25 = (s32[32]{0:T(128)S(1)}, s32[32]{0:T(128)}, u32[]{:S(2)}) copy-start(s32[32]{0:T(128)} %param.16) | copy-start | bytes 388
  109.2 45.3 %all-to-all-start.5 = ((bf16[16,184,128]{2,1,0:T(8,128)(2,1)}), bf16[16,184,128]{2,1,0:T(8,128)(2,1)}, u32[]{:S(2)}, u32[]{:S(2)}) async-start(bf16[16,184,128]{2,1,0:T(8,128)(2,1)} %pad_maximum_fusion.2), calls=%async_computation.5 | async-start | bytes 1507328 | tf_op jit(solution)/shard_map/all_to_all | solution.py:223
  124.2 2.8 %copy-start.6 = (bf16[2,1040,128]{2,1,0:T(8,128)(2,1)S(1)}, bf16[2,1040,128]{2,1,0:T(8,128)(2,1)}, u32[]{:S(2)}) copy-start(bf16[2,1040,128]{2,1,0:T(8,128)(2,1)} %copy-done.5) | copy-start | bytes 1597444
  125.7 0.6 copy-start.18
  138.4 30.0 %copy-start.20 = (s32[32,4]{1,0:T(8,128)S(1)}, s32[32,4]{1,0:T(8,128)}, u32[]{:S(2)}) copy-start(s32[32,4]{1,0:T(8,128)} %fusion.79) | copy-start | bytes 1540
  138.4 30.2 %copy-start.11 = (f32[32,4,1,8,128]{4,3,1,0,2:T(8,128)S(1)}, f32[32,4,1,8,128]{4,3,1,0,2:T(8,128)}, u32[]{:S(2)}) copy-start(f32[32,4,1,8,128]{4,3,1,0,2:T(8,128)} %get-tuple-element.265) | copy-start | bytes 1572868
  138.4 30.7 %copy-start.19 = (f32[32,4,8]{0,2,1:T(8,128)S(1)}, f32[32,4,8]{0,2,1:T(8,128)}, u32[]{:S(2)}) copy-start(f32[32,4,8]{0,2,1:T(8,128)} %copy-done.18) | copy-start | bytes 12292
  154.5 46.1 %all-to-all-start.4 = ((bf16[16,184,128]{2,1,0:T(8,128)(2,1)}), bf16[16,184,128]{2,1,0:T(8,128)(2,1)S(1)}, u32[]{:S(2)}, u32[]{:S(2)}) async-start(bf16[16,184,128]{2,1,0:T(8,128)(2,1)} %pad_maximum_fusion.3), calls=%async_computation.4 | async-start | bytes 1507328 | tf_op jit(solution)/shard_map/all_to_all | solution.py:223
  167.2 3.3 %copy-start.22 = (bf16[32,4,1,128]{3,1,2,0:T(4,128)(2,1)S(1)}, bf16[32,4,1,128]{3,1,2,0:T(4,128)(2,1)}, u32[]{:S(2)}) copy-start(bf16[32,4,1,128]{3,1,2,0:T(4,128)(2,1)} %param.13) | copy-start | bytes 98308
  177.3 2.6 %copy-start.21 = (f32[32,16]{1,0:T(8,128)S(1)}, f32[32,16]{1,0:T(8,128)}, u32[]{:S(2)}) copy-start(f32[32,16]{1,0:T(8,128)} %copy.203) | copy-start | bytes 6148
  179.8 20.8 %copy-start.13 = (f32[128,16]{1,0:T(8,128)}, f32[128,16]{1,0:T(8,128)S(1)}, u32[]{:S(2)}) copy-start(f32[128,16]{1,0:T(8,128)S(1)} %gather_fusion.9) | copy-start | bytes 24580
  206.3 1.1 copy-start.15
  207.4 4.3 %copy-start.2 = (bf16[2,2064,128]{2,1,0:T(8,128)(2,1)S(1)}, bf16[2,2064,128]{2,1,0:T(8,128)(2,1)}, u32[]{:S(2)}) copy-start(bf16[2,2064,128]{2,1,0:T(8,128)(2,1)} %copy-done.1) | copy-start | bytes 3170308
  207.4 4.3 %copy-start.23 = (s32[128]{0:T(128)S(1)}, s32[128]{0:T(128)}, u32[]{:S(2)}) copy-start(s32[128]{0:T(128)} %get-tuple-element.262) | copy-start | bytes 1540
  208.9 2.9 %copy-start.26 = (s32[128]{0:T(128)S(1)}, s32[128]{0:T(128)}, u32[]{:S(2)}) copy-start(s32[128]{0:T(128)} %get-tuple-element.227) | copy-start | bytes 1540
  208.9 2.9 %copy-start.27 = (pred[128]{0:T(512)(128)(4,1)S(1)}, pred[128]{0:T(512)(128)(4,1)}, u32[]{:S(2)}) copy-start(pred[128]{0:T(512)(128)(4,1)} %broadcast_compare_fusion.3) | copy-start | bytes 388

commit v5 on v4

--- a/solution.py
+++ b/solution.py
@@ -20,17 +20,17 @@
 
 
 def row_kernel(
-    tiles_ref, span_ref, block_ref, line_ref,
-    q_ref, mine_ref, right_ref, far_keys_ref, far_rest_ref, left_ref,
-    out_ref, logs_ref, kv_ref, sems,
+    shift, stride, ids_ref, q_ref, mine_ref, right_ref, far_keys_ref, far_rest_ref, left_ref,
+    out_ref, logs_ref, kv_ref, sems, count_ref, block_ref, slot_ref, span_ref, start_ref,
 ):
     blocks, slots, width = logs_ref.shape
     per = out_ref.shape[1] // slots
-    length = kv_ref.shape[1] // 2
+    spans, both = kv_ref.shape[:2]
+    length = both // 2
     items = TILE // per
+    most = blocks * CAP
     scale = width ** (-0.5)
     each = mine_ref.shape[0]
-    both = 2 * length
     pieces = (
         (mine_ref.at[:, :both], kv_ref.at[:each]),
         (right_ref.at[:, :both], kv_ref.at[each : 2 * each]),
@@ -45,85 +45,107 @@
         copy.start()
     out_ref[...] = jnp.zeros_like(out_ref)
     logs_ref[...] = jnp.zeros_like(logs_ref)
+
+    for s in range(spans + 1):
+        count_ref[s] = 0
+
+    def one_block(b, carry):
+        for c in range(slots):
+            name = ids_ref[b * slots + c]
+            name = jnp.where(name < 0, spans, name)
+            place = jnp.minimum(count_ref[name], most - 1)
+            block_ref[name * most + place] = b
+            slot_ref[name * most + place] = c
+            count_ref[name] = place + 1
+        return carry
+
+    lax.fori_loop(0, blocks, one_block, 0)
+    tiles = jnp.int32(0)
+    for s in range(spans):
+        for t in range(-(-most // items)):
+            span_ref[tiles] = s
+            start_ref[tiles] = t * items
+            tiles = tiles + jnp.where(count_ref[s] > t * items, 1, 0)
     for copy in copies:
         copy.wait()
 
-    def one_tile(t, carry):
-        span = span_ref[t]
+    def spots_of(tile):
+        span = span_ref[tile]
+        start = start_ref[tile]
+        last = count_ref[span] - 1
         spots = []
         for u in range(items):
-            line = pl.multiple_of(line_ref[t * items + u] * per, per)
-            spots.append((block_ref[t * items + u], line, line_ref[t * items + u]))
-        q = jnp.concatenate([q_ref[b, pl.ds(line, per), :] for b, line, _ in spots], axis=0)
-        scores = dot(kv_ref[span, :length, :], q, ((1,), (1,)))
-        top = jnp.max(scores, axis=0, keepdims=True)
-        weights = jnp.exp2((scores - top) * (scale * LOG2E))
-        total = jnp.sum(weights, axis=0, keepdims=True)
-        mixed = dot(kv_ref[span, length : 2 * length, :], weights.astype(jnp.bfloat16), ((0,), (0,)))
-        mixed = (mixed * (1.0 / total)).T.astype(jnp.bfloat16)
-        logs = top * scale + jnp.log(total)
-        for u, (b, line, slot) in enumerate(spots):
-            out_ref[b, pl.ds(line, per), :] = mixed[u * per : (u + 1) * per, :]
-            logs_ref[b, pl.ds(slot, 1), 0:per] = logs[:, u * per : (u + 1) * per]
+            at = span * most + jnp.minimum(start + u, last)
+            spots.append((block_ref[at], slot_ref[at]))
+        return span, spots
+
+    def two_tiles(t, carry):
+        work = [spots_of(2 * t), spots_of(jnp.minimum(2 * t + 1, tiles - 1))]
+        scores = []
+        for span, spots in work:
+            q = jnp.concatenate(
+                [
+                    q_ref[b, pl.ds(pl.multiple_of(c * stride + shift, 16), per), :]
+                    for b, c in spots
+                ],
+                axis=0,
+            )
+            scores.append(dot(kv_ref[span, :length, :], q, ((1,), (1,))))
+        done = []
+        for (span, spots), score in zip(work, scores):
+            top = jnp.max(score, axis=0, keepdims=True)
+            weights = jnp.exp2((score - top) * (scale * LOG2E))
+            total = jnp.sum(weights, axis=0, keepdims=True)
+            mixed = dot(kv_ref[span, length:, :], weights.astype(jnp.bfloat16), ((0,), (0,)))
+            done.append((mixed * (1.0 / total), top * scale + jnp.log(total)))
+        for (span, spots), (mixed, logs) in zip(work, done):
+            mixed = mixed.T.astype(jnp.bfloat16)
+            for u, (b, c) in enumerate(spots):
+                line = pl.multiple_of(c * per, 16)
+                out_ref[b, pl.ds(line, per), :] = mixed[u * per : (u + 1) * per, :]
+                logs_ref[b, pl.ds(c, 1), 0:per] = logs[:, u * per : (u + 1) * per]
         return carry
 
-    lax.fori_loop(0, tiles_ref[0], one_tile, 0)
-
-
-def row_states(plan, q, spans, slots, per):
+    lax.fori_loop(0, (tiles + 1) // 2, two_tiles, 0)
+
+
+def row_states(ids, q, spans, slots, shift, per, stride):
     blocks, _, width = q.shape
     lines = slots * per
     each, length = spans[2].shape[:2]
+    count = NX * each
+    most = blocks * CAP
+    tiles = count * -(-most * per // TILE) + 1
     return pl.pallas_call(
-        row_kernel,
+        lambda *refs: row_kernel(shift, stride, *refs),
         grid_spec=pltpu.PrefetchScalarGridSpec(
-            num_scalar_prefetch=4,
+            num_scalar_prefetch=1,
             grid=(1,),
-            in_specs=[
-                pl.BlockSpec((blocks, lines, width), lambda i, *_: (0, 0, 0)),
-            ]
+            in_specs=[pl.BlockSpec((blocks, slots * stride, width), lambda i, *_: (0, 0, 0))]
             + [pl.BlockSpec(memory_space=pl.ANY)] * len(spans),
             out_specs=[
                 pl.BlockSpec((blocks, lines, width), lambda i, *_: (0, 0, 0)),
                 pl.BlockSpec((blocks, slots, width), lambda i, *_: (0, 0, 0)),
             ],
             scratch_shapes=[
-                pltpu.VMEM((NX * each, 2 * length, width), jnp.bfloat16),
+                pltpu.VMEM((count, 2 * length, width), jnp.bfloat16),
                 pltpu.SemaphoreType.DMA((len(spans),)),
+                pltpu.SMEM((count + 1,), jnp.int32),
+                pltpu.SMEM(((count + 1) * most,), jnp.int32),
+                pltpu.SMEM(((count + 1) * most,), jnp.int32),
+                pltpu.SMEM((tiles,), jnp.int32),
+                pltpu.SMEM((tiles,), jnp.int32),
             ],
         ),
         out_shape=[
             jax.ShapeDtypeStruct((blocks, lines, width), jnp.bfloat16),
             jax.ShapeDtypeStruct((blocks, slots, width), jnp.float32),
         ],
-        compiler_params=pltpu.CompilerParams(vmem_limit_bytes=48 * 1024 * 1024),
+        compiler_params=pltpu.CompilerParams(vmem_limit_bytes=24 * 1024 * 1024),
         cost_estimate=pl.CostEstimate(
             flops=q.size, bytes_accessed=4 * q.size, transcendentals=0
         ),
-    )(*plan, q, *spans)
-
-
-def tile_plan(spans, count, per):
-    blocks, slots = spans.shape
-    items = TILE // per
-    most = blocks * CAP
-    rounds = -(-most // items)
-    flat = spans.reshape(-1)
-    names = jnp.arange(count, dtype=jnp.int32)
-    equal = (flat[None, :] == names[:, None]).astype(jnp.int32)
-    place = jnp.cumsum(equal, axis=1) - 1
-    spot = jnp.arange(rounds * items, dtype=jnp.int32)
-    hit = (place[:, None, :] == spot[None, :, None]) & (equal[:, None, :] > 0)
-    lists = jnp.sum(jnp.where(hit, jnp.arange(flat.shape[0], dtype=jnp.int32), 0), axis=2)
-    amount = jnp.sum(equal, axis=1)
-    lists = jnp.where(spot[None, :] < amount[:, None], lists, lists[:, :1])
-    tiles = jnp.minimum((amount + items - 1) // items, rounds)
-    ends = jnp.cumsum(tiles)
-    each = jnp.arange(count * rounds, dtype=jnp.int32)
-    span = jnp.minimum(jnp.sum((ends[None, :] <= each[:, None]).astype(jnp.int32), axis=1), count - 1)
-    turn = jnp.clip(each - (ends - tiles)[span], 0, rounds - 1)
-    picked = lists.reshape(count * rounds, items)[span * rounds + turn].reshape(-1)
-    return ends[-1:], span, picked // slots, picked % slots
+    )(ids, q, *spans)
 
 
 def own_states(grouped, cache_keys, cache_values, fresh_keys, fresh_values, live_len):
@@ -225,12 +247,13 @@
         )
 
     def send(part, sender, span_at):
-        lines = sender.shape[0] // nz * part.shape[1]
+        room = span_at.shape[1]
+        lines = room * part.shape[1]
         outgoing = part[sender].reshape(nz, lines, width)
-        if span_at is not None:
-            extra = ((0, 0), (0, PAD - 1), (0, width - span_at.shape[1]))
-            outgoing = jnp.concatenate([outgoing, jnp.pad(span_at[:, None, :], extra)], axis=1)
-        return along_z(outgoing)
+        extra = ((0, 0), (0, PAD - 1), (0, width - room))
+        outgoing = jnp.concatenate([outgoing, jnp.pad(span_at[:, None, :], extra)], axis=1)
+        incoming = along_z(outgoing)
+        return incoming, incoming[:, lines, :room].astype(jnp.int32).reshape(-1)
 
     def packed(states, logs, note):
         lines = states.shape[1]
@@ -252,12 +275,9 @@
         return parts, logs, note
 
     sender, span_at, slot_ids = seats(0, ROOM)
-    arrived = []
-    for c in range(CHUNKS):
-        part = queries[:, c * per : (c + 1) * per].reshape(requests, rows, width)
-        arrived.append(send(part, sender, span_at if c == 0 else None))
-    spans_named = arrived[0][:, ROOM * rows, :ROOM].astype(jnp.int32)
-    plan = tile_plan(spans_named, in_row, rows)
+    all_rows = steps * heads
+    everything = queries.reshape(requests, all_rows, width)
+    arrived, ids = send(everything, sender, span_at)
 
     def along_x(array, by):
         pairs = [(z * NX + x, z * NX + (x + by) % NX) for z in range(nz) for x in range(NX)]
@@ -284,10 +304,8 @@
     results = []
     held = []
     for c in range(CHUNKS):
-        states, logs = row_states(plan, arrived[c], spans, ROOM, rows)
+        states, logs = row_states(ids, arrived, spans, ROOM, c * rows, rows, all_rows)
         states = packed(states, logs, lacking)
-        if c + 1 < CHUNKS:
-            states, arrived[c + 1] = lax.optimization_barrier((states, arrived[c + 1]))
         states = along_z(states)
         if c > 0:
             states, results[-1] = lax.optimization_barrier((states, results[-1]))
@@ -297,12 +315,9 @@
 
     def one_more_round(merged):
         room = in_row * CAP - ROOM
-        all_rows = steps * heads
         sender, span_at, more_ids = seats(ROOM, room)
-        incoming = send(queries.reshape(requests, all_rows, width), sender, span_at)
-        named_more = incoming[:, room * all_rows, :room].astype(jnp.int32)
-        plan = tile_plan(named_more, in_row, all_rows)
-        states, logs = row_states(plan, incoming, spans, room, all_rows)
+        incoming, ids = send(everything, sender, span_at)
+        states, logs = row_states(ids, incoming, spans, room, 0, all_rows, all_rows)
         states = along_z(packed(states, logs, lacking))
         more, more_logs, _ = opened(states, more_ids, all_rows)
         late = (rank >= ROOM).reshape(requests, depth, 1)

time: 231 us -> 226 us (0.978)
  waiting for transfers between devices: 68.3 us -> 83.3 us
  starting transfers between devices: 65.9 us -> 53.1 us
  local copies, waits for them, and re-layouts: 28.9 us -> 25.2 us
    all_to_all x4 -> x3, starting transfers between devices: 52.4 us -> 39.6 us  [along_z(): lax.all_to_all(array, 'req', split_axis=0, concat_axis=0, tiled=True, axi...]
    all_to_all x4 -> x3, waiting for transfers between devices: 48.5 us -> 59.5 us  [along_z(): lax.all_to_all(array, 'req', split_axis=0, concat_axis=0, tiled=True, axi...]
    ppermute x4, waiting for transfers between devices: 19.7 us -> 23.8 us  [along_x(): return lax.ppermute(array, 'req', pairs)]
  transfers between devices with their start and end apart: 8 -> 7, of which waited for: 4 -> 5; matrix products, arithmetic and copies ran while one was open for 16% -> 10% of each run, Pallas kernels for 9% -> 4%
where the time goes in v5:
time: 226 us; the launch traced here: 225 us
  waiting for transfers between devices  83.3 us (37%)
  starting transfers between devices  53.1 us (23%)
  local copies, waits for them, and re-layouts  25.2 us (11%)
  other arithmetic  19.4 us (9%)
  Pallas kernels  18.4 us (8%)
  blocking collectives  16.1 us (7%)
  matrix products  5.49 us (2%)
  between operations  3.68 us (2%)
    all_to_all x3, waiting for transfers between devices, along_z(): lax.all_to_all(array, 'req', split_axis=0, concat_axis=0, tiled=True, axi...  59.5 us
    all_to_all x3, starting transfers between devices, along_z(): lax.all_to_all(array, 'req', split_axis=0, concat_axis=0, tiled=True, axi...  39.6 us
    ppermute x4, waiting for transfers between devices, along_x(): return lax.ppermute(array, 'req', pairs)  23.8 us
    pallas_call x2, Pallas kernels, row_states(): pl.pallas_call(lambda *refs: row_kernel(shift, stride, *refs), grid_spec=...  18.4 us
    all_to_all x1, blocking collectives, local(): return lax.all_to_all(merged, 'kv', split_axis=1, concat_axis=3, tiled=True)  16.1 us
    ppermute x4, starting transfers between devices, along_x(): return lax.ppermute(array, 'req', pairs)  13.5 us
  transfers between devices with their start and end apart: 7, of which 5 were waited for; matrix products, arithmetic and copies ran while one was open for 10% of the time, Pallas kernels for 4%

profile of v5, /device:TPU:1, one launch (start us, length us, event | category | flops | bytes accessed | tf_op | source)
XLA Modules:
  0.0 225.0 jit_solution(3087335432992427860)
XLA Ops:
  2.0 1.8 gather_fusion.3
  3.9 1.2 fusion.20
  5.1 15.9 %all-to-all-start.2 = ((bf16[16,360,128]{2,1,0:T(8,128)(2,1)}), bf16[16,360,128]{2,1,0:T(8,128)(2,1)S(1)}, u32[]{:S(2)}, u32[]{:S(2)}) async-start(bf16[16,360,128]{2,1,0:T(8,128)(2,1)} %fusion.20), calls=%async_computation.2 | async-start | bytes 2949120 | tf_op jit(solution)/shard_map/all_to_all | solution.py:245
  22.3 1.4 maximum_maximum_fusion.refs_2_
  23.7 4.4 %collective-permute-start = (bf16[2,2064,128]{2,1,0:T(8,128)(2,1)S(1)}, bf16[2,2064,128]{2,1,0:T(8,128)(2,1)S(1)}, u32[]{:S(2)}, u32[]{:S(2)}) collective-permute-start(bf16[2,2064,128]{2,1,0:T(8,128)(2,1)S(1)} %maximum_maximum_fusion.refs_2_), channel_id=1, source_target_pairs={{0,3},{1,0},{2,1},{3,2},{4,7},{5,4},{6,5},{7,6},{8,11},{9,8},{10,9... | collective-permute-start | bytes 3170312 | tf_op jit(solution)/shard_map/ppermute | solution.py:284
  28.1 1.9 collective-permute-start.1
  30.0 19.7 %collective-permute-done.refs_3_ = bf16[2,2064,128]{2,1,0:T(8,128)(2,1)S(1)} collective-permute-done((bf16[2,2064,128]{2,1,0:T(8,128)(2,1)S(1)}, bf16[2,2064,128]{2,1,0:T(8,128)(2,1)S(1)}, u32[]{:S(2)}, u32[]{:S(2)}) %collective-permute-start) | collective-permute-done | bytes 1056800 | tf_op jit(solution)/shard_map/ppermute | solution.py:284
  50.6 5.3 %collective-permute-start.3 = (bf16[2,1040,128]{2,1,0:T(8,128)(2,1)}, bf16[2,1040,128]{2,1,0:T(8,128)(2,1)S(1)}, u32[]{:S(2)}, u32[]{:S(2)}) collective-permute-start(bf16[2,1040,128]{2,1,0:T(8,128)(2,1)} %slice.165), channel_id=1, source_target_pairs={{0,3},{1,0},{2,1},{3,2},{4,7},{5,4},{6,5},{7,6},{8,11},{9,8},{10,9... | collective-permute-start | bytes 1597448 | tf_op jit(solution)/shard_map/ppermute | solution.py:284
  56.9 1.9 collective-permute-start.2
  61.7 4.1 %collective-permute-done.3.refs_5_ = bf16[2,1040,128]{2,1,0:T(8,128)(2,1)S(1)} collective-permute-done((bf16[2,1040,128]{2,1,0:T(8,128)(2,1)}, bf16[2,1040,128]{2,1,0:T(8,128)(2,1)S(1)}, u32[]{:S(2)}, u32[]{:S(2)}) %collective-permute-start.3) | collective-permute-done | bytes 532512 | tf_op jit(solution)/shard_map/ppermute | solution.py:284
  67.0 18.8 %all-to-all-done.2.refs_1_ = bf16[16,360,128]{2,1,0:T(8,128)(2,1)S(1)} async-done(((bf16[16,360,128]{2,1,0:T(8,128)(2,1)}), bf16[16,360,128]{2,1,0:T(8,128)(2,1)S(1)}, u32[]{:S(2)}, u32[]{:S(2)}) %all-to-all-start.2) | async-done | bytes 1474592 | tf_op jit(solution)/shard_map/all_to_all | solution.py:245
  85.9 9.2 %shard_map.92 = (bf16[16,176,128]{2,1,0:T(8,128)(2,1)S(1)}, f32[16,11,128]{2,1,0:T(8,128)S(1)}) custom-call(s32[176]{0:T(256)S(1)} %reshape.593.refs_0_, bf16[16,360,128]{2,1,0:T(8,128)(2,1)S(1)} %all-to-all-done.2.refs_1_, bf16[2,2064,128]{2,1,0:T(8,128)(2,1)} %copy-done.3, bf16[2,2064,128]{2,1,0:T(8,128)(2,1)} %copy-done.5, ...), custom_call_target="tpu_custom_call" | custom-call | flops 737280 | bytes 2949120 | tf_op jit(solution)/shard_map/pallas_call | solution.py:119
  96.3 11.7 %all-to-all-start.4 = ((bf16[16,184,128]{2,1,0:T(8,128)(2,1)}), bf16[16,184,128]{2,1,0:T(8,128)(2,1)}, u32[]{:S(2)}, u32[]{:S(2)}) async-start(bf16[16,184,128]{2,1,0:T(8,128)(2,1)} %pad_maximum_fusion.3), calls=%async_computation.4 | async-start | bytes 1507328 | tf_op jit(solution)/shard_map/all_to_all | solution.py:245
  108.1 2.0 fusion.85
  110.3 1.5 fusion.84
  112.6 9.2 %shard_map.91 = (bf16[16,176,128]{2,1,0:T(8,128)(2,1)S(1)}, f32[16,11,128]{2,1,0:T(8,128)S(1)}) custom-call(s32[176]{0:T(256)S(1)} %reshape.593.refs_0_, bf16[16,360,128]{2,1,0:T(8,128)(2,1)S(1)} %all-to-all-done.2.refs_1_, bf16[2,2064,128]{2,1,0:T(8,128)(2,1)} %copy-done.3, bf16[2,2064,128]{2,1,0:T(8,128)(2,1)} %copy-done.5, ...), custom_call_target="tpu_custom_call" | custom-call | flops 737280 | bytes 2949120 | tf_op jit(solution)/shard_map/pallas_call | solution.py:119
  123.0 18.4 %all-to-all-done.4 = bf16[16,184,128]{2,1,0:T(8,128)(2,1)} async-done(((bf16[16,184,128]{2,1,0:T(8,128)(2,1)}), bf16[16,184,128]{2,1,0:T(8,128)(2,1)}, u32[]{:S(2)}, u32[]{:S(2)}) %all-to-all-start.4) | async-done | bytes 753696 | tf_op jit(solution)/shard_map/all_to_all | solution.py:245
  141.4 12.1 %all-to-all-start.3 = ((bf16[16,184,128]{2,1,0:T(8,128)(2,1)}), bf16[16,184,128]{2,1,0:T(8,128)(2,1)S(1)}, u32[]{:S(2)}, u32[]{:S(2)}) async-start(bf16[16,184,128]{2,1,0:T(8,128)(2,1)} %pad_maximum_fusion.2), calls=%async_computation.3 | async-start | bytes 1507328 | tf_op jit(solution)/shard_map/all_to_all | solution.py:245
  155.6 1.7 fusion.28
  158.3 2.0 slice.174
  160.3 1.8 gather_fusion.5
  164.5 22.3 %all-to-all-done.3 = bf16[16,184,128]{2,1,0:T(8,128)(2,1)S(1)} async-done(((bf16[16,184,128]{2,1,0:T(8,128)(2,1)}), bf16[16,184,128]{2,1,0:T(8,128)(2,1)S(1)}, u32[]{:S(2)}, u32[]{:S(2)}) %all-to-all-start.3) | async-done | bytes 753696 | tf_op jit(solution)/shard_map/all_to_all | solution.py:245
  189.1 1.8 gather_fusion.7
  191.6 1.2 gather_fusion.6
  192.9 1.5 reduce_max.86
  195.9 2.1 fusion.81
  198.0 1.4 copy.170
  199.4 1.3 bitcast_add_fusion.4
  200.7 1.4 copy.171
  202.1 1.4 copy.169
  203.5 1.2 multiply_reduce_fusion.2
  208.0 16.1 %all_to_all.42 = bf16[4,8,4,1024]{3,2,0,1:T(4,128)(2,1)S(1)} all-to-all(bf16[4,8,4,1024]{3,2,0,1:T(4,128)(2,1)S(1)} %copy.173), channel_id=1, replica_groups=mesh['kv'=8,'req'=64] {'kv'}, dimensions={1} | all-to-all | bytes 524288 | tf_op jit(solution)/shard_map/all_to_all | solution.py:336
  (134 shorter events, 23.5 us)
Async XLA Ops:
  0.0 110.3 %copy-start = (bf16[32,128,1,128]{3,1,2,0:T(8,128)(2,1)S(1)}, bf16[32,128,1,128]{3,1,2,0:T(8,128)(2,1)}, u32[]{:S(2)}) copy-start(bf16[32,128,1,128]{3,1,2,0:T(8,128)(2,1)} %param.14) | copy-start | bytes 3145732
  1.0 153.7 %copy-start.32 = (s32[128]{0:T(128)}, s32[128]{0:T(128)S(1)}, u32[]{:S(2)}) copy-start(s32[128]{0:T(128)S(1)} %reshape.569) | copy-start | bytes 1540
  1.7 106.2 %copy-start.34 = (s32[128]{0:T(128)}, s32[128]{0:T(128)S(1)}, u32[]{:S(2)}) copy-start(s32[128]{0:T(128)S(1)} %convert_reduce_fusion) | copy-start | bytes 1540
  5.1 17.2 %copy-start.21 = (bf16[2,1024,1,128]{3,1,2,0:T(8,128)(2,1)S(1)}, bf16[2,1024,1,128]{3,1,2,0:T(8,128)(2,1)}, u32[]{:S(2)}) copy-start(bf16[2,1024,1,128]{3,1,2,0:T(8,128)(2,1)} %param.19) | copy-start | bytes 1572868
  5.1 80.7 %all-to-all-start.2 = ((bf16[16,360,128]{2,1,0:T(8,128)(2,1)}), bf16[16,360,128]{2,1,0:T(8,128)(2,1)S(1)}, u32[]{:S(2)}, u32[]{:S(2)}) async-start(bf16[16,360,128]{2,1,0:T(8,128)(2,1)} %fusion.20), calls=%async_computation.2 | async-start | bytes 2949120 | tf_op jit(solution)/shard_map/all_to_all | solution.py:245
  23.7 4.4 %copy-start.3 = (bf16[2,2064,128]{2,1,0:T(8,128)(2,1)}, bf16[2,2064,128]{2,1,0:T(8,128)(2,1)S(1)}, u32[]{:S(2)}) copy-start(bf16[2,2064,128]{2,1,0:T(8,128)(2,1)S(1)} %maximum_maximum_fusion.refs_2_) | copy-start | bytes 3170308
  23.7 26.1 %collective-permute-start = (bf16[2,2064,128]{2,1,0:T(8,128)(2,1)S(1)}, bf16[2,2064,128]{2,1,0:T(8,128)(2,1)S(1)}, u32[]{:S(2)}, u32[]{:S(2)}) collective-permute-start(bf16[2,2064,128]{2,1,0:T(8,128)(2,1)S(1)} %maximum_maximum_fusion.refs_2_), channel_id=1, source_target_pairs={{0,3},{1,0},{2,1},{3,2},{4,7},{5,4},{6,5},{7,6},{8,11},{9,8},{10,9... | collective-permute-start | bytes 3170312 | tf_op jit(solution)/shard_map/ppermute | solution.py:284
  28.1 27.9 %collective-permute-start.1 = (bf16[2,2064,128]{2,1,0:T(8,128)(2,1)S(1)}, bf16[2,2064,128]{2,1,0:T(8,128)(2,1)S(1)}, u32[]{:S(2)}, u32[]{:S(2)}) collective-permute-start(bf16[2,2064,128]{2,1,0:T(8,128)(2,1)S(1)} %maximum_maximum_fusion.refs_2_), channel_id=1, source_target_pairs={{0,1},{1,2},{2,3},{3,0},{4,5},{5,6},{6,7},{7,4},{8,9},{9,10},{10,1... | collective-permute-start | bytes 3170312 | tf_op jit(solution)/shard_map/ppermute | solution.py:284
  49.7 9.6 %copy-start.5 = (bf16[2,2064,128]{2,1,0:T(8,128)(2,1)}, bf16[2,2064,128]{2,1,0:T(8,128)(2,1)S(1)}, u32[]{:S(2)}) copy-start(bf16[2,2064,128]{2,1,0:T(8,128)(2,1)S(1)} %collective-permute-done.refs_3_) | copy-start | bytes 3170308
  50.6 15.1 %collective-permute-start.3 = (bf16[2,1040,128]{2,1,0:T(8,128)(2,1)}, bf16[2,1040,128]{2,1,0:T(8,128)(2,1)S(1)}, u32[]{:S(2)}, u32[]{:S(2)}) collective-permute-start(bf16[2,1040,128]{2,1,0:T(8,128)(2,1)} %slice.165), channel_id=1, source_target_pairs={{0,3},{1,0},{2,1},{3,2},{4,7},{5,4},{6,5},{7,6},{8,11},{9,8},{10,9... | collective-permute-start | bytes 1597448 | tf_op jit(solution)/shard_map/ppermute | solution.py:284
  56.0 3.9 %copy-start.6 = (bf16[2,2064,128]{2,1,0:T(8,128)(2,1)}, bf16[2,2064,128]{2,1,0:T(8,128)(2,1)S(1)}, u32[]{:S(2)}) copy-start(bf16[2,2064,128]{2,1,0:T(8,128)(2,1)S(1)} %collective-permute-done.1.refs_6_) | copy-start | bytes 3170308
  56.9 29.1 %collective-permute-start.2 = (bf16[2,1024,128]{2,1,0:T(8,128)(2,1)}, bf16[2,1024,128]{2,1,0:T(8,128)(2,1)}, u32[]{:S(2)}, u32[]{:S(2)}) collective-permute-start(bf16[2,1024,128]{2,1,0:T(8,128)(2,1)} %slice.164), channel_id=1, source_target_pairs={{0,1},{1,2},{2,3},{3,0},{4,5},{5,6},{6,7},{7,4},{8,9},{9,10},{10,1... | collective-permute-start | bytes 1572872 | tf_op jit(solution)/shard_map/ppermute | solution.py:284
  65.8 20.0 %copy-start.7 = (bf16[2,1040,128]{2,1,0:T(8,128)(2,1)}, bf16[2,1040,128]{2,1,0:T(8,128)(2,1)S(1)}, u32[]{:S(2)}) copy-start(bf16[2,1040,128]{2,1,0:T(8,128)(2,1)S(1)} %collective-permute-done.3.refs_5_) | copy-start | bytes 1597444
  95.4 12.7 %copy-start.37 = (bf16[32,4,1,128]{3,1,2,0:T(4,128)(2,1)S(1)}, bf16[32,4,1,128]{3,1,2,0:T(4,128)(2,1)}, u32[]{:S(2)}) copy-start(bf16[32,4,1,128]{3,1,2,0:T(4,128)(2,1)} %param.12) | copy-start | bytes 98308
  96.3 11.8 %copy-start.1 = (bf16[32,4,8,128]{3,2,1,0:T(8,128)(2,1)S(1)}, bf16[32,4,8,128]{3,2,1,0:T(8,128)(2,1)}, u32[]{:S(2)}) copy-start(bf16[32,4,8,128]{3,2,1,0:T(8,128)(2,1)} %param.11) | copy-start | bytes 786436
  96.3 13.9 %copy-start.36 = (s32[32]{0:T(128)S(1)}, s32[32]{0:T(128)}, u32[]{:S(2)}) copy-start(s32[32]{0:T(128)} %param.16) | copy-start | bytes 388
  96.3 45.0 %all-to-all-start.4 = ((bf16[16,184,128]{2,1,0:T(8,128)(2,1)}), bf16[16,184,128]{2,1,0:T(8,128)(2,1)}, u32[]{:S(2)}, u32[]{:S(2)}) async-start(bf16[16,184,128]{2,1,0:T(8,128)(2,1)} %pad_maximum_fusion.3), calls=%async_computation.4 | async-start | bytes 1507328 | tf_op jit(solution)/shard_map/all_to_all | solution.py:245
  122.0 31.4 %copy-start.18 = (f32[32,4,1,8,4]{3,4,1,0,2:T(4,128)S(1)}, f32[32,4,1,8,4]{3,4,1,0,2:T(4,128)}, u32[]{:S(2)}) copy-start(f32[32,4,1,8,4]{3,4,1,0,2:T(4,128)} %get-tuple-element.226) | copy-start | bytes 49156
  122.0 31.4 %copy-start.20 = (f32[32,4,8]{2,1,0:T(4,128)S(1)}, f32[32,4,8]{2,1,0:T(4,128)}, u32[]{:S(2)}) copy-start(f32[32,4,8]{2,1,0:T(4,128)} %copy.157) | copy-start | bytes 12292
  122.0 31.9 %copy-start.12 = (f32[32,4,1,8,128]{4,3,1,0,2:T(8,128)S(1)}, f32[32,4,1,8,128]{4,3,1,0,2:T(8,128)}, u32[]{:S(2)}) copy-start(f32[32,4,1,8,128]{4,3,1,0,2:T(8,128)} %get-tuple-element.224) | copy-start | bytes 1572868
  123.0 32.3 %copy-start.19 = (f32[32,4,1,8,4]{3,4,1,0,2:T(4,128)S(1)}, f32[32,4,1,8,4]{3,4,1,0,2:T(4,128)}, u32[]{:S(2)}) copy-start(f32[32,4,1,8,4]{3,4,1,0,2:T(4,128)} %get-tuple-element.226) | copy-start | bytes 49156
  123.0 32.3 %copy-start.31 = (bf16[32,4,1,128]{3,1,2,0:T(4,128)(2,1)S(1)}, bf16[32,4,1,128]{3,1,2,0:T(4,128)(2,1)}, u32[]{:S(2)}) copy-start(bf16[32,4,1,128]{3,1,2,0:T(4,128)(2,1)} %param.13) | copy-start | bytes 98308
  141.4 45.4 %all-to-all-start.3 = ((bf16[16,184,128]{2,1,0:T(8,128)(2,1)}), bf16[16,184,128]{2,1,0:T(8,128)(2,1)S(1)}, u32[]{:S(2)}, u32[]{:S(2)}) async-start(bf16[16,184,128]{2,1,0:T(8,128)(2,1)} %pad_maximum_fusion.2), calls=%async_computation.3 | async-start | bytes 1507328 | tf_op jit(solution)/shard_map/all_to_all | solution.py:245
  154.5 8.6 %copy-start.23 = (f32[32,4,8]{0,2,1:T(8,128)}, f32[32,4,8]{0,2,1:T(8,128)S(1)}, u32[]{:S(2)}) copy-start(f32[32,4,8]{0,2,1:T(8,128)S(1)} %get-tuple-element.197) | copy-start | bytes 12292
  157.3 6.3 %copy-start.13 = (f32[32,4,8,128]{3,2,1,0:T(8,128)}, f32[32,4,8,128]{3,2,1,0:T(8,128)S(1)}, u32[]{:S(2)}) copy-start(f32[32,4,8,128]{3,2,1,0:T(8,128)S(1)} %fusion.28) | copy-start | bytes 1572868
  162.8 24.9 %copy-start.15 = (f32[128,16]{1,0:T(8,128)}, f32[128,16]{1,0:T(8,128)S(1)}, u32[]{:S(2)}) copy-start(f32[128,16]{1,0:T(8,128)S(1)} %gather_fusion.4) | copy-start | bytes 24580
  191.6 15.0 %copy-start.2 = (bf16[32,4,8,128]{3,2,1,0:T(8,128)(2,1)S(1)}, bf16[32,4,8,128]{3,2,1,0:T(8,128)(2,1)}, u32[]{:S(2)}) copy-start(bf16[32,4,8,128]{3,2,1,0:T(8,128)(2,1)} %param.11) | copy-start | bytes 786436
  191.6 15.0 %copy-start.4 = (bf16[2,2064,128]{2,1,0:T(8,128)(2,1)S(1)}, bf16[2,2064,128]{2,1,0:T(8,128)(2,1)}, u32[]{:S(2)}) copy-start(bf16[2,2064,128]{2,1,0:T(8,128)(2,1)} %copy-done.3) | copy-start | bytes 3170308
  192.9 13.0 %copy-start.22 = (bf16[32,2,8,128]{3,2,1,0:T(8,128)(2,1)S(1)}, bf16[32,2,8,128]{3,2,1,0:T(8,128)(2,1)}, u32[]{:S(2)}) copy-start(bf16[32,2,8,128]{3,2,1,0:T(8,128)(2,1)} %fusion.40) | copy-start | bytes 393220
  200.7 5.9 %copy-start.33 = (s32[128]{0:T(128)S(1)}, s32[128]{0:T(128)}, u32[]{:S(2)}) copy-start(s32[128]{0:T(128)} %copy-done.32) | copy-start | bytes 1540
  200.7 5.9 %copy-start.35 = (s32[128]{0:T(128)S(1)}, s32[128]{0:T(128)}, u32[]{:S(2)}) copy-start(s32[128]{0:T(128)} %copy-done.34) | copy-start | bytes 1540

commit v6 on v5

--- a/solution.py
+++ b/solution.py
@@ -293,27 +293,34 @@
     lacking = jnp.maximum(lacking, far_rest[0, -1, 0])
     spans = (mine, right, far_keys, far_rest, left)
 
-    kv_local = new_keys.shape[2]
-    grouped = queries.reshape(requests, steps, kv_local, heads // kv_local, width)
-    own_part, own_log = own_states(
-        grouped, suffix_keys, suffix_values, new_keys, new_values, suffix_len
-    )
-    own_part = own_part.reshape(requests, steps, heads, width)
-    own_log = own_log.reshape(requests, steps, heads)
-
+    def private():
+        kv_local = new_keys.shape[2]
+        grouped = queries.reshape(requests, steps, kv_local, heads // kv_local, width)
+        own_part, own_log = own_states(
+            grouped, suffix_keys, suffix_values, new_keys, new_values, suffix_len
+        )
+        own_part = own_part.reshape(requests, steps, heads, width)
+        return own_part, own_log.reshape(requests, steps, heads)
+
+    own_part, own_log = private()
     results = []
     held = []
     for c in range(CHUNKS):
         states, logs = row_states(ids, arrived, spans, ROOM, c * rows, rows, all_rows)
         states = packed(states, logs, lacking)
         states = along_z(states)
+        held.append(states)
         if c > 0:
             states, results[-1] = lax.optimization_barrier((states, results[-1]))
         parts, logs, note = opened(states, slot_ids, rows)
-        held.append((parts, logs))
         results.append(merge_own(parts, logs, own_part, own_log, c, per))
 
-    def one_more_round(merged):
+    def along_kv(merged):
+        kv_count = lax.axis_size("kv")
+        merged = merged.reshape(requests // kv_count, kv_count, steps, heads * width)
+        return lax.all_to_all(merged, "kv", split_axis=1, concat_axis=3, tiled=True)
+
+    def one_more_round(attended):
         room = in_row * CAP - ROOM
         sender, span_at, more_ids = seats(ROOM, room)
         incoming, ids = send(everything, sender, span_at)
@@ -322,18 +329,17 @@
         more, more_logs, _ = opened(states, more_ids, all_rows)
         late = (rank >= ROOM).reshape(requests, depth, 1)
         results = []
-        for c, (parts, logs) in enumerate(held):
+        own_part, own_log = private()
+        for c, states in enumerate(held):
+            parts, logs, _ = opened(states, slot_ids, rows)
             cut = slice(c * rows, (c + 1) * rows)
             parts = jnp.where(late[..., None], more[:, :, cut], parts)
             logs = jnp.where(late, more_logs[:, :, cut], logs)
             results.append(merge_own(parts, logs, own_part, own_log, c, per))
-        return jnp.concatenate(results, axis=1)
-
-    merged = jnp.concatenate(results, axis=1)
-    merged = lax.cond(note > 0.0, one_more_round, lambda m: m, merged)
-    kv_count = lax.axis_size("kv")
-    merged = merged.reshape(requests // kv_count, kv_count, steps, heads * width)
-    return lax.all_to_all(merged, "kv", split_axis=1, concat_axis=3, tiled=True)
+        return along_kv(jnp.concatenate(results, axis=1))
+
+    attended = along_kv(jnp.concatenate(results, axis=1))
+    return lax.cond(note > 0.0, one_more_round, lambda a: a, attended)
 
 
 def solution(mesh):

time: 226 us -> 210 us (0.929)
  blocking collectives: 16.1 us -> 0 us
  starting transfers between devices: 53.1 us -> 64.2 us
  local copies, waits for them, and re-layouts: 25.2 us -> 14.2 us
  waiting for transfers between devices: 83.3 us -> 90.7 us
  other arithmetic: 19.4 us -> 12.4 us
  Pallas kernels: 18.4 us -> 15.3 us
  matrix products: 5.49 us -> 8.26 us
    all_to_all x1 -> x0, blocking collectives: 16.1 us -> none  [local(): return lax.all_to_all(merged, 'kv', split_axis=1, concat_axis=3, tiled=True)]
    all_to_all x0 -> x1, starting transfers between devices: none -> 9.85 us  [along_kv(): return lax.all_to_all(merged, 'kv', split_axis=1, concat_axis=3, tiled=True)]
    all_to_all x0 -> x1, waiting for transfers between devices: none -> 5.14 us  [along_kv(): return lax.all_to_all(merged, 'kv', split_axis=1, concat_axis=3, tiled=True)]
    pallas_call x2, Pallas kernels: 18.4 us -> 15.3 us  [row_states(): pl.pallas_call(lambda *refs: row_kernel(shift, stride, *refs), grid_spec=...]
    slice x2, local copies, waits for them, and re-layouts: 2.96 us -> 0.1 us  [opened(): parts = states[:, :lines].reshape(-1, rows, width)[slot_ids]]
  transfers between devices with their start and end apart: 7 -> 8, of which waited for: 5 -> 6; matrix products, arithmetic and copies ran while one was open for 10% -> 11% of each run, Pallas kernels for 4% -> 4%
where the time goes in v6:
time: 210 us; the launch traced here: 209 us
  waiting for transfers between devices  90.7 us (43%)
  starting transfers between devices  64.2 us (31%)
  Pallas kernels  15.3 us (7%)
  local copies, waits for them, and re-layouts  14.2 us (7%)
  other arithmetic  12.4 us (6%)
  matrix products  8.26 us (4%)
  between operations  3.75 us (2%)
    all_to_all x3, waiting for transfers between devices, along_z(): lax.all_to_all(array, 'req', split_axis=0, concat_axis=0, tiled=True, axi...  61.7 us
    all_to_all x3, starting transfers between devices, along_z(): lax.all_to_all(array, 'req', split_axis=0, concat_axis=0, tiled=True, axi...  40.8 us
    ppermute x4, waiting for transfers between devices, along_x(): return lax.ppermute(array, 'req', pairs)  23.9 us
    pallas_call x2, Pallas kernels, row_states(): pl.pallas_call(lambda *refs: row_kernel(shift, stride, *refs), grid_spec=...  15.3 us
    ppermute x4, starting transfers between devices, along_x(): return lax.ppermute(array, 'req', pairs)  13.5 us
    all_to_all x1, starting transfers between devices, along_kv(): return lax.all_to_all(merged, 'kv', split_axis=1, concat_axis=3, tiled=True)  9.85 us
    all_to_all x1, waiting for transfers between devices, along_kv(): return lax.all_to_all(merged, 'kv', split_axis=1, concat_axis=3, tiled=True)  5.14 us
  transfers between devices with their start and end apart: 8, of which 6 were waited for; matrix products, arithmetic and copies ran while one was open for 11% of the time, Pallas kernels for 4%

profile of v6, /device:TPU:1, one launch (start us, length us, event | category | flops | bytes accessed | tf_op | source)
XLA Modules:
  0.0 208.9 jit_solution(7300492867784028149)
XLA Ops:
  0.0 0.8 copy.200
  2.0 1.8 gather_fusion.7
  3.8 1.3 fusion.45
  5.1 15.9 %all-to-all-start.3 = ((bf16[16,360,128]{2,1,0:T(8,128)(2,1)}), bf16[16,360,128]{2,1,0:T(8,128)(2,1)S(1)}, u32[]{:S(2)}, u32[]{:S(2)}) async-start(bf16[16,360,128]{2,1,0:T(8,128)(2,1)} %fusion.45), calls=%async_computation.3 | async-start | bytes 2949120 | tf_op jit(solution)/shard_map/all_to_all | solution.py:245
  22.2 1.4 maximum_maximum_fusion.refs_2_
  23.6 4.4 %collective-permute-start = (bf16[2,2064,128]{2,1,0:T(8,128)(2,1)S(1)}, bf16[2,2064,128]{2,1,0:T(8,128)(2,1)S(1)}, u32[]{:S(2)}, u32[]{:S(2)}) collective-permute-start(bf16[2,2064,128]{2,1,0:T(8,128)(2,1)S(1)} %maximum_maximum_fusion.refs_2_), channel_id=1, source_target_pairs={{0,3},{1,0},{2,1},{3,2},{4,7},{5,4},{6,5},{7,6},{8,11},{9,8},{10,9... | collective-permute-start | bytes 3170312 | tf_op jit(solution)/shard_map/ppermute | solution.py:284
  28.0 1.9 collective-permute-start.1
  30.0 19.7 %collective-permute-done.refs_3_ = bf16[2,2064,128]{2,1,0:T(8,128)(2,1)S(1)} collective-permute-done((bf16[2,2064,128]{2,1,0:T(8,128)(2,1)S(1)}, bf16[2,2064,128]{2,1,0:T(8,128)(2,1)S(1)}, u32[]{:S(2)}, u32[]{:S(2)}) %collective-permute-start) | collective-permute-done | bytes 1056800 | tf_op jit(solution)/shard_map/ppermute | solution.py:284
  49.7 0.9 slice.213
  50.6 5.3 %collective-permute-start.3 = (bf16[2,1040,128]{2,1,0:T(8,128)(2,1)}, bf16[2,1040,128]{2,1,0:T(8,128)(2,1)S(1)}, u32[]{:S(2)}, u32[]{:S(2)}) collective-permute-start(bf16[2,1040,128]{2,1,0:T(8,128)(2,1)} %slice.213), channel_id=1, source_target_pairs={{0,3},{1,0},{2,1},{3,2},{4,7},{5,4},{6,5},{7,6},{8,11},{9,8},{10,9... | collective-permute-start | bytes 1597448 | tf_op jit(solution)/shard_map/ppermute | solution.py:284
  55.9 0.9 slice.212
  56.9 1.9 collective-permute-start.2
  61.6 4.1 %collective-permute-done.3.refs_5_ = bf16[2,1040,128]{2,1,0:T(8,128)(2,1)S(1)} collective-permute-done((bf16[2,1040,128]{2,1,0:T(8,128)(2,1)}, bf16[2,1040,128]{2,1,0:T(8,128)(2,1)S(1)}, u32[]{:S(2)}, u32[]{:S(2)}) %collective-permute-start.3) | collective-permute-done | bytes 532512 | tf_op jit(solution)/shard_map/ppermute | solution.py:284
  67.0 18.8 %all-to-all-done.3.refs_1_ = bf16[16,360,128]{2,1,0:T(8,128)(2,1)S(1)} async-done(((bf16[16,360,128]{2,1,0:T(8,128)(2,1)}), bf16[16,360,128]{2,1,0:T(8,128)(2,1)S(1)}, u32[]{:S(2)}, u32[]{:S(2)}) %all-to-all-start.3) | async-done | bytes 1474592 | tf_op jit(solution)/shard_map/all_to_all | solution.py:245
  85.9 7.8 %shard_map.94 = (bf16[16,176,128]{2,1,0:T(8,128)(2,1)S(1)}, f32[16,11,128]{2,1,0:T(8,128)S(1)}) custom-call(s32[176]{0:T(256)S(1)} %reshape.724.refs_0_, bf16[16,360,128]{2,1,0:T(8,128)(2,1)S(1)} %all-to-all-done.3.refs_1_, bf16[2,2064,128]{2,1,0:T(8,128)(2,1)S(1)} %maximum_maximum_fusion.refs_2_, bf16[2,2064,128]{2,1,0:T(8,128)(2,1)} %copy-done.4, ...), custom_call_target="tpu_custom_call" | custom-call | flops 737280 | bytes 2949120 | tf_op jit(solution)/shard_map/pallas_call | solution.py:119
  93.9 0.9 pad_maximum_fusion.3
  94.8 12.9 %all-to-all-start.5 = ((bf16[16,184,128]{2,1,0:T(8,128)(2,1)}), bf16[16,184,128]{2,1,0:T(8,128)(2,1)S(1)}, u32[]{:S(2)}, u32[]{:S(2)}) async-start(bf16[16,184,128]{2,1,0:T(8,128)(2,1)} %pad_maximum_fusion.3), calls=%async_computation.5 | async-start | bytes 1507328 | tf_op jit(solution)/shard_map/all_to_all | solution.py:245
  108.4 0.9 iota_compare_fusion.9
  109.3 3.4 %fusion.114 = (f32[32,4,8]{2,1,0:T(4,128)}, f32[32,4,1,8,4]{3,4,1,0,2:T(4,128)}) fusion(bf16[32,4,8,128]{3,2,1,0:T(8,128)(2,1)S(1)} %copy-done, bf16[32,4,1,128]{3,1,2,0:T(4,128)(2,1)} %param.12, pred[4,4]{1,0:T(4,128)(4,1)S(1)} %iota_compare_fusion.10), kind=kOutput, calls=%fused_computation.257 | convolution fusion | flops 1059840 | bytes 315408 | tf_op jit(solution)/shard_map/rsngd,rtnd->rsngt/dot_general | solution.py:160
  112.7 2.1 %fusion.113 = (f32[32,4,8]{2,1,0:T(4,128)}, f32[32,4,1,8,128]{4,3,1,0,2:T(8,128)}) fusion(bf16[32,4,8,128]{3,2,1,0:T(8,128)(2,1)S(1)} %copy-done, bf16[32,128,1,128]{3,1,2,0:T(8,128)(2,1)S(1)} %copy-done.8, pred[32,128]{1,0:T(8,128)(4,1)S(1)} %iota_compare_fusion.9), kind=kOutput, calls=%fused_computation.256 | convolution fusion | flops 33946624 | bytes 1843200 | tf_op jit(solution)/shard_map/rsngd,rtnd->rsngt/dot_general | solution.py:156
  114.8 7.5 %shard_map.93 = (bf16[16,176,128]{2,1,0:T(8,128)(2,1)S(1)}, f32[16,11,128]{2,1,0:T(8,128)S(1)}) custom-call(s32[176]{0:T(256)S(1)} %reshape.724.refs_0_, bf16[16,360,128]{2,1,0:T(8,128)(2,1)S(1)} %all-to-all-done.3.refs_1_, bf16[2,2064,128]{2,1,0:T(8,128)(2,1)S(1)} %copy-done.2, bf16[2,2064,128]{2,1,0:T(8,128)(2,1)S(1)} %copy-done.5, ...), custom_call_target="tpu_custom_call" | custom-call | flops 737280 | bytes 2949120 | tf_op jit(solution)/shard_map/pallas_call | solution.py:119
  122.6 0.9 pad_maximum_fusion.2
  123.6 17.5 %all-to-all-done.5 = bf16[16,184,128]{2,1,0:T(8,128)(2,1)S(1)} async-done(((bf16[16,184,128]{2,1,0:T(8,128)(2,1)}), bf16[16,184,128]{2,1,0:T(8,128)(2,1)S(1)}, u32[]{:S(2)}, u32[]{:S(2)}) %all-to-all-start.5) | async-done | bytes 753696 | tf_op jit(solution)/shard_map/all_to_all | solution.py:245
  141.0 12.1 %all-to-all-start.4 = ((bf16[16,184,128]{2,1,0:T(8,128)(2,1)}), bf16[16,184,128]{2,1,0:T(8,128)(2,1)S(1)}, u32[]{:S(2)}, u32[]{:S(2)}) async-start(bf16[16,184,128]{2,1,0:T(8,128)(2,1)} %pad_maximum_fusion.2), calls=%async_computation.4 | async-start | bytes 1507328 | tf_op jit(solution)/shard_map/all_to_all | solution.py:245
  155.0 2.5 %fusion.53 = f32[32,4,8,128]{3,2,1,0:T(8,128)} fusion(f32[32,4,8,128]{3,2,1,0:T(8,128)S(1)} %fusion.72, bf16[32,128,1,128]{3,1,2,0:T(8,128)(2,1)} %param.15, f32[32,4,1,8,128]{4,3,1,0,2:T(8,128)S(1)} %copy-done.10, f32[32,4,8]{2,1,0:T(4,128)S(1)} %copy.215, f32[32,4,8]{2,1,0:T(4,128)S(1)} %copy.208), kind=kOutput, calls=%fused_computation.133 | convolution fusion | flops 34078720 | bytes 2629632 | tf_op jit(solution)/shard_map/rsngt,rtnd->rsngd/dot_general | solution.py:174
  159.9 1.2 fusion.67
  161.0 25.4 %all-to-all-done.4 = bf16[16,184,128]{2,1,0:T(8,128)(2,1)S(1)} async-done(((bf16[16,184,128]{2,1,0:T(8,128)(2,1)}), bf16[16,184,128]{2,1,0:T(8,128)(2,1)S(1)}, u32[]{:S(2)}, u32[]{:S(2)}) %all-to-all-start.4) | async-done | bytes 753696 | tf_op jit(solution)/shard_map/all_to_all | solution.py:245
  187.9 0.7 gather_fusion.11
  189.0 1.2 fusion.68
  190.6 0.8 copy.240
  191.4 9.8 %all-to-all-start.6 = ((bf16[4,8,4,1024]{3,2,0,1:T(4,128)(2,1)}), bf16[4,8,4,1024]{3,2,0,1:T(4,128)(2,1)S(1)}, u32[]{:S(2)}, u32[]{:S(2)}) async-start(bf16[4,8,4,1024]{3,2,0,1:T(4,128)(2,1)} %copy.240), calls=%async_computation.6 | async-start | bytes 524288 | tf_op jit(solution)/shard_map/all_to_all | solution.py:321
  202.6 5.1 %all-to-all-done.6 = bf16[4,8,4,1024]{3,2,0,1:T(4,128)(2,1)S(1)} async-done(((bf16[4,8,4,1024]{3,2,0,1:T(4,128)(2,1)}), bf16[4,8,4,1024]{3,2,0,1:T(4,128)(2,1)S(1)}, u32[]{:S(2)}, u32[]{:S(2)}) %all-to-all-start.6) | async-done | bytes 262176 | tf_op jit(solution)/shard_map/all_to_all | solution.py:321
  (137 shorter events, 13.6 us)
Async XLA Ops:
  0.8 3.0 %copy-start.20 = (s32[32,4]{1,0:T(8,128)}, s32[32,4]{1,0:T(8,128)S(1)}, u32[]{:S(2)}) copy-start(s32[32,4]{1,0:T(8,128)S(1)} %copy.200) | copy-start | bytes 1540
  1.6 19.3 %copy-start.26 = (s32[128]{0:T(128)}, s32[128]{0:T(128)S(1)}, u32[]{:S(2)}) copy-start(s32[128]{0:T(128)S(1)} %convert_reduce_fusion) | copy-start | bytes 1540
  5.1 17.2 %copy-start.14 = (bf16[2,1024,1,128]{3,1,2,0:T(8,128)(2,1)S(1)}, bf16[2,1024,1,128]{3,1,2,0:T(8,128)(2,1)}, u32[]{:S(2)}) copy-start(bf16[2,1024,1,128]{3,1,2,0:T(8,128)(2,1)} %param.19) | copy-start | bytes 1572868
  5.1 80.7 %all-to-all-start.3 = ((bf16[16,360,128]{2,1,0:T(8,128)(2,1)}), bf16[16,360,128]{2,1,0:T(8,128)(2,1)S(1)}, u32[]{:S(2)}, u32[]{:S(2)}) async-start(bf16[16,360,128]{2,1,0:T(8,128)(2,1)} %fusion.45), calls=%async_computation.3 | async-start | bytes 2949120 | tf_op jit(solution)/shard_map/all_to_all | solution.py:245
  23.6 70.0 %copy-start.1 = (bf16[2,2064,128]{2,1,0:T(8,128)(2,1)}, bf16[2,2064,128]{2,1,0:T(8,128)(2,1)S(1)}, u32[]{:S(2)}) copy-start(bf16[2,2064,128]{2,1,0:T(8,128)(2,1)S(1)} %maximum_maximum_fusion.refs_2_) | copy-start | bytes 3170308
  23.6 26.1 %collective-permute-start = (bf16[2,2064,128]{2,1,0:T(8,128)(2,1)S(1)}, bf16[2,2064,128]{2,1,0:T(8,128)(2,1)S(1)}, u32[]{:S(2)}, u32[]{:S(2)}) collective-permute-start(bf16[2,2064,128]{2,1,0:T(8,128)(2,1)S(1)} %maximum_maximum_fusion.refs_2_), channel_id=1, source_target_pairs={{0,3},{1,0},{2,1},{3,2},{4,7},{5,4},{6,5},{7,6},{8,11},{9,8},{10,9... | collective-permute-start | bytes 3170312 | tf_op jit(solution)/shard_map/ppermute | solution.py:284
  28.0 27.9 %collective-permute-start.1 = (bf16[2,2064,128]{2,1,0:T(8,128)(2,1)S(1)}, bf16[2,2064,128]{2,1,0:T(8,128)(2,1)S(1)}, u32[]{:S(2)}, u32[]{:S(2)}) collective-permute-start(bf16[2,2064,128]{2,1,0:T(8,128)(2,1)S(1)} %maximum_maximum_fusion.refs_2_), channel_id=1, source_target_pairs={{0,1},{1,2},{2,3},{3,0},{4,5},{5,6},{6,7},{7,4},{8,9},{9,10},{10,1... | collective-permute-start | bytes 3170312 | tf_op jit(solution)/shard_map/ppermute | solution.py:284
  49.7 9.6 %copy-start.4 = (bf16[2,2064,128]{2,1,0:T(8,128)(2,1)}, bf16[2,2064,128]{2,1,0:T(8,128)(2,1)S(1)}, u32[]{:S(2)}) copy-start(bf16[2,2064,128]{2,1,0:T(8,128)(2,1)S(1)} %collective-permute-done.refs_3_) | copy-start | bytes 3170308
  50.6 15.1 %collective-permute-start.3 = (bf16[2,1040,128]{2,1,0:T(8,128)(2,1)}, bf16[2,1040,128]{2,1,0:T(8,128)(2,1)S(1)}, u32[]{:S(2)}, u32[]{:S(2)}) collective-permute-start(bf16[2,1040,128]{2,1,0:T(8,128)(2,1)} %slice.213), channel_id=1, source_target_pairs={{0,3},{1,0},{2,1},{3,2},{4,7},{5,4},{6,5},{7,6},{8,11},{9,8},{10,9... | collective-permute-start | bytes 1597448 | tf_op jit(solution)/shard_map/ppermute | solution.py:284
  55.9 3.9 %copy-start.6 = (bf16[2,2064,128]{2,1,0:T(8,128)(2,1)}, bf16[2,2064,128]{2,1,0:T(8,128)(2,1)S(1)}, u32[]{:S(2)}) copy-start(bf16[2,2064,128]{2,1,0:T(8,128)(2,1)S(1)} %collective-permute-done.1.refs_6_) | copy-start | bytes 3170308
  56.9 29.0 %collective-permute-start.2 = (bf16[2,1024,128]{2,1,0:T(8,128)(2,1)}, bf16[2,1024,128]{2,1,0:T(8,128)(2,1)}, u32[]{:S(2)}, u32[]{:S(2)}) collective-permute-start(bf16[2,1024,128]{2,1,0:T(8,128)(2,1)} %slice.212), channel_id=1, source_target_pairs={{0,1},{1,2},{2,3},{3,0},{4,5},{5,6},{6,7},{7,4},{8,9},{9,10},{10,1... | collective-permute-start | bytes 1572872 | tf_op jit(solution)/shard_map/ppermute | solution.py:284
  65.7 20.1 %copy-start.7 = (bf16[2,1040,128]{2,1,0:T(8,128)(2,1)}, bf16[2,1040,128]{2,1,0:T(8,128)(2,1)S(1)}, u32[]{:S(2)}) copy-start(bf16[2,1040,128]{2,1,0:T(8,128)(2,1)S(1)} %collective-permute-done.3.refs_5_) | copy-start | bytes 1597444
  93.9 13.8 %copy-start.27 = (s32[128]{0:T(128)S(1)}, s32[128]{0:T(128)}, u32[]{:S(2)}) copy-start(s32[128]{0:T(128)} %copy-done.26) | copy-start | bytes 1540
  93.9 15.4 %copy-start = (bf16[32,4,8,128]{3,2,1,0:T(8,128)(2,1)S(1)}, bf16[32,4,8,128]{3,2,1,0:T(8,128)(2,1)}, u32[]{:S(2)}) copy-start(bf16[32,4,8,128]{3,2,1,0:T(8,128)(2,1)} %param.11) | copy-start | bytes 786436
  94.8 17.9 %copy-start.8 = (bf16[32,128,1,128]{3,1,2,0:T(8,128)(2,1)S(1)}, bf16[32,128,1,128]{3,1,2,0:T(8,128)(2,1)}, u32[]{:S(2)}) copy-start(bf16[32,128,1,128]{3,1,2,0:T(8,128)(2,1)} %param.14) | copy-start | bytes 3145732
  94.8 46.2 %all-to-all-start.5 = ((bf16[16,184,128]{2,1,0:T(8,128)(2,1)}), bf16[16,184,128]{2,1,0:T(8,128)(2,1)S(1)}, u32[]{:S(2)}, u32[]{:S(2)}) async-start(bf16[16,184,128]{2,1,0:T(8,128)(2,1)} %pad_maximum_fusion.3), calls=%async_computation.5 | async-start | bytes 1507328 | tf_op jit(solution)/shard_map/all_to_all | solution.py:245
  108.4 6.4 %copy-start.2 = (bf16[2,2064,128]{2,1,0:T(8,128)(2,1)S(1)}, bf16[2,2064,128]{2,1,0:T(8,128)(2,1)}, u32[]{:S(2)}) copy-start(bf16[2,2064,128]{2,1,0:T(8,128)(2,1)} %copy-done.1) | copy-start | bytes 3170308
  108.4 6.4 %copy-start.5 = (bf16[2,2064,128]{2,1,0:T(8,128)(2,1)S(1)}, bf16[2,2064,128]{2,1,0:T(8,128)(2,1)}, u32[]{:S(2)}) copy-start(bf16[2,2064,128]{2,1,0:T(8,128)(2,1)} %copy-done.4) | copy-start | bytes 3170308
  122.6 30.6 %copy-start.21 = (s32[32,4]{1,0:T(8,128)S(1)}, s32[32,4]{1,0:T(8,128)}, u32[]{:S(2)}) copy-start(s32[32,4]{1,0:T(8,128)} %copy-done.20) | copy-start | bytes 1540
  122.6 30.6 %copy-start.25 = (s32[32,4]{1,0:T(8,128)S(1)}, s32[32,4]{1,0:T(8,128)}, u32[]{:S(2)}) copy-start(s32[32,4]{1,0:T(8,128)} %reduce_sum.179) | copy-start | bytes 1540
  122.6 30.7 %copy-start.24 = (f32[32,4,8]{2,1,0:T(4,128)S(1)}, f32[32,4,8]{2,1,0:T(4,128)}, u32[]{:S(2)}) copy-start(f32[32,4,8]{2,1,0:T(4,128)} %get-tuple-element.332) | copy-start | bytes 12292
  122.6 30.8 %copy-start.17 = (f32[32,4,8]{2,1,0:T(4,128)S(1)}, f32[32,4,8]{2,1,0:T(4,128)}, u32[]{:S(2)}) copy-start(f32[32,4,8]{2,1,0:T(4,128)} %get-tuple-element.330) | copy-start | bytes 12292
  122.6 30.9 %copy-start.13 = (f32[32,4,1,8,4]{3,4,1,0,2:T(4,128)S(1)}, f32[32,4,1,8,4]{3,4,1,0,2:T(4,128)}, u32[]{:S(2)}) copy-start(f32[32,4,1,8,4]{3,4,1,0,2:T(4,128)} %get-tuple-element.333) | copy-start | bytes 49156
  123.6 30.3 %copy-start.10 = (f32[32,4,1,8,128]{4,3,1,0,2:T(8,128)S(1)}, f32[32,4,1,8,128]{4,3,1,0,2:T(8,128)}, u32[]{:S(2)}) copy-start(f32[32,4,1,8,128]{4,3,1,0,2:T(8,128)} %get-tuple-element.331) | copy-start | bytes 1572868
  123.6 31.1 %copy-start.22 = (bf16[32,4,1,128]{3,1,2,0:T(4,128)(2,1)S(1)}, bf16[32,4,1,128]{3,1,2,0:T(4,128)(2,1)}, u32[]{:S(2)}) copy-start(bf16[32,4,1,128]{3,1,2,0:T(4,128)(2,1)} %param.13) | copy-start | bytes 98308
  141.0 45.4 %all-to-all-start.4 = ((bf16[16,184,128]{2,1,0:T(8,128)(2,1)}), bf16[16,184,128]{2,1,0:T(8,128)(2,1)S(1)}, u32[]{:S(2)}, u32[]{:S(2)}) async-start(bf16[16,184,128]{2,1,0:T(8,128)(2,1)} %pad_maximum_fusion.2), calls=%async_computation.4 | async-start | bytes 1507328 | tf_op jit(solution)/shard_map/all_to_all | solution.py:245
  189.0 18.8 %copy-start.3 = (bf16[2,2064,128]{2,1,0:T(8,128)(2,1)S(1)}, bf16[2,2064,128]{2,1,0:T(8,128)(2,1)}, u32[]{:S(2)}) copy-start(bf16[2,2064,128]{2,1,0:T(8,128)(2,1)} %copy-done.1) | copy-start | bytes 3170308
  189.0 18.8 %copy-start.29 = (s32[128]{0:T(128)S(1)}, s32[128]{0:T(128)}, u32[]{:S(2)}) copy-start(s32[128]{0:T(128)} %get-tuple-element.327) | copy-start | bytes 1540
  189.0 18.8 %copy-start.30 = (s32[128]{0:T(128)S(1)}, s32[128]{0:T(128)}, u32[]{:S(2)}) copy-start(s32[128]{0:T(128)} %get-tuple-element.328) | copy-start | bytes 1540
  189.0 18.8 %copy-start.32 = (s32[128]{0:T(128)S(1)}, s32[128]{0:T(128)}, u32[]{:S(2)}) copy-start(s32[128]{0:T(128)} %get-tuple-element.301) | copy-start | bytes 1540
  191.4 16.4 %all-to-all-start.6 = ((bf16[4,8,4,1024]{3,2,0,1:T(4,128)(2,1)}), bf16[4,8,4,1024]{3,2,0,1:T(4,128)(2,1)S(1)}, u32[]{:S(2)}, u32[]{:S(2)}) async-start(bf16[4,8,4,1024]{3,2,0,1:T(4,128)(2,1)} %copy.240), calls=%async_computation.6 | async-start | bytes 524288 | tf_op jit(solution)/shard_map/all_to_all | solution.py:321
  208.2 0.7 copy-start.16
